TPU v7x, 32 devices: a whole 2x2x4 slice. The times are simulated.
32 devices in a mesh: seq: 4 (over y, x), batch: 8 (over z, core).
Axes of the slice: x: 2, y: 2, z: 4, core: 2. Of those that a mesh axis runs over, the one named last changes fastest.
Arguments:
- tokens: bfloat16 [8, 512, 768], P('batch', 'seq'), may hold values from -6 to 6
- segments: int32 [8, 512], P('batch'), may hold values from 0 to 5, as said below
- ln1_gain: float32 [768], replicated, may hold values from 0.1 to 1.9
- ln1_bias: float32 [768], replicated, may hold values from -3 to 3
- w_qkv: bfloat16 [768, 2304], replicated, may hold values from -0.3125 to 0.3125
- bias_qv: float32 [1536], replicated, may hold values from -3 to 3
- w_out: bfloat16 [768, 768], replicated, may hold values from -0.875 to 0.875
- bias_out: float32 [768], replicated, may hold values from -3 to 3
- ln2_gain: float32 [768], replicated, may hold values from 0.1 to 1.9
- ln2_bias: float32 [768], replicated, may hold values from -3 to 3
- w_in: bfloat16 [768, 3072], replicated, may hold values from -0.21875 to 0.21875
- bias_in: float32 [3072], replicated, may hold values from -3 to 3
- w_down: bfloat16 [3072, 768], replicated, may hold values from -0.109375 to 0.109375
- bias_down: float32 [768], replicated, may hold values from -3 to 3
- cotangent: bfloat16 [8, 512, 768], P('batch', 'seq'), may hold values from -6 to 6
Outputs:
- activations: bfloat16 [8, 512, 768], P('batch', 'seq')
- d_tokens: float32 [8, 512, 768], P('batch', 'seq')
- d_ln1_gain: float32 [768], P('batch')
- d_ln1_bias: float32 [768], P('batch')
- d_w_qkv: float32 [768, 2304], P('batch')
- d_bias_qv: float32 [1536], P('batch')
- d_w_out: float32 [768, 768], P('batch')
- d_bias_out: float32 [768], P('batch')
- d_ln2_gain: float32 [768], P('batch')
- d_ln2_bias: float32 [768], P('batch')
- d_w_in: float32 [768, 3072], P('batch')
- d_bias_in: float32 [3072], P('batch')
- d_w_down: float32 [3072, 768], P('batch')
- d_bias_down: float32 [768], P('batch')
Inputs may be any that keep to these rules, and one draw needn't show every extreme that they name: `segments`: each row holds exactly six documents, numbered 0 to 5 in order (ids never fall); document 2 starts in the first quarter of the row and ends in its last quarter.
All inputs are finite; a program needn't handle non-finite values.
Results may differ from a plain program's by a relative error of at most 0.012.
The roundings to bfloat16 on the way count: a program that leaves them out, or rounds other values in their place, can miss the bound.
Values may be sent and summed in bfloat16 or wider, within the bound.
No kernel may reach another device: no remote copies, remote signals or barrier semaphores. Data moves between devices by JAX's collectives and lax.ppermute only.
A program may use at most 128 MiB of HBM per device.

v0:
```python
import jax
import jax.numpy as jnp
from jax import lax
from jax.sharding import PartitionSpec as P

HEADS = 12
HEAD_DIM = 64


def norm_rows(values, gain, shift):
    mean = jnp.mean(values, axis=-1, keepdims=True)
    centred = values - mean
    var = jnp.mean(centred * centred, axis=-1, keepdims=True)
    return centred * lax.rsqrt(var + 1e-06) * gain + shift


def gelu_tanh(values):
    return jax.nn.gelu(values, approximate=True)


def masked_scores(query, keys, seg_query, seg_keys, scale):
    scores = jnp.einsum("rqhd,rkhd->rhqk", query, keys, preferred_element_type=jnp.float32) * scale
    mask = seg_query[:, None, :, None] == seg_keys[:, None, None, :]
    return jnp.where(mask, scores, -1e30)


def shards(
    tokens,
    segments,
    ln1_gain,
    ln1_bias,
    w_qkv,
    bias_qv,
    w_out,
    bias_out,
    ln2_gain,
    ln2_bias,
    w_in,
    bias_in,
    w_down,
    bias_down,
    cotangent,
):
    rows, local_len, width = tokens.shape
    count = rows * local_len
    scale = HEAD_DIM ** (-0.5)
    offset = lax.axis_index("seq") * local_len
    seg_query = lax.dynamic_slice_in_dim(segments, offset, local_len, 1)
    x_rows = tokens.astype(jnp.float32).reshape(count, width)
    h1, ln1_back = jax.vjp(norm_rows, x_rows, ln1_gain, ln1_bias)
    h1_low = h1.astype(jnp.bfloat16)
    bias_all = jnp.concatenate([bias_qv[:width], jnp.zeros((width,), jnp.float32), bias_qv[width:]])
    qkv = jnp.dot(h1_low, w_qkv, preferred_element_type=jnp.float32) + bias_all
    qkv_low = qkv.astype(jnp.bfloat16).reshape(rows, local_len, 3, HEADS, HEAD_DIM)
    query = qkv_low[:, :, 0]
    keys = qkv_low[:, :, 1]
    values = qkv_low[:, :, 2]
    keys_all, values_all = (
        lax.all_gather(keys, "seq", axis=1, tiled=True),
        lax.all_gather(values, "seq", axis=1, tiled=True),
    )
    scores = masked_scores(query, keys_all, seg_query, segments, scale)
    top = jnp.max(scores, axis=-1, keepdims=True)
    expo = jnp.exp(scores - top)
    total = jnp.sum(expo, axis=-1, keepdims=True)
    probs = expo / total
    log_total = top + jnp.log(total)
    probs_low = probs.astype(jnp.bfloat16)
    attn = jnp.einsum("rhqk,rkhd->rqhd", probs_low, values_all, preferred_element_type=jnp.float32)
    attn_low = attn.reshape(count, width).astype(jnp.bfloat16)
    x1 = x_rows + jnp.dot(attn_low, w_out, preferred_element_type=jnp.float32) + bias_out
    h2, ln2_back = jax.vjp(norm_rows, x1, ln2_gain, ln2_bias)
    h2_low = h2.astype(jnp.bfloat16)
    hidden = jnp.dot(h2_low, w_in, preferred_element_type=jnp.float32) + bias_in
    act, gelu_back = jax.vjp(gelu_tanh, hidden)
    act_low = act.astype(jnp.bfloat16)
    mixed = jnp.dot(act_low, w_down, preferred_element_type=jnp.float32) + bias_down
    activations = (x1 + mixed).astype(jnp.bfloat16).reshape(tokens.shape)
    grad_low = cotangent.reshape(count, width)
    grad_rows = grad_low.astype(jnp.float32)
    d_w_down = jnp.dot(act_low.T, grad_low, preferred_element_type=jnp.float32)
    d_bias_down = jnp.sum(grad_rows, axis=0)
    d_act = jnp.dot(grad_low, w_down.T, preferred_element_type=jnp.float32)
    (d_hidden,) = gelu_back(d_act)
    d_hidden_low = d_hidden.astype(jnp.bfloat16)
    d_w_in = jnp.dot(h2_low.T, d_hidden_low, preferred_element_type=jnp.float32)
    d_bias_in = jnp.sum(d_hidden_low.astype(jnp.float32), axis=0)
    d_h2 = jnp.dot(d_hidden_low, w_in.T, preferred_element_type=jnp.float32)
    d_x1_norm, d_ln2_gain, d_ln2_bias = ln2_back(d_h2)
    mlp_grads = (d_ln2_gain, d_ln2_bias, d_w_in, d_bias_in, d_w_down, d_bias_down)
    d_x1 = grad_rows + d_x1_norm
    d_branch = d_x1.astype(jnp.bfloat16)
    d_w_out = jnp.dot(attn_low.T, d_branch, preferred_element_type=jnp.float32)
    d_bias_out = jnp.sum(d_branch.astype(jnp.float32), axis=0)
    d_attn = jnp.dot(d_branch, w_out.T, preferred_element_type=jnp.float32)
    d_attn = d_attn.astype(jnp.bfloat16).reshape(rows, local_len, HEADS, HEAD_DIM)
    keys_back, values_back = (keys_all, values_all)
    scores_back = masked_scores(query, keys_back, seg_query, segments, scale)
    probs_back = jnp.exp(scores_back - log_total)
    probs_back_low = probs_back.astype(jnp.bfloat16)
    d_probs = jnp.einsum("rqhd,rkhd->rhqk", d_attn, values_back, preferred_element_type=jnp.float32)
    inner = jnp.sum(probs_back * d_probs, axis=-1, keepdims=True)
    d_scores = (probs_back * (d_probs - inner)).astype(jnp.bfloat16)
    d_query = (
        jnp.einsum("rhqk,rkhd->rqhd", d_scores, keys_back, preferred_element_type=jnp.float32)
        * scale
    )
    d_keys_all = (
        jnp.einsum("rhqk,rqhd->rkhd", d_scores, query, preferred_element_type=jnp.float32) * scale
    )
    d_values_all = jnp.einsum(
        "rhqk,rqhd->rkhd", probs_back_low, d_attn, preferred_element_type=jnp.float32
    )
    d_keys, d_values = (
        lax.psum_scatter(d_keys_all, "seq", scatter_dimension=1, tiled=True),
        lax.psum_scatter(d_values_all, "seq", scatter_dimension=1, tiled=True),
    )
    d_qkv = (
        jnp.stack([d_query, d_keys, d_values], axis=2)
        .astype(jnp.bfloat16)
        .reshape(count, 3 * width)
    )
    d_qkv_wide = d_qkv.astype(jnp.float32)
    d_bias_qv = jnp.concatenate(
        [jnp.sum(d_qkv_wide[:, :width], axis=0), jnp.sum(d_qkv_wide[:, 2 * width :], axis=0)]
    )
    d_w_qkv = jnp.dot(h1_low.T, d_qkv, preferred_element_type=jnp.float32)
    d_h1 = jnp.dot(d_qkv, w_qkv.T, preferred_element_type=jnp.float32)
    d_x_norm, d_ln1_gain, d_ln1_bias = ln1_back(d_h1)
    d_tokens = (d_x1 + d_x_norm).reshape(tokens.shape)
    attn_grads = (d_ln1_gain, d_ln1_bias, d_w_qkv, d_bias_qv, d_w_out, d_bias_out)
    shares = lax.psum_scatter(attn_grads + mlp_grads, "batch", scatter_dimension=0, tiled=True)
    totals = lax.psum(shares, "seq")
    return (
        activations,
        d_tokens,
        totals[0],
        totals[1],
        totals[2],
        totals[3],
        totals[4],
        totals[5],
        totals[6],
        totals[7],
        totals[8],
        totals[9],
        totals[10],
        totals[11],
    )


def solution(mesh):
    placed = (
        P("batch", "seq", None),
        P("batch", None),
        P(),
        P(),
        P(),
        P(),
        P(),
        P(),
        P(),
        P(),
        P(),
        P(),
        P(),
        P(),
        P("batch", "seq", None),
    )
    return jax.shard_map(
        shards,
        mesh=mesh,
        in_specs=placed,
        out_specs=(
            P("batch", "seq", None),
            P("batch", "seq", None),
            P("batch"),
            P("batch"),
            P("batch", None),
            P("batch"),
            P("batch", None),
            P("batch"),
            P("batch"),
            P("batch"),
            P("batch", None),
            P("batch"),
            P("batch", None),
            P("batch"),
        ),
        check_vma=False,
    )
```

profile of v0, /device:TPU:0, one launch (start us, length us, event | category | flops | bytes accessed | tf_op | source)
XLA Modules:
  0.0 555.3 jit_solution(18176027585578233211)
XLA Ops:
  10.4 2.5 fusion
  16.1 14.2 %all-gather = bf16[1,512,1,12,64]{1,4,3,2,0:T(8,128)(2,1)} all-gather(bf16[1,128,1,12,64]{1,4,3,2,0:T(8,128)(2,1)S(1)} %get-tuple-element.47), channel_id=2, replica_groups=mesh['seq'=4,'batch'=8] {'seq'}, dimensions={1}, use_global_device_ids=true | all-gather | bytes 983040 | tf_op jit(solution)/shard_map/all_gather | solution.py:60
  30.3 10.9 %all-gather.1 = bf16[1,512,1,12,64]{1,4,3,2,0:T(8,128)(2,1)} all-gather(bf16[1,128,1,12,64]{1,4,3,2,0:T(8,128)(2,1)S(1)} %get-tuple-element.48), channel_id=3, replica_groups=mesh['seq'=4,'batch'=8] {'seq'}, dimensions={1}, use_global_device_ids=true | all-gather | bytes 983040 | tf_op jit(solution)/shard_map/all_gather | solution.py:59
  49.9 2.6 convert_reduce_fusion
  52.5 2.3 multiply_reduce_fusion.1
  60.2 3.9 fusion.14
  64.2 3.4 multiply_reduce_fusion
  69.5 2.5 multiply_bitcast_fusion
  72.1 2.9 fusion.74
  75.3 3.1 fusion.17
  78.3 17.5 %reduce-scatter.9.cloned.1.call-done = f32[1,128,12,64]{1,3,2,0:T(8,128)} async-done(((f32[1,512,12,64]{1,3,2,0:T(8,128)}), f32[1,128,12,64]{1,3,2,0:T(8,128)}) %reduce-scatter.9.cloned.1.call-update) | async-done | bytes 393232 | tf_op jit(solution)/shard_map/reduce_scatter | solution.py:116
  95.8 34.0 %reduce-scatter.7.cloned.1.call-done = f32[1,128,12,64]{1,3,2,0:T(8,128)} async-done(((f32[1,512,12,64]{1,3,2,0:T(8,128)}), f32[1,128,12,64]{1,3,2,0:T(8,128)}) %reduce-scatter.7.cloned.1.call-update) | async-done | bytes 393232 | tf_op jit(solution)/shard_map/reduce_scatter | solution.py:115
  131.9 4.8 fusion.46
  136.8 6.7 %fusion.49 = f32[3072,768]{1,0:T(8,128)} fusion(bf16[1,128,768]{2,1,0:T(8,128)(2,1)} %param.29, f32[128,3072]{1,0:T(8,128)} %copy-done.10), kind=kOutput, calls=%fused_computation.78 | convolution fusion | flops 607518720 | bytes 11206656 | tf_op jit(solution)/shard_map/dot_general | solution.py:81
  144.2 6.4 %fusion.66 = f32[768,3072]{1,0:T(8,128)} fusion(bf16[128,3072]{1,0:T(8,128)(2,1)} %copy-done.14, f32[128,768]{1,0:T(8,128)} %copy-done.3, f32[768]{0:T(1024)S(1)} %copy-done.26, f32[768]{0:T(1024)S(1)} %copy-done.24, f32[128]{0:T(128)} %copy-done.33, f32[128]{0:T(128)} %copy-done.30), kind=kOutput, calls=%fused_computation.106 | convolution fusion | flops 604471296 | bytes 10624000 | tf_op jit(solution)/shard_map/dot_general | solution.py:86
  150.7 17.9 %reduce-scatter.13.cloned.1.call-done = f32[96,768]{1,0:T(8,128)} async-done(((f32[768,768]{1,0:T(8,128)}), f32[96,768]{1,0:T(8,128)}) %reduce-scatter.13.cloned.1.call-update) | async-done | bytes 294928 | tf_op jit(solution)/shard_map/reduce_scatter | solution.py:132
  168.6 78.5 %reduce-scatter.11.cloned.1.call-done = f32[96,2304]{1,0:T(8,128)} async-done(((f32[768,2304]{1,0:T(8,128)}), f32[96,2304]{1,0:T(8,128)}) %reduce-scatter.11.cloned.1.call-update) | async-done | bytes 884752 | tf_op jit(solution)/shard_map/reduce_scatter | solution.py:132
  247.1 100.1 %reduce-scatter.17.cloned.1.call-done = f32[384,768]{1,0:T(8,128)} async-done(((f32[3072,768]{1,0:T(8,128)}), f32[384,768]{1,0:T(8,128)}) %reduce-scatter.17.cloned.1.call-update) | async-done | bytes 1179664 | tf_op jit(solution)/shard_map/reduce_scatter | solution.py:132
  347.2 100.1 %reduce-scatter.15.cloned.1.call-done = f32[96,3072]{1,0:T(8,128)} async-done(((f32[768,3072]{1,0:T(8,128)}), f32[96,3072]{1,0:T(8,128)}) %reduce-scatter.15.cloned.1.call-update) | async-done | bytes 1179664 | tf_op jit(solution)/shard_map/reduce_scatter | solution.py:132
  450.5 4.7 fusion.22
  460.5 27.5 %all-reduce.8 = (f32[768]{0:T(1024)S(1)}, f32[768]{0:T(1024)}, f32[1536]{0:T(1024)}, f32[768]{0:T(1024)}, f32[768]{0:T(1024)}, /*index=5*/f32[768]{0:T(1024)}, f32[3072]{0:T(1024)}, f32[768]{0:T(1024)S(1)}) all-reduce(f32[768]{0:T(1024)} %get-tuple-element.18, ...), channel_id=6, replica_groups=mesh['seq'=4,'batch'=8] {'batch'}, use_global_device_ids=true, to_apply=%region_14.15.clone | all-reduce | flops 9216 | bytes 73728
  494.7 10.7 %all-reduce.9 = (f32[96]{0:T(128)}, f32[96]{0:T(128)}, f32[192]{0:T(256)}, f32[96]{0:T(128)}, f32[96]{0:T(128)}, /*index=5*/f32[96]{0:T(128)}, f32[384]{0:T(512)}, f32[96]{0:T(128)}) all-reduce(f32[96]{0:T(128)S(1)} %dynamic-slice.1, f32[96]{0:T(128)S(1)} %dynamic-slice.3, ...), channel_id=1, replica_groups=mesh['seq'=4,'batch'=8] {'seq'}, use_global_device_ids=true, to_apply=%region_15.16 | all-reduce | flops 1152 | bytes 9216 | tf_op jit(solution)/shard_map/psum | solution.py:133
  505.4 38.0 %all-reduce.13.cloned.1.call-done = (f32[96,2304]{1,0:T(8,128)}, f32[96,768]{1,0:T(8,128)}, f32[96,3072]{1,0:T(8,128)}, f32[384,768]{1,0:T(8,128)}) async-done(((f32[96,2304]{1,0:T(8,128)}, f32[96,768]{1,0:T(8,128)}, f32[96,3072]{1,0:T(8,128)}, f32[384,768]{1,0:T(8,128)}), (f32[96,2304]{1,0:T(8,128)}, f32[96,768]{1,0:T(8,128)}, f32[96,3072]{1,0:T(8,128)}, ...) | async-done | bytes 3538960 | tf_op jit(solution)/shard_map/psum | solution.py:133
  543.4 2.2 copy.42
  (158 shorter events, 41.4 us)
Async XLA Ops:
  7.2 3.3 copy-start
  7.2 88.6 %reduce-scatter.9.cloned.1.call-start = ((), (), s32[]{:S(2)}) async-start(), calls=%async_computation.7 | async-start | bytes 1966080 | tf_op jit(solution)/shard_map/reduce_scatter | solution.py:116
  15.0 26.2 %copy-start.36 = (s32[1,512]{1,0:T(1,128)S(1)}, s32[1,512]{1,0:T(1,128)}, u32[]{:S(2)}) copy-start(s32[1,512]{1,0:T(1,128)} %param.16) | copy-start | bytes 6148
  43.4 6.5 %slice-start.2 = ((s8[4718592]{0:T(1024)(128)(4,1)}), s8[4194304]{0:T(1024)(128)(4,1)S(1)}, s32[]{:S(2)}) async-start(s8[4718592]{0:T(1024)(128)(4,1)} %bitcast.138), calls=%async_computation.15 | async-start | bytes 8388608
  44.3 4.6 slice-start
  45.1 3.9 slice-start.1
  45.1 4.8 slice-start.3
  47.7 7.2 %copy-start.3 = (f32[128,768]{1,0:T(8,128)}, f32[128,768]{1,0:T(8,128)S(1)}, u32[]{:S(2)}) copy-start(f32[128,768]{1,0:T(8,128)S(1)} %get-tuple-element.56) | copy-start | bytes 1179652
  47.7 7.2 %copy-start.30 = (f32[128]{0:T(128)}, f32[128]{0:T(128)S(1)}, u32[]{:S(2)}) copy-start(f32[128]{0:T(128)S(1)} %broadcast_multiply_fusion) | copy-start | bytes 1540
  49.0 5.9 %copy-start.33 = (f32[128]{0:T(128)}, f32[128]{0:T(128)S(1)}, u32[]{:S(2)}) copy-start(f32[128]{0:T(128)S(1)} %fusion.64) | copy-start | bytes 1540
  64.2 65.6 %reduce-scatter.7.cloned.1.call-start = ((), (), s32[]{:S(2)}) async-start(), calls=%async_computation.6 | async-start | bytes 1966080 | tf_op jit(solution)/shard_map/reduce_scatter | solution.py:115
  64.2 3.4 copy-start.2
  72.0 96.6 %reduce-scatter.13.cloned.1.call-start = ((), (), s32[]{:S(2)}) async-start(), calls=%async_computation.9 | async-start | bytes 2654208 | tf_op jit(solution)/shard_map/reduce_scatter | solution.py:132
  75.0 56.9 %copy-start.23 = (f32[768]{0:T(1024)S(1)}, f32[768]{0:T(1024)}, u32[]{:S(2)}) copy-start(f32[768]{0:T(1024)} %param.17) | copy-start | bytes 9220
  75.0 56.9 %copy-start.27 = (f32[768]{0:T(1024)S(1)}, f32[768]{0:T(1024)}, u32[]{:S(2)}) copy-start(f32[768]{0:T(1024)} %param.18) | copy-start | bytes 9220
  75.0 56.9 %copy-start.29 = (f32[128]{0:T(128)S(1)}, f32[128]{0:T(128)}, u32[]{:S(2)}) copy-start(f32[128]{0:T(128)} %copy-done.28) | copy-start | bytes 1540
  75.0 172.1 %reduce-scatter.11.cloned.1.call-start = ((), (), s32[]{:S(2)}) async-start(), calls=%async_computation.8 | async-start | bytes 7962624 | tf_op jit(solution)/shard_map/reduce_scatter | solution.py:132
  136.7 210.5 %reduce-scatter.17.cloned.1.call-start = ((), (), s32[]{:S(2)}) async-start(), calls=%async_computation.11 | async-start | bytes 10616832 | tf_op jit(solution)/shard_map/reduce_scatter | solution.py:132
  143.5 303.8 %reduce-scatter.15.cloned.1.call-start = ((), (), s32[]{:S(2)}) async-start(), calls=%async_computation.10 | async-start | bytes 10616832 | tf_op jit(solution)/shard_map/reduce_scatter | solution.py:132
  150.6 392.8 %all-reduce.13.cloned.1.call-start = ((), (), s32[]{:S(2)}) async-start(), calls=%async_computation.12 | async-start | bytes 7077888 | tf_op jit(solution)/shard_map/psum | solution.py:133
  447.3 3.2 copy-start.41
  450.4 4.7 copy-start.9
  456.1 2.8 copy-start.17
  543.4 3.0 copy-start.20
  (30 other events, 51.1 us)
Sparse Core Ops, SparseCore 0:
  64.3 31.4 reduce-scatter.8
  98.8 30.9 reduce-scatter.6
  132.1 36.4 reduce-scatter.12
  170.8 76.2 reduce-scatter.10
  249.3 97.8 reduce-scatter.16
  349.4 97.8 reduce-scatter.14
  450.7 92.6 all-reduce.12
where the time goes:
time: 556 us; the launch traced here: 555 us
  waiting for transfers between devices  386 us (69%)
  blocking collectives  63.3 us (11%)
  matrix products  53.4 us (10%)
  local copies, waits for them, and re-layouts  26 us (5%)
  between operations  16.6 us (3%)
  other arithmetic  9.34 us (2%)
    reduce_scatter x4, waiting for transfers between devices, shards(): lax.psum_scatter(attn_grads + mlp_grads, 'batch', scatter_dimension=0, ti...  297 us
    psum x1, waiting for transfers between devices, shards(): totals = lax.psum(shares, 'seq')  38 us
    reduce_scatter x1, waiting for transfers between devices, shards(): lax.psum_scatter(d_keys_all, 'seq', scatter_dimension=1, tiled=True)  34 us
    unnamed x1, blocking collectives  27.5 us
    unnamed x107, local copies, waits for them, and re-layouts  20.3 us
    reduce_scatter x1, waiting for transfers between devices, shards(): lax.psum_scatter(d_values_all, 'seq', scatter_dimension=1, tiled=True)  17.5 us
    all_gather x1, blocking collectives, shards(): lax.all_gather(values, 'seq', axis=1, tiled=True)  14.2 us
  transfers between devices with their start and end apart: 7, of which 7 were waited for; matrix products, arithmetic and copies ran while one was open for 9% of the time, Pallas kernels for 0%

commit v1 on v0

v1 whole, which is shorter than its diff:
```python
import jax
import jax.numpy as jnp
from jax import lax
from jax.sharding import PartitionSpec as P

HEADS = 12
HEAD_DIM = 64
BF = jnp.bfloat16
F32 = jnp.float32


def dot(a, b, dims=((1,), (0,))):
    return lax.dot_general(a, b, (dims, ((), ())), preferred_element_type=F32)


def exchange(value, axis, size, step):
    return lax.ppermute(value, axis, [(j, j ^ step) for j in range(size)])


def gather_seq(value, size):
    return [value] + [exchange(value, "seq", size, k) for k in range(1, size)]


def norm_parts(values):
    mean = jnp.mean(values, axis=-1, keepdims=True)
    centred = values - mean
    var = jnp.mean(centred * centred, axis=-1, keepdims=True)
    scale = lax.rsqrt(var + 1e-06)
    return centred * scale, scale


def norm_back(grad, unit, scale, gain):
    grad = grad * gain
    mean = jnp.mean(grad, axis=-1, keepdims=True)
    along = jnp.mean(grad * unit, axis=-1, keepdims=True)
    return (grad - mean - unit * along) * scale


def gelu_both(v):
    c = 0.7978845608028654
    inner = c * (v + 0.044715 * v * v * v)
    t = jnp.tanh(inner)
    value = 0.5 * v * (1.0 + t)
    slope = 0.5 * (1.0 + t) + 0.5 * v * (1.0 - t * t) * c * (1.0 + 3.0 * 0.044715 * v * v)
    return value, slope


def make(S, NB):
    def shards(tokens, segments, ln1_gain, ln1_bias, w_qkv, bias_qv, w_out, bias_out,
               ln2_gain, ln2_bias, w_in, bias_in, w_down, bias_down, cotangent):
        rows, t, D = tokens.shape
        FF = w_in.shape[1]
        L = t * S
        hs = HEADS // S
        cs = hs * HEAD_DIM
        R = D // NB
        FJ = FF // (NB * S)
        scale = HEAD_DIM ** (-0.5)
        s = lax.axis_index("seq")
        b = lax.axis_index("batch")
        rel_s = jnp.arange(S, dtype=jnp.int32) ^ s
        rel_b = jnp.arange(NB, dtype=jnp.int32) ^ b

        x_own = tokens.reshape(t, D)
        cot_own = cotangent.reshape(t, D)
        wq_s = lax.dynamic_slice_in_dim(w_qkv.reshape(D, 3, S, cs), s, 1, 2).reshape(D, 3 * cs)
        bq_s = lax.dynamic_slice_in_dim(bias_qv.reshape(2, S, cs), s, 1, 1).reshape(2, cs)
        bqkv_s = jnp.concatenate([bq_s[0], jnp.zeros((cs,), F32), bq_s[1]])
        win_s = lax.dynamic_slice_in_dim(w_in.reshape(D, NB, S, FJ), s, 1, 2).reshape(D, NB * FJ)
        bin_s = lax.dynamic_slice_in_dim(bias_in.reshape(NB, S, FJ), s, 1, 1).reshape(NB * FJ)
        wdn_s = lax.dynamic_slice_in_dim(w_down.reshape(NB, S, FJ, D), s, 1, 1).reshape(NB * FJ, D)
        wout_rel = jnp.take(w_out.reshape(S, cs, D), rel_s, axis=0).reshape(D, D)
        seg_rel = jnp.take(segments.reshape(S, t), rel_s, axis=0).reshape(L)

        x_all = jnp.concatenate(gather_seq(x_own, S), 0)
        cot_in, x_all = lax.optimization_barrier((cot_own, x_all))
        cot_all = jnp.concatenate(gather_seq(cot_in, S), 0)

        x_f = x_all.astype(F32)
        unit1, scale1 = norm_parts(x_f)
        h1 = (unit1 * ln1_gain + ln1_bias).astype(BF)
        qkv = (dot(h1, wq_s) + bqkv_s).astype(BF)
        q = qkv[:, :cs].reshape(L, hs, HEAD_DIM)
        k = qkv[:, cs:2 * cs].reshape(L, hs, HEAD_DIM)
        v = qkv[:, 2 * cs:].reshape(L, hs, HEAD_DIM)
        mask = seg_rel[:, None] == seg_rel[None, :]
        scores = jnp.einsum("qhd,khd->hqk", q, k, preferred_element_type=F32) * scale
        scores = jnp.where(mask[None], scores, -1e30)
        top = jnp.max(scores, axis=-1, keepdims=True)
        expo = jnp.exp(scores - top)
        total = jnp.sum(expo, axis=-1, keepdims=True)
        probs = expo / total
        probs_low = probs.astype(BF)
        attn = jnp.einsum("hqk,khd->qhd", probs_low, v, preferred_element_type=F32).reshape(L, cs).astype(BF)

        got = gather_seq(attn, S)
        blocks = []
        for m, g in enumerate(got):
            g4 = g.reshape(S, t, cs)
            blocks.append(jnp.concatenate([g4[kk ^ m] for kk in range(S)], 0))
        attn_all = jnp.concatenate(blocks, 1)

        x1 = x_f + dot(attn_all, wout_rel) + bias_out
        unit2, scale2 = norm_parts(x1)
        h2 = (unit2 * ln2_gain + ln2_bias).astype(BF)

        u_s = dot(h2, win_s) + bin_s
        act_s, slope_s = gelu_both(u_s)
        act_s = act_s.astype(BF)
        dact_s = dot(cot_all, wdn_s, ((1,), (1,)))
        du_s = (dact_s * slope_s).astype(BF)
        g_win = dot(h2, du_s, ((0,), (0,)))
        g_wdn = dot(act_s, cot_all, ((0,), (0,)))
        g_bin = jnp.sum(du_s.astype(F32), 0)
        mlp = jnp.concatenate([g_win.reshape(NB, R, NB * FJ), g_wdn.reshape(NB, FJ, D)], 1).astype(BF)

        h2o = h2[:t]
        u = dot(h2o, w_in) + bias_in
        act, slope = gelu_both(u)
        act = act.astype(BF)
        activations = (x1[:t] + dot(act, w_down) + bias_down).astype(BF)
        dy = cot_own.astype(F32)
        du = (dot(cot_own, w_down, ((1,), (1,))) * slope).astype(BF)
        dh2 = dot(du, w_in, ((1,), (1,)))
        g_ln2g = jnp.sum(dh2 * unit2[:t], 0)
        g_ln2b = jnp.sum(dh2, 0)
        dx1 = dy + norm_back(dh2, unit2[:t], scale2[:t], ln2_gain)
        da = dx1.astype(BF)
        g_bout = jnp.sum(da.astype(F32), 0)
        g_bdn = jnp.sum(dy, 0)
        dattn = dot(da, wout_rel, ((1,), (1,))).astype(BF)
        da_rel = jnp.take(da.reshape(t, S, cs), rel_s, axis=1)
        both = [jnp.concatenate([dattn[:, kk * cs:(kk + 1) * cs], da_rel[:, kk]], 1) for kk in range(S)]
        both = jnp.concatenate([both[0]] + [exchange(both[kk], "seq", S, kk) for kk in range(1, S)], 0)
        dattn_all = both[:, :cs].reshape(L, hs, HEAD_DIM)
        da_s = both[:, cs:]

        log_total = top + jnp.log(total)
        p = jnp.exp(scores - log_total)
        p_low = p.astype(BF)
        dp = jnp.einsum("qhd,khd->hqk", dattn_all, v, preferred_element_type=F32)
        inner = jnp.sum(p * dp, axis=-1, keepdims=True)
        ds = (p * (dp - inner)).astype(BF)
        dq = jnp.einsum("hqk,khd->qhd", ds, k, preferred_element_type=F32) * scale
        dk = jnp.einsum("hqk,qhd->khd", ds, q, preferred_element_type=F32) * scale
        dv = jnp.einsum("hqk,qhd->khd", p_low, dattn_all, preferred_element_type=F32)
        dqkv = jnp.concatenate([dq.reshape(L, cs), dk.reshape(L, cs), dv.reshape(L, cs)], 1).astype(BF)

        dh1_part = dot(dqkv, wq_s, ((1,), (1,)))
        g_ln1g = jnp.sum(dh1_part * unit1, 0)
        g_ln1b = jnp.sum(dh1_part, 0)
        dh1_low = dh1_part.astype(BF)
        dh1 = dh1_part[:t]
        for kk in range(1, S):
            dh1 = dh1 + exchange(dh1_low[kk * t:(kk + 1) * t], "seq", S, kk).astype(F32)
        d_tokens = (dx1 + norm_back(dh1, unit1[:t], scale1[:t], ln1_gain)).reshape(tokens.shape)

        g_wqkv = dot(h1, dqkv, ((0,), (0,)))
        g_wout = dot(attn_all, da_s, ((0,), (0,)))
        g_wout = jnp.take(g_wout.reshape(S, cs, cs), rel_s, axis=0).reshape(D, cs)
        bsum = jnp.sum(dqkv.astype(F32), 0)
        g_bqv = jnp.zeros((2, S, cs), F32)
        g_bqv = lax.dynamic_update_slice(g_bqv, jnp.stack([bsum[:cs], bsum[2 * cs:]])[:, None], (0, s, 0))
        small = jnp.concatenate(
            [v_.reshape(NB, -1) for v_ in (g_ln1g, g_ln1b, g_bqv, g_bout, g_ln2g, g_ln2b, g_bdn, g_bin)], 1)
        small_n = small.shape[1]
        small_rows = -(-small_n // D)
        pad_rows = -(-small_rows // 16) * 16
        small = jnp.pad(small, ((0, 0), (0, pad_rows * D - small_n))).reshape(NB, pad_rows, D)
        att = jnp.concatenate(
            [jnp.concatenate([g_wqkv.reshape(NB, R, 3 * cs), g_wout.reshape(NB, R, cs)], 2), small], 1).astype(BF)

        def reduce_batch(buf):
            buf = jnp.take(buf, rel_b, axis=0).reshape((NB // 2, 2) + buf.shape[1:])
            buf = (buf[:, 0].astype(F32) + exchange(buf[:, 1], "batch", NB, 1).astype(F32)).astype(BF)
            n = NB // 2
            while n > 4:
                n //= 2
                buf = (buf[:n].astype(F32) + exchange(buf[n:], "batch", NB, 2 * n).astype(F32)).astype(BF)
            acc = buf[0].astype(F32)
            for m in range(1, n):
                acc = acc + exchange(buf[m], "batch", NB, 2 * m).astype(F32)
            parts = jnp.stack(gather_seq(acc.astype(BF), S))
            return jnp.take(parts, rel_s, axis=0).astype(F32)

        mlp = reduce_batch(mlp)
        att = reduce_batch(att)
        o_win = mlp[:, :R].reshape(S, R, NB, FJ).transpose(1, 2, 0, 3).reshape(R, FF)
        o_wdn = mlp[:, R:].reshape(S * FJ, D)
        o_wqkv = att[:, :R, :3 * cs].reshape(S, R, 3, cs).transpose(1, 2, 0, 3).reshape(R, 3 * D)
        o_wout = att[:, :R, 3 * cs:].transpose(1, 0, 2).reshape(R, D)
        flat = att[:, R:].reshape(S, -1)
        o_bin = flat[:, 8 * R:8 * R + FJ].reshape(S * FJ)
        tot = jnp.sum(flat[:, :8 * R], 0)
        o_ln1g, o_ln1b, o_bqv, o_bout, o_ln2g, o_ln2b, o_bdn = (
            tot[:R], tot[R:2 * R], tot[2 * R:4 * R], tot[4 * R:5 * R], tot[5 * R:6 * R], tot[6 * R:7 * R], tot[7 * R:])
        return (activations.reshape(tokens.shape), d_tokens, o_ln1g, o_ln1b, o_wqkv, o_bqv, o_wout, o_bout,
                o_ln2g, o_ln2b, o_win, o_bin, o_wdn, o_bdn)
    return shards


def solution(mesh):
    rowwise = P("batch", "seq", None)
    placed = (rowwise, P("batch", None)) + (P(),) * 12 + (rowwise,)
    b, bn = P("batch"), P("batch", None)
    return jax.shard_map(
        make(mesh.shape["seq"], mesh.shape["batch"]),
        mesh=mesh,
        in_specs=placed,
        out_specs=(rowwise, rowwise, b, b, bn, b, bn, b, b, b, bn, b, bn, b),
        check_vma=False,
    )
```

time: 556 us -> 221 us (0.40)
  waiting for transfers between devices: 386 us -> 50.4 us
  blocking collectives: 63.3 us -> 0 us
  local copies, waits for them, and re-layouts: 26 us -> 68.9 us
  starting transfers between devices: 0.47 us -> 37 us
  matrix products: 53.4 us -> 31.9 us
  other arithmetic: 9.34 us -> 29.1 us
  between operations: 16.6 us -> 2.06 us
    reduce_scatter x6 -> x0, waiting for transfers between devices: 348 us -> none  [the longest x4 297 us: shards(): lax.psum_scatter(attn_grads + mlp_grads, 'batch', scatter_dimension=0, ti...]
    ppermute x0 -> x29, waiting for transfers between devices: none -> 50.4 us  [exchange(): return lax.ppermute(value, axis, [(j, j ^ step) for j in range(size)])]
    psum x1 -> x0, waiting for transfers between devices: 38 us -> none  [shards(): totals = lax.psum(shares, 'seq')]
    ppermute x0 -> x29, starting transfers between devices: none -> 37 us  [exchange(): return lax.ppermute(value, axis, [(j, j ^ step) for j in range(size)])]
    unnamed x1 -> x0, blocking collectives: 27.5 us -> none
    all_gather x2 -> x0, blocking collectives: 25.1 us -> none  [the longest x1 14.2 us: shards(): lax.all_gather(values, 'seq', axis=1, tiled=True)]
    dot_general x18, matrix products: 53.4 us -> 31.4 us  [the longest x12 27.7 us: dot(): return lax.dot_general(a, b, (dims, ((), ())), preferred_element_type=F32)]
    reshape x0 -> x16, local copies, waits for them, and re-layouts: none -> 14.7 us  [the longest x3 7.72 us: shards(): mlp[:, :R].reshape(S, R, NB, FJ).transpose(1, 2, 0, 3).reshape(R, FF)]
  transfers between devices with their start and end apart: 7 -> 29, of which waited for: 7 -> 9; matrix products, arithmetic and copies ran while one was open for 9% -> 43% of each run, Pallas kernels for 0% -> 0%
where the time goes in v1:
time: 221 us; the launch traced here: 219 us
  local copies, waits for them, and re-layouts  68.9 us (31%)
  waiting for transfers between devices  50.4 us (23%)
  starting transfers between devices  37 us (17%)
  matrix products  31.9 us (14%)
  other arithmetic  29.1 us (13%)
    ppermute x29, waiting for transfers between devices, exchange(): return lax.ppermute(value, axis, [(j, j ^ step) for j in range(size)])  50.4 us
    ppermute x29, starting transfers between devices, exchange(): return lax.ppermute(value, axis, [(j, j ^ step) for j in range(size)])  37 us
    dot_general x12, matrix products, dot(): return lax.dot_general(a, b, (dims, ((), ())), preferred_element_type=F32)  27.7 us
    unnamed x180, local copies, waits for them, and re-layouts  18.5 us
    reshape x3, local copies, waits for them, and re-layouts, shards(): mlp[:, :R].reshape(S, R, NB, FJ).transpose(1, 2, 0, 3).reshape(R, FF)  7.72 us
    gather x2, local copies, waits for them, and re-layouts, reduce_batch(): buf = jnp.take(buf, rel_b, axis=0).reshape((NB // 2, 2) + buf.shape[1:])  5.9 us
    select_n x3, other arithmetic, reduce_batch(): buf = jnp.take(buf, rel_b, axis=0).reshape((NB // 2, 2) + buf.shape[1:])  5.04 us
  transfers between devices with their start and end apart: 29, of which 9 were waited for; matrix products, arithmetic and copies ran while one was open for 43% of the time, Pallas kernels for 0%

profile of v1, /device:TPU:0, one launch (start us, length us, event | category | flops | bytes accessed | tf_op | source)
XLA Modules:
  0.0 219.4 jit_solution(1255401364208978340)
XLA Ops:
  0.7 4.0 %collective-permute-start.2 = (bf16[128,768]{1,0:T(8,128)(2,1)}, bf16[128,768]{1,0:T(8,128)(2,1)S(1)}, u32[]{:S(2)}, u32[]{:S(2)}) collective-permute-start(bf16[128,768]{1,0:T(8,128)(2,1)} %bitcast.207), channel_id=1, source_target_pairs={{0,24},{8,16},{16,8},{24,0},{1,25},{9,17},{17,9},{25,1},{2,26},{10... | collective-permute-start | bytes 589832 | tf_op jit(solution)/shard_map/ppermute | solution.py:17
  5.3 5.8 %copy.58 = bf16[768,2304]{0,1:T(8,128)(2,1)} copy(bf16[768,2304]{1,0:T(8,128)(2,1)} %param.21) | data formatting | bytes 7077888 | tf_op args[4]
  15.1 6.6 %copy.68 = bf16[768,3072]{0,1:T(8,128)(2,1)} copy(bf16[768,3072]{1,0:T(8,128)(2,1)} %param.27) | data formatting | bytes 9437184 | tf_op args[10]
  22.9 2.7 %constant_dynamic-slice_fusion.1 = bf16[768,8,1,96]{0,3,2,1:T(8,128)(2,1)} fusion(bf16[768,8,4,96]{0,3,2,1:T(8,128)(2,1)} %bitcast.158, s32[]{:T(128)S(6)} %select_n.97), kind=kLoop, calls=%fused_computation.170 | loop fusion | bytes 2359300 | tf_op jit(solution)/shard_map/dynamic_slice | solution.py:69
  26.4 2.4 %constant_dynamic-slice_fusion.2 = bf16[8,1,96,768]{3,2,1,0:T(8,128)(2,1)} fusion(bf16[8,4,96,768]{3,2,1,0:T(8,128)(2,1)} %bitcast.204, s32[]{:T(128)S(6)} %select_n.97), kind=kLoop, calls=%fused_computation.171 | loop fusion | bytes 2359300 | tf_op jit(solution)/shard_map/dynamic_slice | solution.py:71
  34.0 2.9 %collective-permute-start.5 = (bf16[512,192]{0,1:T(8,128)(2,1)S(1)}, bf16[512,192]{0,1:T(8,128)(2,1)S(1)}, u32[]{:S(2)}, u32[]{:S(2)}) collective-permute-start(bf16[512,192]{0,1:T(8,128)(2,1)S(1)} %bitcast.219), channel_id=1, source_target_pairs={{0,24},{8,16},{16,8},{24,0},{1,25},{9,17},{17,9},{25,1},{2,26},{10... | collective-permute-start | bytes 589832 | tf_op jit(solution)/shard_map/ppermute | solution.py:17
  41.7 4.2 %collective-permute-done.4 = bf16[512,192]{0,1:T(8,128)(2,1)S(1)} collective-permute-done((bf16[512,192]{0,1:T(8,128)(2,1)S(1)}, bf16[512,192]{0,1:T(8,128)(2,1)S(1)}, u32[]{:S(2)}, u32[]{:S(2)}) %collective-permute-start.4) | collective-permute-done | bytes 196640 | tf_op jit(solution)/shard_map/ppermute | solution.py:17
  54.4 8.6 %multiply_reduce_fusion.3 = (bf16[768]{0:T(1024)(128)(2,1)}, f32[128]{0:T(128)S(1)}, f32[128]{0:T(128)S(1)}, bf16[768]{0:T(1024)(128)(2,1)}, f32[128,768]{1,0:T(8,128)}) fusion(f32[512,768]{1,0:T(8,128)} %get-tuple-element.32, f32[768]{0:T(1024)S(1)} %copy-done.53, bf16[768,3072]{1,0:T(8,128)(2,1)} %param.27, bf16[3072,768]{1,0:T(8,128)(2,1)} %param.29, ...), kind=kOutput, calls=%fused_computation.117 | convolution fusion | flops 1216116992 | bytes 12000256 | tf_op jit(solution)/shard_map/dot_general | solution.py:13
  63.1 2.6 %fusion.83 = (bf16[768]{0:T(1024)(128)(2,1)}, bf16[128,768]{1,0:T(8,128)(2,1)S(1)}, f32[128,768]{1,0:T(8,128)}) fusion(f32[128]{0:T(128)} %slice.237, f32[128]{0:T(128)S(1)} %broadcast_multiply_fusion.4, f32[512,768]{1,0:T(8,128)} %get-tuple-element.32, f32[128]{0:T(128)S(1)} %broadcast_multiply_fusion.5, f32[128,768]{1,0:T(8,128)} %get-tuple-element.81, ...), kind=kLoop, calls=%fused_computation.199 | loop fusion | flops 883968 | bytes 1579008 | tf_op jit(solution)/shard_map/reduce_sum | solution.py:129
  66.5 2.6 %convolution_convert_fusion.3 = bf16[128,768]{1,0:T(8,128)(2,1)} fusion(bf16[128,768]{1,0:T(8,128)(2,1)S(1)} %get-tuple-element.28, bf16[768,768]{1,0:T(8,128)(2,1)} %bitcast.162), kind=kOutput, calls=%fused_computation.82 | convolution fusion | flops 151093248 | bytes 1572864 | tf_op jit(solution)/shard_map/dot_general | solution.py:13
  69.1 4.2 %fusion.34 = bf16[1,128,768]{2,1,0:T(8,128)(2,1)} fusion(bf16[3072,768]{1,0:T(8,128)(2,1)} %param.29, f32[128,3072]{1,0:T(8,128)S(1)} %copy-done.14, f32[512,768]{1,0:T(8,128)} %copy-done.6, f32[768]{0:T(1024)S(1)} %copy-done.81), kind=kOutput, calls=%fused_computation.83 | convolution fusion | flops 607813632 | bytes 6884352 | tf_op jit(solution)/shard_map/dot_general | solution.py:13
  92.5 3.9 %gather_fusion.5 = bf16[8,192,768]{2,1,0:T(8,128)(2,1)} fusion(bf16[8,192,768]{2,1,0:T(8,128)(2,1)} %pad_maximum_fusion, s32[1024]{0:T(1024)} %get-tuple-element.87), kind=kCustom, calls=%fused_computation.7 | custom fusion | bytes 4718624 | tf_op jit(solution)/shard_map/jit(_take)/gather | solution.py:174
  96.5 3.4 %broadcast_select_fusion = bf16[4,2,192,768]{3,2,1,0:T(8,128)(2,1)} fusion(bf16[4,2,192,768]{3,2,1,0:T(8,128)(2,1)} %bitcast.157, pred[4,2]{1,0:T(4,128)(4,1)S(1)} %copy-done.76), kind=kLoop, calls=%fused_computation.29 | loop fusion | flops 1179648 | bytes 4718600 | tf_op jit(solution)/shard_map/jit(_take)/select_n | solution.py:174
  110.4 2.6 %fusion.81 = (bf16[768]{0:T(1024)(128)(2,1)S(1)}, bf16[768]{0:T(1024)(128)(2,1)S(1)}, bf16[512,768]{1,0:T(8,128)(2,1)S(1)}, f32[512,768]{1,0:T(8,128)}, f32[512,768]{1,0:T(8,128)}) fusion(f32[512]{0:T(512)S(1)} %copy-done.71, f32[512]{0:T(512)S(1)} %copy-done.56, bf16[512,768]{1,0:T(8,128)(2,1)S(1)} %copy-done.4, bf16[768,576]{0,1:T(8,128)(2,1)S(1)} %bitcast.185, ...), kind=kOutput, calls=%fused_computation.197 | convolution fusion | flops 457505280 | bytes 6200320 | tf_op jit(solution)/shard_map/dot_general | solution.py:13
  129.6 3.7 %collective-permute-start.18 = (bf16[112,768]{1,0:T(8,128)(2,1)S(1)}, bf16[112,768]{1,0:T(8,128)(2,1)S(1)}, u32[]{:S(2)}, u32[]{:S(2)}) collective-permute-start(bf16[112,768]{1,0:T(8,128)(2,1)S(1)} %get-tuple-element.44), channel_id=1, source_target_pairs={{0,6},{1,7},{2,4},{3,5},{4,2},{5,3},{6,0},{7,1},{8,14},{9,15},{10,... | collective-permute-start | bytes 516104 | tf_op jit(solution)/shard_map/ppermute | solution.py:17
  134.1 4.7 %collective-permute-done.18 = bf16[112,768]{1,0:T(8,128)(2,1)S(1)} collective-permute-done((bf16[112,768]{1,0:T(8,128)(2,1)S(1)}, bf16[112,768]{1,0:T(8,128)(2,1)S(1)}, u32[]{:S(2)}, u32[]{:S(2)}) %collective-permute-start.18) | collective-permute-done | bytes 172064 | tf_op jit(solution)/shard_map/ppermute | solution.py:17
  138.8 9.5 %collective-permute-done.17 = bf16[112,768]{1,0:T(8,128)(2,1)S(1)} collective-permute-done((bf16[112,768]{1,0:T(8,128)(2,1)S(1)}, bf16[112,768]{1,0:T(8,128)(2,1)S(1)}, u32[]{:S(2)}, u32[]{:S(2)}) %collective-permute-start.17) | collective-permute-done | bytes 172064 | tf_op jit(solution)/shard_map/ppermute | solution.py:17
  152.9 3.8 %collective-permute-done.21 = bf16[112,768]{1,0:T(8,128)(2,1)S(1)} collective-permute-done((bf16[112,768]{1,0:T(8,128)(2,1)S(1)}, bf16[112,768]{1,0:T(8,128)(2,1)S(1)}, u32[]{:S(2)}, u32[]{:S(2)}) %collective-permute-start.21) | collective-permute-done | bytes 172064 | tf_op jit(solution)/shard_map/ppermute | solution.py:17
  163.6 2.5 %collective-permute-start.25 = (bf16[192,768]{1,0:T(8,128)(2,1)S(1)}, bf16[192,768]{1,0:T(8,128)(2,1)}, u32[]{:S(2)}, u32[]{:S(2)}) collective-permute-start(bf16[192,768]{1,0:T(8,128)(2,1)S(1)} %get-tuple-element.37), channel_id=1, source_target_pairs={{0,6},{1,7},{2,4},{3,5},{4,2},{5,3},{6,0},{7,1},{8,14},{9,15},{10,... | collective-permute-start | bytes 884744 | tf_op jit(solution)/shard_map/ppermute | solution.py:17
  172.3 3.2 %collective-permute-done.25 = bf16[192,768]{1,0:T(8,128)(2,1)} collective-permute-done((bf16[192,768]{1,0:T(8,128)(2,1)S(1)}, bf16[192,768]{1,0:T(8,128)(2,1)}, u32[]{:S(2)}, u32[]{:S(2)}) %collective-permute-start.25) | collective-permute-done | bytes 294944 | tf_op jit(solution)/shard_map/ppermute | solution.py:17
  175.5 14.8 %collective-permute-done.24 = bf16[192,768]{1,0:T(8,128)(2,1)} collective-permute-done((bf16[192,768]{1,0:T(8,128)(2,1)S(1)}, bf16[192,768]{1,0:T(8,128)(2,1)}, u32[]{:S(2)}, u32[]{:S(2)}) %collective-permute-start.24) | collective-permute-done | bytes 294944 | tf_op jit(solution)/shard_map/ppermute | solution.py:17
  198.4 4.2 %collective-permute-done.28 = bf16[192,768]{1,0:T(8,128)(2,1)S(1)} collective-permute-done((bf16[192,768]{1,0:T(8,128)(2,1)S(1)}, bf16[192,768]{1,0:T(8,128)(2,1)S(1)}, u32[]{:S(2)}, u32[]{:S(2)}) %collective-permute-start.28) | collective-permute-done | bytes 294944 | tf_op jit(solution)/shard_map/ppermute | solution.py:17
  202.7 4.1 %collective-permute-done.27 = bf16[192,768]{1,0:T(8,128)(2,1)S(1)} collective-permute-done((bf16[192,768]{1,0:T(8,128)(2,1)S(1)}, bf16[192,768]{1,0:T(8,128)(2,1)S(1)}, u32[]{:S(2)}, u32[]{:S(2)}) %collective-permute-start.27) | collective-permute-done | bytes 294944 | tf_op jit(solution)/shard_map/ppermute | solution.py:17
  215.8 3.6 %reshape.464 = f32[96,3072]{1,0:T(8,128)} reshape(f32[96,8,4,96]{3,2,1,0:T(4,128)} %bitcast.159) | data formatting | bytes 2359296 | tf_op jit(solution)/shard_map/reshape | solution.py:188
  (355 shorter events, 106.8 us)
Async XLA Ops:
  0.7 29.8 %collective-permute-start.2 = (bf16[128,768]{1,0:T(8,128)(2,1)}, bf16[128,768]{1,0:T(8,128)(2,1)S(1)}, u32[]{:S(2)}, u32[]{:S(2)}) collective-permute-start(bf16[128,768]{1,0:T(8,128)(2,1)} %bitcast.207), channel_id=1, source_target_pairs={{0,24},{8,16},{16,8},{24,0},{1,25},{9,17},{17,9},{25,1},{2,26},{10... | collective-permute-start | bytes 589832 | tf_op jit(solution)/shard_map/ppermute | solution.py:17
  4.6 25.8 %collective-permute-start.1 = (bf16[128,768]{1,0:T(8,128)(2,1)}, bf16[128,768]{1,0:T(8,128)(2,1)S(1)}, u32[]{:S(2)}, u32[]{:S(2)}) collective-permute-start(bf16[128,768]{1,0:T(8,128)(2,1)} %bitcast.208), channel_id=1, source_target_pairs={{0,16},{8,24},{16,0},{24,8},{1,17},{9,25},{17,1},{25,9},{2,18},{10... | collective-permute-start | bytes 589832 | tf_op jit(solution)/shard_map/ppermute | solution.py:17
  5.1 25.3 %collective-permute-start = (bf16[128,768]{1,0:T(8,128)(2,1)}, bf16[128,768]{1,0:T(8,128)(2,1)S(1)}, u32[]{:S(2)}, u32[]{:S(2)}) collective-permute-start(bf16[128,768]{1,0:T(8,128)(2,1)} %bitcast.209), channel_id=1, source_target_pairs={{0,8},{8,0},{16,24},{24,16},{1,9},{9,1},{17,25},{25,17},{2,10},{10... | collective-permute-start | bytes 589832 | tf_op jit(solution)/shard_map/ppermute | solution.py:17
  34.0 14.0 %collective-permute-start.5 = (bf16[512,192]{0,1:T(8,128)(2,1)S(1)}, bf16[512,192]{0,1:T(8,128)(2,1)S(1)}, u32[]{:S(2)}, u32[]{:S(2)}) collective-permute-start(bf16[512,192]{0,1:T(8,128)(2,1)S(1)} %bitcast.219), channel_id=1, source_target_pairs={{0,24},{8,16},{16,8},{24,0},{1,25},{9,17},{17,9},{25,1},{2,26},{10... | collective-permute-start | bytes 589832 | tf_op jit(solution)/shard_map/ppermute | solution.py:17
  37.4 10.7 %collective-permute-start.3 = (bf16[512,192]{0,1:T(8,128)(2,1)S(1)}, bf16[512,192]{0,1:T(8,128)(2,1)S(1)}, u32[]{:S(2)}, u32[]{:S(2)}) collective-permute-start(bf16[512,192]{0,1:T(8,128)(2,1)S(1)} %bitcast.221), channel_id=1, source_target_pairs={{0,8},{8,0},{16,24},{24,16},{1,9},{9,1},{17,25},{25,17},{2,10},{10... | collective-permute-start | bytes 589832 | tf_op jit(solution)/shard_map/ppermute | solution.py:17
  38.3 44.5 %collective-permute-start.12 = (bf16[128,768]{1,0:T(8,128)(2,1)S(1)}, bf16[128,768]{1,0:T(8,128)(2,1)}, u32[]{:S(2)}, u32[]{:S(2)}) collective-permute-start(bf16[128,768]{1,0:T(8,128)(2,1)S(1)} %bitcast.169), channel_id=1, source_target_pairs={{0,8},{8,0},{16,24},{24,16},{1,9},{9,1},{17,25},{25,17},{2,10},{10... | collective-permute-start | bytes 589832 | tf_op jit(solution)/shard_map/ppermute | solution.py:17
  40.1 45.4 %collective-permute-start.13 = (bf16[128,768]{1,0:T(8,128)(2,1)S(1)}, bf16[128,768]{1,0:T(8,128)(2,1)}, u32[]{:S(2)}, u32[]{:S(2)}) collective-permute-start(bf16[128,768]{1,0:T(8,128)(2,1)S(1)} %bitcast.170), channel_id=1, source_target_pairs={{0,16},{8,24},{16,0},{24,8},{1,17},{9,25},{17,1},{25,9},{2,18},{10... | collective-permute-start | bytes 589832 | tf_op jit(solution)/shard_map/ppermute | solution.py:17
  45.9 40.6 %collective-permute-start.14 = (bf16[128,768]{1,0:T(8,128)(2,1)S(1)}, bf16[128,768]{1,0:T(8,128)(2,1)}, u32[]{:S(2)}, u32[]{:S(2)}) collective-permute-start(bf16[128,768]{1,0:T(8,128)(2,1)S(1)} %bitcast.171), channel_id=1, source_target_pairs={{0,24},{8,16},{16,8},{24,0},{1,25},{9,17},{17,9},{25,1},{2,26},{10... | collective-permute-start | bytes 589832 | tf_op jit(solution)/shard_map/ppermute | solution.py:17
  78.8 23.7 %collective-permute-start.8 = (bf16[128,384]{1,0:T(8,128)(2,1)}, bf16[128,384]{1,0:T(8,128)(2,1)}, u32[]{:S(2)}, u32[]{:S(2)}) collective-permute-start(bf16[128,384]{1,0:T(8,128)(2,1)} %pad_maximum_fusion.9), channel_id=1, source_target_pairs={{0,24},{8,16},{16,8},{24,0},{1,25},{9,17},{17,9},{25,1},{2,26},{10... | collective-permute-start | bytes 294920 | tf_op jit(solution)/shard_map/ppermute | solution.py:17
  80.4 22.2 %collective-permute-start.7 = (bf16[128,384]{1,0:T(8,128)(2,1)}, bf16[128,384]{1,0:T(8,128)(2,1)}, u32[]{:S(2)}, u32[]{:S(2)}) collective-permute-start(bf16[128,384]{1,0:T(8,128)(2,1)} %pad_maximum_fusion.8), channel_id=1, source_target_pairs={{0,16},{8,24},{16,0},{24,8},{1,17},{9,25},{17,1},{25,9},{2,18},{10... | collective-permute-start | bytes 294920 | tf_op jit(solution)/shard_map/ppermute | solution.py:17
  82.8 19.7 %collective-permute-start.6 = (bf16[128,384]{1,0:T(8,128)(2,1)}, bf16[128,384]{1,0:T(8,128)(2,1)}, u32[]{:S(2)}, u32[]{:S(2)}) collective-permute-start(bf16[128,384]{1,0:T(8,128)(2,1)} %pad_maximum_fusion.7), channel_id=1, source_target_pairs={{0,8},{8,0},{16,24},{24,16},{1,9},{9,1},{17,25},{25,17},{2,10},{10... | collective-permute-start | bytes 294920 | tf_op jit(solution)/shard_map/ppermute | solution.py:17
  116.5 11.4 %collective-permute-start.11 = (bf16[128,768]{1,0:T(8,128)(2,1)}, bf16[128,768]{1,0:T(8,128)(2,1)S(1)}, u32[]{:S(2)}, u32[]{:S(2)}) collective-permute-start(bf16[128,768]{1,0:T(8,128)(2,1)} %get-tuple-element.41), channel_id=1, source_target_pairs={{0,24},{8,16},{16,8},{24,0},{1,25},{9,17},{17,9},{25,1},{2,26},{10... | collective-permute-start | bytes 589832 | tf_op jit(solution)/shard_map/ppermute | solution.py:17
  117.3 10.6 %collective-permute-start.10 = (bf16[128,768]{1,0:T(8,128)(2,1)}, bf16[128,768]{1,0:T(8,128)(2,1)}, u32[]{:S(2)}, u32[]{:S(2)}) collective-permute-start(bf16[128,768]{1,0:T(8,128)(2,1)} %get-tuple-element.42), channel_id=1, source_target_pairs={{0,16},{8,24},{16,0},{24,8},{1,17},{9,25},{17,1},{25,9},{2,18},{10... | collective-permute-start | bytes 589832 | tf_op jit(solution)/shard_map/ppermute | solution.py:17
  118.2 9.7 %collective-permute-start.9 = (bf16[128,768]{1,0:T(8,128)(2,1)}, bf16[128,768]{1,0:T(8,128)(2,1)}, u32[]{:S(2)}, u32[]{:S(2)}) collective-permute-start(bf16[128,768]{1,0:T(8,128)(2,1)} %get-tuple-element.40), channel_id=1, source_target_pairs={{0,8},{8,0},{16,24},{24,16},{1,9},{9,1},{17,25},{25,17},{2,10},{10... | collective-permute-start | bytes 589832 | tf_op jit(solution)/shard_map/ppermute | solution.py:17
  127.7 33.8 %collective-permute-start.22 = (bf16[4,192,768]{2,1,0:T(8,128)(2,1)}, bf16[4,192,768]{2,1,0:T(8,128)(2,1)}, u32[]{:S(2)}, u32[]{:S(2)}) collective-permute-start(bf16[4,192,768]{2,1,0:T(8,128)(2,1)} %slice_bitcast_fusion), channel_id=1, source_target_pairs={{0,1},{1,0},{2,3},{3,2},{4,5},{5,4},{6,7},{7,6},{8,9},{9,8},{10,11... | collective-permute-start | bytes 3538952 | tf_op jit(solution)/shard_map/ppermute | solution.py:17
  129.6 9.2 %collective-permute-start.18 = (bf16[112,768]{1,0:T(8,128)(2,1)S(1)}, bf16[112,768]{1,0:T(8,128)(2,1)S(1)}, u32[]{:S(2)}, u32[]{:S(2)}) collective-permute-start(bf16[112,768]{1,0:T(8,128)(2,1)S(1)} %get-tuple-element.44), channel_id=1, source_target_pairs={{0,6},{1,7},{2,4},{3,5},{4,2},{5,3},{6,0},{7,1},{8,14},{9,15},{10,... | collective-permute-start | bytes 516104 | tf_op jit(solution)/shard_map/ppermute | solution.py:17
  133.3 15.0 %collective-permute-start.17 = (bf16[112,768]{1,0:T(8,128)(2,1)S(1)}, bf16[112,768]{1,0:T(8,128)(2,1)S(1)}, u32[]{:S(2)}, u32[]{:S(2)}) collective-permute-start(bf16[112,768]{1,0:T(8,128)(2,1)S(1)} %get-tuple-element.45), channel_id=1, source_target_pairs={{0,4},{1,5},{2,6},{3,7},{4,0},{5,1},{6,2},{7,3},{8,12},{9,13},{10,... | collective-permute-start | bytes 516104 | tf_op jit(solution)/shard_map/ppermute | solution.py:17
  133.3 15.0 %collective-permute-start.16 = (bf16[112,768]{1,0:T(8,128)(2,1)S(1)}, bf16[112,768]{1,0:T(8,128)(2,1)S(1)}, u32[]{:S(2)}, u32[]{:S(2)}) collective-permute-start(bf16[112,768]{1,0:T(8,128)(2,1)S(1)} %get-tuple-element.43), channel_id=1, source_target_pairs={{0,2},{1,3},{2,0},{3,1},{4,6},{5,7},{6,4},{7,5},{8,10},{9,11},{10,... | collective-permute-start | bytes 516104 | tf_op jit(solution)/shard_map/ppermute | solution.py:17
  163.6 12.0 %collective-permute-start.25 = (bf16[192,768]{1,0:T(8,128)(2,1)S(1)}, bf16[192,768]{1,0:T(8,128)(2,1)}, u32[]{:S(2)}, u32[]{:S(2)}) collective-permute-start(bf16[192,768]{1,0:T(8,128)(2,1)S(1)} %get-tuple-element.37), channel_id=1, source_target_pairs={{0,6},{1,7},{2,4},{3,5},{4,2},{5,3},{6,0},{7,1},{8,14},{9,15},{10,... | collective-permute-start | bytes 884744 | tf_op jit(solution)/shard_map/ppermute | solution.py:17
  166.1 24.3 %collective-permute-start.24 = (bf16[192,768]{1,0:T(8,128)(2,1)S(1)}, bf16[192,768]{1,0:T(8,128)(2,1)}, u32[]{:S(2)}, u32[]{:S(2)}) collective-permute-start(bf16[192,768]{1,0:T(8,128)(2,1)S(1)} %get-tuple-element.38), channel_id=1, source_target_pairs={{0,4},{1,5},{2,6},{3,7},{4,0},{5,1},{6,2},{7,3},{8,12},{9,13},{10,... | collective-permute-start | bytes 884744 | tf_op jit(solution)/shard_map/ppermute | solution.py:17
  166.1 24.3 %collective-permute-start.23 = (bf16[192,768]{1,0:T(8,128)(2,1)S(1)}, bf16[192,768]{1,0:T(8,128)(2,1)}, u32[]{:S(2)}, u32[]{:S(2)}) collective-permute-start(bf16[192,768]{1,0:T(8,128)(2,1)S(1)} %get-tuple-element.36), channel_id=1, source_target_pairs={{0,2},{1,3},{2,0},{3,1},{4,6},{5,7},{6,4},{7,5},{8,10},{9,11},{10,... | collective-permute-start | bytes 884744 | tf_op jit(solution)/shard_map/ppermute | solution.py:17
  191.8 10.9 %collective-permute-start.28 = (bf16[192,768]{1,0:T(8,128)(2,1)S(1)}, bf16[192,768]{1,0:T(8,128)(2,1)S(1)}, u32[]{:S(2)}, u32[]{:S(2)}) collective-permute-start(bf16[192,768]{1,0:T(8,128)(2,1)S(1)} %fusion.51), channel_id=1, source_target_pairs={{0,24},{8,16},{16,8},{24,0},{1,25},{9,17},{17,9},{25,1},{2,26},{10... | collective-permute-start | bytes 884744 | tf_op jit(solution)/shard_map/ppermute | solution.py:17
  193.1 13.6 %collective-permute-start.27 = (bf16[192,768]{1,0:T(8,128)(2,1)S(1)}, bf16[192,768]{1,0:T(8,128)(2,1)S(1)}, u32[]{:S(2)}, u32[]{:S(2)}) collective-permute-start(bf16[192,768]{1,0:T(8,128)(2,1)S(1)} %fusion.51), channel_id=1, source_target_pairs={{0,16},{8,24},{16,0},{24,8},{1,17},{9,25},{17,1},{25,9},{2,18},{10... | collective-permute-start | bytes 884744 | tf_op jit(solution)/shard_map/ppermute | solution.py:17
  194.0 12.7 %collective-permute-start.26 = (bf16[192,768]{1,0:T(8,128)(2,1)S(1)}, bf16[192,768]{1,0:T(8,128)(2,1)S(1)}, u32[]{:S(2)}, u32[]{:S(2)}) collective-permute-start(bf16[192,768]{1,0:T(8,128)(2,1)S(1)} %fusion.51), channel_id=1, source_target_pairs={{0,8},{8,0},{16,24},{24,16},{1,9},{9,1},{17,25},{25,17},{2,10},{10... | collective-permute-start | bytes 884744 | tf_op jit(solution)/shard_map/ppermute | solution.py:17
  (92 other events, 404.0 us)

commit v2 on v1

--- a/solution.py
+++ b/solution.py
@@ -1,16 +1,22 @@
+import functools
+
 import jax
 import jax.numpy as jnp
 from jax import lax
+from jax.experimental import pallas as pl
+from jax.experimental.pallas import tpu as pltpu
 from jax.sharding import PartitionSpec as P
 
 HEADS = 12
 HEAD_DIM = 64
+BLOCK_ROWS = HEADS * HEAD_DIM
 BF = jnp.bfloat16
 F32 = jnp.float32
-
-
-def dot(a, b, dims=((1,), (0,))):
-    return lax.dot_general(a, b, (dims, ((), ())), preferred_element_type=F32)
+MIB = 1 << 20
+
+
+def dot(a, b, ca=1, cb=0):
+    return lax.dot_general(a, b, (((ca,), (cb,)), ((), ())), preferred_element_type=F32)
 
 
 def exchange(value, axis, size, step):
@@ -19,6 +25,19 @@
 
 def gather_seq(value, size):
     return [value] + [exchange(value, "seq", size, k) for k in range(1, size)]
+
+
+def gather_steps(value, size, steps):
+    arrays, ks = [value], [[0]]
+    held = value[None]
+    for step in steps:
+        got = exchange(held, "seq", size, step)
+        ks.append([k ^ step for part in ks for k in part])
+        arrays.append(got)
+        if step != steps[-1]:
+            held = jnp.concatenate([held, got], 0)
+    arrays = [a if len(k) > 1 else a.reshape(value.shape) for a, k in zip(arrays, ks)]
+    return arrays, ks
 
 
 def norm_parts(values):
@@ -38,14 +57,476 @@
 
 def gelu_both(v):
     c = 0.7978845608028654
-    inner = c * (v + 0.044715 * v * v * v)
-    t = jnp.tanh(inner)
-    value = 0.5 * v * (1.0 + t)
-    slope = 0.5 * (1.0 + t) + 0.5 * v * (1.0 - t * t) * c * (1.0 + 3.0 * 0.044715 * v * v)
-    return value, slope
+    square = v * v
+    t = jnp.tanh(c * v * (1.0 + 0.044715 * square))
+    half = 0.5 * (1.0 + t)
+    slope = half + (0.5 * c) * v * (1.0 - t * t) * (1.0 + 3.0 * 0.044715 * square)
+    return v * half, slope
+
+
+def call(kernel, outs, args, name, flops=0, limit=24):
+    size = sum(a.size * a.dtype.itemsize for a in args) + sum(o.size * o.dtype.itemsize for o in outs)
+    return pl.pallas_call(
+        kernel,
+        out_shape=outs,
+        name=name,
+        cost_estimate=pl.CostEstimate(flops=flops, bytes_accessed=size, transcendentals=0),
+        compiler_params=pltpu.CompilerParams(vmem_limit_bytes=limit * MIB),
+    )(*args)
+
+
+def sds(shape, dtype):
+    return jax.ShapeDtypeStruct(shape, dtype)
+
+
+def flat(ref):
+    return ref[...].reshape(1, -1)
 
 
 def make(S, NB):
+    def rel_row(row, t):
+        s = lax.axis_index("seq")
+        parts = [row[:, i * t:(i + 1) * t] for i in range(S)]
+        bit = 1
+        while bit < S:
+            on = (s & bit) != 0
+            parts = [jnp.where(on, parts[i ^ bit], parts[i]) for i in range(S)]
+            bit *= 2
+        return jnp.concatenate(parts, 1)
+
+    def prep_qkv_kernel(wqkv, pack, wq_o, bq_o, row_o, col_o):
+        D = wqkv.shape[0]
+        cs = D // S
+        L = row_o.shape[1]
+        s = lax.axis_index("seq")
+        row = rel_row(pack[4:5, :L], L // S)
+        row_o[...] = jnp.broadcast_to(row, row_o.shape)
+        col_o[...] = jnp.transpose(jnp.broadcast_to(row, (128, L)))
+        bq_o[0:2, :] = pack[0:2, :]
+        for p in range(S):
+            @pl.when(s == p)
+            def _(p=p):
+                for c in range(3):
+                    wq_o[:, c * cs:(c + 1) * cs] = wqkv[:, c * D + p * cs:c * D + (p + 1) * cs]
+                zero = jnp.zeros((1, cs), F32)
+                bq_o[2:3, :] = jnp.concatenate(
+                    [pack[2:3, p * cs:(p + 1) * cs], zero, pack[3:4, p * cs:(p + 1) * cs], zero], 1)
+
+    def prep_mlp_kernel(win, wout, wdown, bout, ln2g, ln2b, bin_, bdown, win_o, wout_o, wdn_o, pack_o):
+        D = wout.shape[0]
+        FF = win.shape[1]
+        cs = D // S
+        FJ = FF // (NB * S)
+        s = lax.axis_index("seq")
+        vin = flat(bin_)
+        pack_o[3:4, :] = flat(bout)
+        pack_o[4:5, :] = flat(ln2g)
+        pack_o[5:6, :] = flat(ln2b)
+        pack_o[7:8, :] = flat(bdown)
+        for c in range(FF // D):
+            pack_o[8 + c:9 + c, :] = vin[:, c * D:(c + 1) * D]
+        for m in range(S):
+            wout_o[m * cs:(m + 1) * cs, :] = wout[pl.ds(pl.multiple_of((s ^ m) * cs, 16), cs), :]
+        for i in range(NB):
+            wdn_o[i * FJ:(i + 1) * FJ, :] = wdown[pl.ds(pl.multiple_of((i * S + s) * FJ, 16), FJ), :]
+        for p in range(S):
+            @pl.when(s == p)
+            def _(p=p):
+                for i in range(NB):
+                    at = (i * S + p) * FJ
+                    win_o[:, i * FJ:(i + 1) * FJ] = win[:, at:at + FJ]
+                pack_o[6:7, :] = jnp.concatenate(
+                    [vin[:, (i * S + p) * FJ:(i * S + p + 1) * FJ] for i in range(NB)], 1)
+
+    def attn_fwd_kernel(*refs):
+        xs, (row_ref, col_ref, pack, wq_ref, attn_o, qkv_o, lse_o) = refs[:S], refs[S:]
+        t, D = xs[0].shape
+        L = S * t
+        cs = D // S
+        for k in range(S):
+            unit, _ = norm_parts(xs[k][...].astype(F32))
+            h1 = (unit * pack[0:1, :] + pack[1:2, :]).astype(BF)
+            qkv_o[k * t:(k + 1) * t, :] = (dot(h1, wq_ref[...]) + pack[2:3, :3 * cs]).astype(BF)
+        row = row_ref[0:1, :]
+        outs = [[] for _ in range(S)]
+        for h in range(cs // HEAD_DIM):
+            at = h * HEAD_DIM
+            keys = qkv_o[:, cs + at:cs + at + HEAD_DIM]
+            vals = qkv_o[:, 2 * cs + at:2 * cs + at + HEAD_DIM]
+            for k in range(S):
+                q = qkv_o[k * t:(k + 1) * t, at:at + HEAD_DIM]
+                sc = dot(q, keys, 1, 1) * (HEAD_DIM ** -0.5)
+                sc = jnp.where(col_ref[k * t:(k + 1) * t, :1] == row, sc, -1e30)
+                top = jnp.max(sc, axis=-1, keepdims=True)
+                ex = jnp.exp(sc - top)
+                total = jnp.sum(ex, axis=-1, keepdims=True)
+                pr = (ex * (1.0 / total)).astype(BF)
+                outs[k].append(dot(pr, vals).astype(BF))
+                lse_o[k * t:(k + 1) * t, h:h + 1] = top + jnp.log(total)
+        blocks = [jnp.concatenate(o, 1) for o in outs]
+        half = S // 2
+        for k in range(half):
+            attn_o[k * t:(k + 1) * t, :] = jnp.concatenate([blocks[k], blocks[k + half]], 1)
+
+    def order():
+        bits = NB.bit_length() - 1
+        return [int(format(p, "b").zfill(bits)[::-1], 2) for p in range(NB)]
+
+    def store_blocks(scr, keep_o, send_o, b):
+        for p, m in enumerate(order()):
+            o, at = (keep_o, p) if p < NB // 2 else (send_o, p - NB // 2)
+            o[at] = scr[b ^ m].astype(BF)
+
+    def up_kernel(*refs):
+        xs, ats, cots = refs[:S], refs[S:2 * S], refs[2 * S:3 * S]
+        (wout, pack, win, attn_all, h2_o, slope_o, keep_o, send_o, act_s, cot_s, gw_s) = refs[3 * S:]
+        t, D = xs[0].shape
+        cs = D // S
+        FJ = win.shape[1] // NB
+        half = S // 2
+        b = lax.axis_index("batch")
+        for k in range(S):
+            pieces = []
+            for m in range(S):
+                j = k ^ m
+                lo, hi = (j % half) * t, (j // half) * cs
+                pieces.append(ats[m][lo:lo + t, hi:hi + cs])
+            attn_all[k * t:(k + 1) * t, :] = jnp.concatenate(pieces, 1)
+        for k in range(S):
+            rows = slice(k * t, (k + 1) * t)
+            x1 = xs[k][...].astype(F32) + dot(attn_all[rows, :], wout[...]) + pack[3:4, :]
+            unit, _ = norm_parts(x1)
+            h2 = (unit * pack[4:5, :] + pack[5:6, :]).astype(BF)
+            h2_o[rows, :] = h2
+            u = dot(h2, win[...]) + pack[6:7, :]
+            act, slope = gelu_both(u)
+            act_s[rows, :] = act.astype(BF)
+            slope_o[rows, :] = slope
+            cot_s[rows, :] = cots[k][...]
+        gw_s[...] = dot(act_s[...], cot_s[...], 0, 0).reshape(NB, FJ, D)
+        store_blocks(gw_s, keep_o, send_o, b)
+
+    def down_kernel(*refs):
+        cots, boths = refs[:S], refs[S:2 * S]
+        h2, slope, wdn, attn_all, vec, keep_o, send_o, du_s, da_s, gw_s = refs[2 * S:]
+        t, D = cots[0].shape
+        R = D // NB
+        cs = D // S
+        NF = slope.shape[1]
+        s = lax.axis_index("seq")
+        b = lax.axis_index("batch")
+        gbin = jnp.zeros((1, NF), F32)
+        for k in range(S):
+            rows = slice(k * t, (k + 1) * t)
+            du = (dot(cots[k][...], wdn[...], 1, 1) * slope[rows, :]).astype(BF)
+            du_s[rows, :] = du
+            da_s[rows, :] = boths[k][:, cs:]
+            gbin = gbin + jnp.sum(du.astype(F32), axis=0, keepdims=True)
+        gw_s[:, :, :NF] = dot(h2[...], du_s[...], 0, 0).reshape(NB, R, NF)
+        go = dot(attn_all[...], da_s[...], 0, 0)
+        per = NB // S
+        for m in range(S):
+            for j in range(per):
+                gw_s[(s ^ m) * per + j, :, NF:NF + cs] = go[m * cs + j * R:m * cs + (j + 1) * R, :]
+        gw_s[:, :, NF + cs:] = columns([vec[:4, :], gbin], gw_s.shape[2] - NF - cs)
+        store_blocks(gw_s, keep_o, send_o, b)
+
+    def columns(rows, width):
+        rows = jnp.concatenate(rows, 0)
+        D = rows.shape[1]
+        rows = jnp.concatenate([rows, jnp.zeros((128 - rows.shape[0], D), F32)], 0)
+        return jnp.transpose(rows)[:, :width].reshape(NB, D // NB, width)
+
+    def local_kernel(*refs):
+        x_ref, ats, refs = refs[0], refs[1:1 + S], refs[1 + S:]
+        cot_ref, wout, pack, win, wdown = refs[:5]
+        refs = refs[5:]
+        out_o, dx1_o, vec_o = refs[0], refs[1], refs[2]
+        both = refs[3:3 + S]
+        t, D = x_ref.shape
+        FF = win.shape[1]
+        cs = D // S
+        s = lax.axis_index("seq")
+        half = S // 2
+        attn = jnp.concatenate(
+            [ats[m][(m % half) * t:(m % half + 1) * t, (m // half) * cs:(m // half + 1) * cs] for m in range(S)], 1)
+        x1 = x_ref[...].astype(F32) + dot(attn, wout[...]) + pack[3:4, :]
+        unit, scale = norm_parts(x1)
+        h2 = (unit * pack[4:5, :] + pack[5:6, :]).astype(BF)
+        cot = cot_ref[...]
+        C = D
+        mixed = jnp.zeros((t, D), F32)
+        dh2 = jnp.zeros((t, D), F32)
+        for c in range(FF // C):
+            cols = slice(c * C, (c + 1) * C)
+            u = dot(h2, win[:, cols]) + pack[8 + c:9 + c, :]
+            act, slope = gelu_both(u)
+            mixed = mixed + dot(act.astype(BF), wdown[cols, :])
+            du = (dot(cot, wdown[cols, :], 1, 1) * slope).astype(BF)
+            dh2 = dh2 + dot(du, win[:, cols], 1, 1)
+        out_o[...] = (x1 + mixed + pack[7:8, :]).astype(BF)
+        dy = cot.astype(F32)
+        dx1 = dy + norm_back(dh2, unit, scale, pack[4:5, :])
+        dx1_o[...] = dx1
+        da = dx1.astype(BF)
+        vec_o[...] = jnp.concatenate([
+            jnp.sum(da.astype(F32), axis=0, keepdims=True),
+            jnp.sum(dh2 * unit, axis=0, keepdims=True),
+            jnp.sum(dh2, axis=0, keepdims=True),
+            jnp.sum(dy, axis=0, keepdims=True),
+            jnp.zeros((4, D), F32)], 0)
+        dattn = dot(da, wout[...], 1, 1).astype(BF)
+        parts = [da[:, i * cs:(i + 1) * cs] for i in range(S)]
+        bit = 1
+        while bit < S:
+            on = (s & bit) != 0
+            parts = [jnp.where(on, parts[i ^ bit], parts[i]) for i in range(S)]
+            bit *= 2
+        for k in range(S):
+            both[k][...] = jnp.concatenate([dattn[:, k * cs:(k + 1) * cs], parts[k]], 1)
+
+    def attn_bwd_kernel(*refs):
+        xs, boths = refs[:S], refs[S:2 * S]
+        row_ref, col_ref, pack, wq, qkv, lse = refs[2 * S:2 * S + 6]
+        own_o, next_o, away_o, keep_o, send_o, h1_s, dqkv_s, gw_s = refs[2 * S + 6:]
+        t, D = xs[0].shape
+        L = S * t
+        cs = D // S
+        R = D // NB
+        s = lax.axis_index("seq")
+        b = lax.axis_index("batch")
+        scale = HEAD_DIM ** -0.5
+        row = row_ref[0:1, :]
+        dattn = jnp.concatenate([r[:, :cs] for r in boths], 0)
+        dattn_t = jnp.transpose(dattn)
+        q_t = jnp.transpose(qkv[:, :cs])
+        for h in range(cs // HEAD_DIM):
+            at = h * HEAD_DIM
+            keys = qkv[:, cs + at:cs + at + HEAD_DIM]
+            vals = qkv[:, 2 * cs + at:2 * cs + at + HEAD_DIM]
+            dk = jnp.zeros((HEAD_DIM, L), F32)
+            dv = jnp.zeros((HEAD_DIM, L), F32)
+            for k in range(S):
+                rows = slice(k * t, (k + 1) * t)
+                sc = dot(qkv[rows, at:at + HEAD_DIM], keys, 1, 1) * scale
+                sc = jnp.where(col_ref[rows, :1] == row, sc, -1e30)
+                p = jnp.exp(sc - lse[rows, h:h + 1])
+                dp = dot(dattn[rows, at:at + HEAD_DIM], vals, 1, 1)
+                inner = jnp.sum(p * dp, axis=-1, keepdims=True)
+                ds = (p * (dp - inner)).astype(BF)
+                dqkv_s[rows, at:at + HEAD_DIM] = (dot(ds, keys) * scale).astype(BF)
+                dk = dk + dot(q_t[at:at + HEAD_DIM, rows], ds)
+                dv = dv + dot(dattn_t[at:at + HEAD_DIM, rows], p.astype(BF))
+            dqkv_s[:, cs + at:cs + at + HEAD_DIM] = jnp.transpose((dk * scale).astype(BF))
+            dqkv_s[:, 2 * cs + at:2 * cs + at + HEAD_DIM] = jnp.transpose(dv.astype(BF))
+        bsum = jnp.sum(dqkv_s[...].astype(F32), axis=0, keepdims=True)
+        gg = jnp.zeros((1, D), F32)
+        gb = jnp.zeros((1, D), F32)
+        for k in range(S):
+            rows = slice(k * t, (k + 1) * t)
+            unit, _ = norm_parts(xs[k][...].astype(F32))
+            h1_s[rows, :] = (unit * pack[0:1, :] + pack[1:2, :]).astype(BF)
+            dh1 = dot(dqkv_s[rows, :], wq[...], 1, 1)
+            gg = gg + jnp.sum(dh1 * unit, axis=0, keepdims=True)
+            gb = gb + jnp.sum(dh1, axis=0, keepdims=True)
+            if k == 0:
+                own_o[...] = dh1
+            elif k == 1:
+                next_o[...] = dh1
+            else:
+                away_o[k - 2] = dh1.astype(BF)
+        gw = dot(h1_s[...], dqkv_s[...], 0, 0)
+        gw_s[:, :, :3 * cs] = gw.reshape(NB, R, 3 * cs)
+        zero = jnp.zeros((1, cs), F32)
+        wide_q = jnp.concatenate([jnp.where(s == i, bsum[:, :cs], zero) for i in range(S)], 1)
+        wide_v = jnp.concatenate([jnp.where(s == i, bsum[:, 2 * cs:], zero) for i in range(S)], 1)
+        wide = jnp.concatenate([wide_q, wide_v], 1)
+        first = jnp.concatenate([wide[:, 2 * i * R:(2 * i + 1) * R] for i in range(NB)], 1)
+        second = jnp.concatenate([wide[:, (2 * i + 1) * R:(2 * i + 2) * R] for i in range(NB)], 1)
+        gw_s[:, :, 3 * cs:] = columns([gg, gb, first, second], gw_s.shape[2] - 3 * cs)
+        store_blocks(gw_s, keep_o, send_o, b)
+
+    def down_final_kernel(ks, *refs):
+        parts, (wdn_o,) = refs[:-1], refs[-1:]
+        FJ = parts[0].shape[0]
+        s = lax.axis_index("seq")
+        for k, block in order_of(zip(parts, ks)):
+            wdn_o[pl.ds(pl.multiple_of((s ^ k) * FJ, 8), FJ), :] = block.astype(F32)
+
+    def order_of(refs):
+        out = []
+        for ref, ks in refs:
+            out += [(k, ref[...] if len(ks) == 1 else ref[i]) for i, k in enumerate(ks)]
+        return out
+
+    def up_final_kernel(ks, *refs):
+        parts = refs[:len(ks)]
+        win_o, wo_o, bo_o, g2_o, b2_o, bd_o, bin_o, scr = refs[len(ks):]
+        R, FF = win_o.shape
+        D = wo_o.shape[1]
+        cs = D // S
+        FJ = FF // (NB * S)
+        NF = NB * FJ
+        s = lax.axis_index("seq")
+        for k, block in order_of(zip(parts, ks)):
+            scr[s ^ k] = block.astype(F32)
+        for i in range(NB):
+            win_o[:, i * S * FJ:(i + 1) * S * FJ] = jnp.concatenate(
+                [scr[p, :, i * FJ:(i + 1) * FJ] for p in range(S)], 1)
+        wo_o[...] = jnp.concatenate([scr[p, :, NF:NF + cs] for p in range(S)], 1)
+        vecs = [as_rows(scr[p, :, NF + cs:]) for p in range(S)]
+        total = sum(vecs[1:], vecs[0])
+        for i, o in enumerate((bo_o, g2_o, b2_o, bd_o)):
+            o[...] = total[i:i + 1, :].reshape(R)
+        bin_o[...] = jnp.concatenate([v[4:5, :] for v in vecs], 1).reshape(S * FJ)
+
+    def as_rows(cols):
+        R, width = cols.shape
+        cols = jnp.concatenate([cols, jnp.zeros((R, 128 - width), F32)], 1)
+        cols = jnp.concatenate([cols, jnp.zeros((128 - R, 128), F32)], 0)
+        return jnp.transpose(cols)[:8, :R]
+
+    def att_final_kernel(ks, *refs):
+        parts = refs[:len(ks)]
+        wq_o, g1_o, b1_o, bqv_o, scr = refs[len(ks):]
+        R = wq_o.shape[0]
+        D = wq_o.shape[1] // 3
+        cs = D // S
+        s = lax.axis_index("seq")
+        for k, block in order_of(zip(parts, ks)):
+            scr[s ^ k] = block.astype(F32)
+        for c in range(3):
+            wq_o[:, c * D:(c + 1) * D] = jnp.concatenate(
+                [scr[p, :, c * cs:(c + 1) * cs] for p in range(S)], 1)
+        total = as_rows(sum([scr[p, :, 3 * cs:] for p in range(1, S)], scr[0, :, 3 * cs:]))
+        g1_o[...] = total[0:1, :].reshape(R)
+        b1_o[...] = total[1:2, :].reshape(R)
+        bqv_o[...] = jnp.concatenate([total[2:3, :], total[3:4, :]], 1).reshape(2 * R)
+
+    def shards(tokens, segments, ln1_gain, ln1_bias, w_qkv, bias_qv, w_out, bias_out,
+               ln2_gain, ln2_bias, w_in, bias_in, w_down, bias_down, cotangent):
+        _, t, D = tokens.shape
+        FF = w_in.shape[1]
+        L = t * S
+        cs = D // S
+        R = D // NB
+        FJ = FF // (NB * S)
+        NF = NB * FJ
+        x_own = tokens.reshape(t, D)
+        cot_own = cotangent.reshape(t, D)
+
+        xs = gather_seq(x_own, S)
+        at = lax.broadcasted_iota(jnp.int32, (8, D), 0)
+        seg_wide = jnp.pad(segments.astype(F32), ((0, 0), (0, D - L)))
+        pack1 = seg_wide
+        for i, v in enumerate((ln1_gain, ln1_bias, bias_qv[:D], bias_qv[D:])):
+            pack1 = jnp.where(at == i, v[None, :], pack1)
+        wq_s, pack1, seg_row, seg_col = call(
+            prep_qkv_kernel,
+            [sds((D, 3 * cs), BF), sds((8, D), F32), sds((8, L), F32), sds((L, 128), F32)],
+            [w_qkv, pack1], "prep_qkv")
+        cots = gather_seq(cot_own, S)
+        attn, qkv, lse = call(
+            attn_fwd_kernel,
+            [sds((L // 2, 2 * cs), BF), sds((L, 3 * cs), BF), sds((L, 128), F32)],
+            [*xs, seg_row, seg_col, pack1, wq_s], "attn_fwd", flops=2 * L * D * 3 * cs)
+        attn, *cots = lax.optimization_barrier((attn, *cots))
+        ats = gather_seq(attn, S)
+        w_in_late, _ = lax.optimization_barrier((w_in, attn))
+        win_s, wout_s, wdn_s, pack = call(
+            prep_mlp_kernel,
+            [sds((D, NF), BF), sds((D, D), BF), sds((NF, D), BF), sds((16, D), F32)],
+            [w_in_late, w_out, w_down, bias_out, ln2_gain, ln2_bias, bias_in, bias_down], "prep_mlp")
+
+        def halve(keep, send, step, after=()):
+            got = exchange(send, "batch", NB, step)
+            got, keep, after = lax.optimization_barrier((got, keep, after))
+            n = keep.shape[0]
+            total = lambda lo, hi: (keep[lo:hi].astype(F32) + got[lo:hi].astype(F32)).astype(BF)
+            if n == 1:
+                return total(0, 1)
+            return total(0, n // 2), total(n // 2, n)
+
+        out, dx1, vec, *both = pl.pallas_call(
+            local_kernel,
+            out_shape=[sds((t, D), BF), sds((t, D), F32), sds((8, D), F32)] + [sds((t, 2 * cs), BF)] * S,
+            name="local",
+            cost_estimate=pl.CostEstimate(flops=2 * t * D * FF * 4, bytes_accessed=10 * MIB, transcendentals=0),
+            compiler_params=pltpu.CompilerParams(vmem_limit_bytes=40 * MIB),
+        )(x_own, *ats, cot_own, wout_s, pack, w_in, w_down)
+        boths = [both[0]] + [exchange(both[k], "seq", S, k) for k in range(1, S)]
+        ats = lax.optimization_barrier((*ats, dx1))[:S]
+        attn_all, h2, slope, keep_d, send_d = pl.pallas_call(
+            up_kernel,
+            out_shape=[sds((L, D), BF), sds((L, D), BF), sds((L, NF), F32),
+                       sds((NB // 2, FJ, D), BF), sds((NB // 2, FJ, D), BF)],
+            scratch_shapes=[pltpu.VMEM((L, NF), BF), pltpu.VMEM((L, D), BF),
+                            pltpu.VMEM((NB, FJ, D), F32)],
+            name="up",
+            compiler_params=pltpu.CompilerParams(vmem_limit_bytes=32 * MIB),
+        )(*xs, *ats, *cots, wout_s, pack, win_s)
+        send_d, *boths = lax.optimization_barrier((send_d, *boths))
+        wide_u, wide_a = -(-(NF + cs + 8) // 128) * 128, -(-(3 * cs + 8) // 128) * 128
+        keep_u, send_u = pl.pallas_call(
+            down_kernel,
+            out_shape=[sds((NB // 2, R, wide_u), BF), sds((NB // 2, R, wide_u), BF)],
+            scratch_shapes=[pltpu.VMEM((L, NF), BF), pltpu.VMEM((L, cs), BF), pltpu.VMEM((NB, R, wide_u), F32)],
+            name="down",
+            compiler_params=pltpu.CompilerParams(vmem_limit_bytes=32 * MIB),
+        )(*cots, *boths, h2, slope, wdn_s, attn_all, vec)
+        kd, sd = halve(keep_d, send_d, 1)
+        kd, sd, send_u = lax.optimization_barrier((kd, sd, send_u))
+        ku, su = halve(keep_u, send_u, 1, sd)
+        qkv, su = lax.optimization_barrier((qkv, su))
+        own, beside, away, keep_a, send_a = pl.pallas_call(
+            attn_bwd_kernel,
+            out_shape=[sds((t, D), F32), sds((t, D), F32), sds((S - 2, t, D), BF),
+                       sds((NB // 2, R, wide_a), BF), sds((NB // 2, R, wide_a), BF)],
+            scratch_shapes=[pltpu.VMEM((L, D), BF), pltpu.VMEM((L, 3 * cs), BF), pltpu.VMEM((NB, R, wide_a), F32)],
+            name="attn_bwd",
+            cost_estimate=pl.CostEstimate(flops=2 * L * D * D * 4, bytes_accessed=10 * MIB, transcendentals=0),
+            compiler_params=pltpu.CompilerParams(vmem_limit_bytes=40 * MIB),
+        )(*xs, *boths, seg_row, seg_col, pack1, wq_s, qkv, lse)
+        kd, sd = halve(kd, sd, 2, keep_a)
+        ku, su = halve(ku, su, 2, sd)
+        ka, sa = halve(keep_a, send_a, 1, su)
+        away, sa = lax.optimization_barrier((away, sa))
+        got = exchange(away, "seq", S, 2)
+        kd = halve(kd, sd, 4, sa)
+        ka, sa = halve(ka, sa, 2, kd)
+        got, sa = lax.optimization_barrier((got, sa))
+        beside = exchange((beside + got[1].astype(F32)).astype(BF), "seq", S, 1)
+        dh1 = own + got[0].astype(F32) + beside.astype(F32)
+        kd, sa = lax.optimization_barrier((kd, sa))
+        down, ks_d = gather_steps(kd[0], S, (1, 2))
+        ku = halve(ku, su, 4, sa)
+        up, ks_u = gather_steps(ku[0], S, (2, 1))
+        ka = halve(ka, sa, 4, ku)
+        att = gather_seq(ka[0], S)
+        ks_a = [[k] for k in range(S)]
+        unit1, scale1 = norm_parts(x_own.astype(F32))
+        d_tokens = (dx1 + norm_back(dh1, unit1, scale1, ln1_gain)).reshape(tokens.shape)
+
+        o_wdn, = pl.pallas_call(
+            functools.partial(down_final_kernel, ks_d), out_shape=[sds((S * FJ, D), F32)], name="down_final",
+            compiler_params=pltpu.CompilerParams(vmem_limit_bytes=24 * MIB))(*down)
+        vec_out = sds((R,), F32)
+        o_win, o_wout, o_bout, o_ln2g, o_ln2b, o_bdn, o_bin = pl.pallas_call(
+            functools.partial(up_final_kernel, ks_u),
+            out_shape=[sds((R, FF), F32), sds((R, D), F32)] + [vec_out] * 4 + [sds((S * FJ,), F32)],
+            scratch_shapes=[pltpu.VMEM((S, R, wide_u), F32)], name="up_final",
+            compiler_params=pltpu.CompilerParams(vmem_limit_bytes=24 * MIB))(*up)
+        o_wqkv, o_ln1g, o_ln1b, o_bqv = pl.pallas_call(
+            functools.partial(att_final_kernel, ks_a),
+            out_shape=[sds((R, 3 * D), F32), vec_out, vec_out, sds((2 * R,), F32)],
+            scratch_shapes=[pltpu.VMEM((S, R, wide_a), F32)], name="att_final",
+            compiler_params=pltpu.CompilerParams(vmem_limit_bytes=24 * MIB))(*att)
+        return (out.reshape(tokens.shape), d_tokens, o_ln1g, o_ln1b, o_wqkv, o_bqv, o_wout, o_bout,
+                o_ln2g, o_ln2b, o_win, o_bin, o_wdn, o_bdn)
+    return shards
+
+
+def make_plain(S, NB):
     def shards(tokens, segments, ln1_gain, ln1_bias, w_qkv, bias_qv, w_out, bias_out,
                ln2_gain, ln2_bias, w_in, bias_in, w_down, bias_down, cotangent):
         rows, t, D = tokens.shape
@@ -107,10 +588,10 @@
         u_s = dot(h2, win_s) + bin_s
         act_s, slope_s = gelu_both(u_s)
         act_s = act_s.astype(BF)
-        dact_s = dot(cot_all, wdn_s, ((1,), (1,)))
+        dact_s = dot(cot_all, wdn_s, 1, 1)
         du_s = (dact_s * slope_s).astype(BF)
-        g_win = dot(h2, du_s, ((0,), (0,)))
-        g_wdn = dot(act_s, cot_all, ((0,), (0,)))
+        g_win = dot(h2, du_s, 0, 0)
+        g_wdn = dot(act_s, cot_all, 0, 0)
         g_bin = jnp.sum(du_s.astype(F32), 0)
         mlp = jnp.concatenate([g_win.reshape(NB, R, NB * FJ), g_wdn.reshape(NB, FJ, D)], 1).astype(BF)
 
@@ -120,15 +601,15 @@
         act = act.astype(BF)
         activations = (x1[:t] + dot(act, w_down) + bias_down).astype(BF)
         dy = cot_own.astype(F32)
-        du = (dot(cot_own, w_down, ((1,), (1,))) * slope).astype(BF)
-        dh2 = dot(du, w_in, ((1,), (1,)))
+        du = (dot(cot_own, w_down, 1, 1) * slope).astype(BF)
+        dh2 = dot(du, w_in, 1, 1)
         g_ln2g = jnp.sum(dh2 * unit2[:t], 0)
         g_ln2b = jnp.sum(dh2, 0)
         dx1 = dy + norm_back(dh2, unit2[:t], scale2[:t], ln2_gain)
         da = dx1.astype(BF)
         g_bout = jnp.sum(da.astype(F32), 0)
         g_bdn = jnp.sum(dy, 0)
-        dattn = dot(da, wout_rel, ((1,), (1,))).astype(BF)
+        dattn = dot(da, wout_rel, 1, 1).astype(BF)
         da_rel = jnp.take(da.reshape(t, S, cs), rel_s, axis=1)
         both = [jnp.concatenate([dattn[:, kk * cs:(kk + 1) * cs], da_rel[:, kk]], 1) for kk in range(S)]
         both = jnp.concatenate([both[0]] + [exchange(both[kk], "seq", S, kk) for kk in range(1, S)], 0)
@@ -146,7 +627,7 @@
         dv = jnp.einsum("hqk,qhd->khd", p_low, dattn_all, preferred_element_type=F32)
         dqkv = jnp.concatenate([dq.reshape(L, cs), dk.reshape(L, cs), dv.reshape(L, cs)], 1).astype(BF)
 
-        dh1_part = dot(dqkv, wq_s, ((1,), (1,)))
+        dh1_part = dot(dqkv, wq_s, 1, 1)
         g_ln1g = jnp.sum(dh1_part * unit1, 0)
         g_ln1b = jnp.sum(dh1_part, 0)
         dh1_low = dh1_part.astype(BF)
@@ -155,8 +636,8 @@
             dh1 = dh1 + exchange(dh1_low[kk * t:(kk + 1) * t], "seq", S, kk).astype(F32)
         d_tokens = (dx1 + norm_back(dh1, unit1[:t], scale1[:t], ln1_gain)).reshape(tokens.shape)
 
-        g_wqkv = dot(h1, dqkv, ((0,), (0,)))
-        g_wout = dot(attn_all, da_s, ((0,), (0,)))
+        g_wqkv = dot(h1, dqkv, 0, 0)
+        g_wout = dot(attn_all, da_s, 0, 0)
         g_wout = jnp.take(g_wout.reshape(S, cs, cs), rel_s, axis=0).reshape(D, cs)
         bsum = jnp.sum(dqkv.astype(F32), 0)
         g_bqv = jnp.zeros((2, S, cs), F32)
@@ -200,11 +681,13 @@
 
 
 def solution(mesh):
+    S, NB = mesh.shape["seq"], mesh.shape["batch"]
+    shards = (make if BLOCK_ROWS // NB % 32 == 0 else make_plain)(S, NB)
     rowwise = P("batch", "seq", None)
     placed = (rowwise, P("batch", None)) + (P(),) * 12 + (rowwise,)
     b, bn = P("batch"), P("batch", None)
     return jax.shard_map(
-        make(mesh.shape["seq"], mesh.shape["batch"]),
+        shards,
         mesh=mesh,
         in_specs=placed,
         out_specs=(rowwise, rowwise, b, b, bn, b, bn, b, b, b, bn, b, bn, b),

time: 221 us -> 110 us (0.50)
  local copies, waits for them, and re-layouts: 68.9 us -> 6.43 us
  matrix products: 31.9 us -> 0 us
  Pallas kernels: 0 us -> 30.7 us
  other arithmetic: 29.1 us -> 4.05 us
  waiting for transfers between devices: 50.4 us -> 29 us
    dot_general x18 -> x0, matrix products: 31.4 us -> none  [the longest x12 27.7 us: dot(): return lax.dot_general(a, b, (dims, ((), ())), preferred_element_type=F32)]
    pallas_call x0 -> x10, Pallas kernels: none -> 30.7 us  [the longest x1 7.17 us: shards(): pl.pallas_call(attn_bwd_kernel, out_shape=[sds((t, D), F32), sds((t, D),...]
    ppermute x29 -> x30, waiting for transfers between devices: 50.4 us -> 29 us  [exchange(): return lax.ppermute(value, axis, [(j, j ^ step) for j in range(size)])]
    reshape x16 -> x0, local copies, waits for them, and re-layouts: 14.7 us -> none  [the longest x3 7.72 us: shards(): mlp[:, :R].reshape(S, R, NB, FJ).transpose(1, 2, 0, 3).reshape(R, FF)]
    gather x9 -> x0, local copies, waits for them, and re-layouts: 13.6 us -> none  [the longest x2 5.9 us: reduce_batch(): buf = jnp.take(buf, rel_b, axis=0).reshape((NB // 2, 2) + buf.shape[1:])]
    unnamed x180 -> x26, local copies, waits for them, and re-layouts: 18.5 us -> 5.65 us
    convert_element_type x8 -> x10, other arithmetic: 8.78 us -> 1.65 us  [the longest x8 0.92 us: halve(): (keep[lo:hi].astype(F32) + got[lo:hi].astype(F32)).astype(BF)]
    slice x19 -> x1, local copies, waits for them, and re-layouts: 7.63 us -> 0.77 us  [shards(): bias_qv[D:]]
  transfers between devices with their start and end apart: 29 -> 30, of which waited for: 9 -> 12; matrix products, arithmetic and copies ran while one was open for 43% -> 4% of each run, Pallas kernels for 0% -> 21%
where the time goes in v2:
time: 110 us; the launch traced here: 109 us
  starting transfers between devices  38.1 us (35%)
  Pallas kernels  30.7 us (28%)
  waiting for transfers between devices  29 us (26%)
  local copies, waits for them, and re-layouts  6.43 us (6%)
  other arithmetic  4.05 us (4%)
    ppermute x30, starting transfers between devices, exchange(): return lax.ppermute(value, axis, [(j, j ^ step) for j in range(size)])  38.1 us
    ppermute x30, waiting for transfers between devices, exchange(): return lax.ppermute(value, axis, [(j, j ^ step) for j in range(size)])  29 us
    pallas_call x1, Pallas kernels, shards(): pl.pallas_call(attn_bwd_kernel, out_shape=[sds((t, D), F32), sds((t, D),...  7.17 us
    pallas_call x3, Pallas kernels, call(): pl.pallas_call(kernel, out_shape=outs, name=name, cost_estimate=pl.CostEs...  6.83 us
    pallas_call x1, Pallas kernels, shards(): pl.pallas_call(local_kernel, out_shape=[sds((t, D), BF), sds((t, D), F32)...  5.89 us
    unnamed x26, local copies, waits for them, and re-layouts  5.65 us
    pallas_call x1, Pallas kernels, shards(): pl.pallas_call(up_kernel, out_shape=[sds((L, D), BF), sds((L, D), BF), sd...  3.89 us
    pallas_call x1, Pallas kernels, shards(): pl.pallas_call(down_kernel, out_shape=[sds((NB // 2, R, wide_u), BF), sds...  2.79 us
  transfers between devices with their start and end apart: 30, of which 12 were waited for; matrix products, arithmetic and copies ran while one was open for 4% of the time, Pallas kernels for 21%

profile of v2, /device:TPU:0, one launch (start us, length us, event | category | flops | bytes accessed | tf_op | source)
XLA Modules:
  0.0 109.3 jit_solution(2534512266259108683)
XLA Ops:
  0.6 3.0 %collective-permute-start = (bf16[128,768]{1,0:T(8,128)(2,1)}, bf16[128,768]{1,0:T(8,128)(2,1)S(1)}, u32[]{:S(2)}, u32[]{:S(2)}) collective-permute-start(bf16[128,768]{1,0:T(8,128)(2,1)} %bitcast.22), channel_id=1, source_target_pairs={{0,8},{8,0},{16,24},{24,16},{1,9},{9,1},{17,25},{25,17},{2,10},{10... | collective-permute-start | bytes 589832 | tf_op jit(solution)/shard_map/ppermute | solution.py:23
  3.6 1.5 %collective-permute-start.1 = (bf16[128,768]{1,0:T(8,128)(2,1)}, bf16[128,768]{1,0:T(8,128)(2,1)S(1)}, u32[]{:S(2)}, u32[]{:S(2)}) collective-permute-start(bf16[128,768]{1,0:T(8,128)(2,1)} %bitcast.23), channel_id=1, source_target_pairs={{0,16},{8,24},{16,0},{24,8},{1,17},{9,25},{17,1},{25,9},{2,18},{10... | collective-permute-start | bytes 589832 | tf_op jit(solution)/shard_map/ppermute | solution.py:23
  5.2 1.9 %collective-permute-start.3 = (bf16[128,768]{1,0:T(8,128)(2,1)}, bf16[128,768]{1,0:T(8,128)(2,1)S(1)}, u32[]{:S(2)}, u32[]{:S(2)}) collective-permute-start(bf16[128,768]{1,0:T(8,128)(2,1)} %bitcast.29), channel_id=1, source_target_pairs={{0,8},{8,0},{16,24},{24,16},{1,9},{9,1},{17,25},{25,17},{2,10},{10... | collective-permute-start | bytes 589832 | tf_op jit(solution)/shard_map/ppermute | solution.py:23
  10.1 2.5 %collective-permute-start.5 = (bf16[128,768]{1,0:T(8,128)(2,1)}, bf16[128,768]{1,0:T(8,128)(2,1)S(1)}, u32[]{:S(2)}, u32[]{:S(2)}) collective-permute-start(bf16[128,768]{1,0:T(8,128)(2,1)} %bitcast.31), channel_id=1, source_target_pairs={{0,24},{8,16},{16,8},{24,0},{1,25},{9,17},{17,9},{25,1},{2,26},{10... | collective-permute-start | bytes 589832 | tf_op jit(solution)/shard_map/ppermute | solution.py:23
  13.4 2.0 %copy-done.4 = bf16[768,2304]{1,0:T(8,128)(2,1)S(1)} copy-done((bf16[768,2304]{1,0:T(8,128)(2,1)S(1)}, bf16[768,2304]{1,0:T(8,128)(2,1)}, u32[]{:S(2)}) %copy-start.4) | copy-done | bytes 3538968
  15.9 5.5 %attn_fwd.1 = (bf16[256,384]{1,0:T(8,128)(2,1)S(1)}, bf16[512,576]{1,0:T(8,128)(2,1)S(1)}, f32[512,128]{1,0:T(8,128)S(1)}) custom-call(bf16[128,768]{1,0:T(8,128)(2,1)S(1)} %bitcast.25, bf16[128,768]{1,0:T(8,128)(2,1)S(1)} %collective-permute-done.refs_1_, bf16[128,768]{1,0:T(8,128)(2,1)S(1)} %collective-permute-done.1.refs_2_, ...), custom_call_target="tpu_custom_call" | custom-call | flops 452984832 | bytes 3022848 | tf_op jit(solution)/shard_map/attn_fwd/pallas_call | solution.py:69
  26.4 2.3 %copy-done.1 = bf16[3072,768]{1,0:T(8,128)(2,1)S(1)} copy-done((bf16[3072,768]{1,0:T(8,128)(2,1)S(1)}, bf16[3072,768]{1,0:T(8,128)(2,1)}, u32[]{:S(2)}) %copy-start.1) | copy-done | bytes 4718616
  31.1 2.8 %collective-permute-done.7.refs_3_.refs_6_ = bf16[256,384]{1,0:T(8,128)(2,1)S(1)} collective-permute-done((bf16[256,384]{1,0:T(8,128)(2,1)S(1)}, bf16[256,384]{1,0:T(8,128)(2,1)S(1)}, u32[]{:S(2)}, u32[]{:S(2)}) %collective-permute-start.7) | collective-permute-done | bytes 196640 | tf_op jit(solution)/shard_map/ppermute | solution.py:23
  33.9 5.9 %local.1 = (bf16[128,768]{1,0:T(8,128)(2,1)}, f32[128,768]{1,0:T(8,128)S(1)}, f32[8,768]{1,0:T(8,128)S(1)}, bf16[128,384]{1,0:T(8,128)(2,1)S(1)}, bf16[128,384]{...) custom-call(bf16[128,768]{1,0:T(8,128)(2,1)S(1)} %bitcast.26, ...), custom_call_target="tpu_custom_call" | custom-call | flops 2415919104 | bytes 10485760 | tf_op jit(solution)/shard_map/local/pallas_call | solution.py:450
  43.2 3.9 %up.1 = (bf16[512,768]{1,0:T(8,128)(2,1)S(1)}, bf16[512,768]{1,0:T(8,128)(2,1)S(1)}, f32[512,768]{1,0:T(8,128)S(1)}, bf16[4,96,768]{2,1,0:T(8,128)(2,1)S(1)}, bf16[4,96,768]{2,1,0:T(8,128)(2,1)S(1)}) custom-call(bf16[128,768]{1,0:T(8,128)(2,1)S(1)} %bitcast.27, bf16[128,768]{1,0:T(8,128)(2,1)S(1)} %collective-permute-done.refs_1_, ...), custom_call_target="tpu_custom_call" | custom-call | tf_op jit(solution)/shard_map/up/pallas_call | solution.py:459
  47.2 2.8 %down.1 = (bf16[4,96,1024]{2,1,0:T(8,128)(2,1)S(1)}, bf16[4,96,1024]{2,1,0:T(8,128)(2,1)S(1)}) custom-call(bf16[128,768]{1,0:T(8,128)(2,1)S(1)} %bitcast.34, bf16[128,768]{1,0:T(8,128)(2,1)S(1)} %collective-permute-done.3.refs_9_.refs_1_, bf16[128,768]{1,0:T(8,128)(2,1)S(1)} %collective-permute-done.4.refs_10_.refs_2_, ...), custom_call_target="tpu_custom_call" | custom-call | tf_op jit(solution)/shard_map/down/pallas_call | solution.py:470
  50.9 1.6 %collective-permute-start.16 = (bf16[2,96,768]{2,1,0:T(8,128)(2,1)S(1)}, bf16[2,96,768]{2,1,0:T(8,128)(2,1)S(1)}, u32[]{:S(2)}, u32[]{:S(2)}) collective-permute-start(bf16[2,96,768]{2,1,0:T(8,128)(2,1)S(1)} %get-tuple-element.141), channel_id=1, source_target_pairs={{0,2},{1,3},{2,0},{3,1},{4,6},{5,7},{6,4},{7,5},{8,10},{9,11},{10,... | collective-permute-start | bytes 884744 | tf_op jit(solution)/shard_map/ppermute | solution.py:23
  53.0 1.6 %collective-permute-start.15 = (bf16[2,96,1024]{2,1,0:T(8,128)(2,1)S(1)}, bf16[2,96,1024]{2,1,0:T(8,128)(2,1)S(1)}, u32[]{:S(2)}, u32[]{:S(2)}) collective-permute-start(bf16[2,96,1024]{2,1,0:T(8,128)(2,1)S(1)} %get-tuple-element.150), channel_id=1, source_target_pairs={{0,2},{1,3},{2,0},{3,1},{4,6},{5,7},{6,4},{7,5},{8,10},{9,11},{10,... | collective-permute-start | bytes 1179656 | tf_op jit(solution)/shard_map/ppermute | solution.py:23
  54.6 7.2 %attn_bwd.1 = (f32[128,768]{1,0:T(8,128)S(1)}, f32[128,768]{1,0:T(8,128)S(1)}, bf16[2,128,768]{2,1,0:T(8,128)(2,1)S(1)}, bf16[4,96,640]{2,1,0:T(8,128)(2,1)S(1)}, bf16[4,96,640]{2,1,0:T(8,128)(2,1)S(1)}) custom-call(bf16[128,768]{1,0:T(8,128)(2,1)S(1)} %bitcast.28, bf16[128,768]{1,0:T(8,128)(2,1)S(1)} %collective-permute-done.refs_1_, ...), custom_call_target="tpu_custom_call" | custom-call | flops 2415919104 | bytes 10485760 | tf_op jit(solution)/shard_map/attn_bwd/pallas_call | solution.py:481
  62.2 2.7 %collective-permute-start.19 = (bf16[1,96,768]{2,1,0:T(8,128)(2,1)S(1)}, bf16[1,96,768]{2,1,0:T(8,128)(2,1)S(1)}, u32[]{:S(2)}, u32[]{:S(2)}) collective-permute-start(bf16[1,96,768]{2,1,0:T(8,128)(2,1)S(1)} %get-tuple-element.196), channel_id=1, source_target_pairs={{0,4},{1,5},{2,6},{3,7},{4,0},{5,1},{6,2},{7,3},{8,12},{9,13},{10,... | collective-permute-start | bytes 442376 | tf_op jit(solution)/shard_map/ppermute | solution.py:23
  64.9 6.6 %collective-permute-done.15 = bf16[2,96,1024]{2,1,0:T(8,128)(2,1)S(1)} collective-permute-done((bf16[2,96,1024]{2,1,0:T(8,128)(2,1)S(1)}, bf16[2,96,1024]{2,1,0:T(8,128)(2,1)S(1)}, u32[]{:S(2)}, u32[]{:S(2)}) %collective-permute-start.15) | collective-permute-done | bytes 393248 | tf_op jit(solution)/shard_map/ppermute | solution.py:23
  71.8 4.0 %collective-permute-start.22 = (bf16[1,96,1024]{2,1,0:T(8,128)(2,1)S(1)}, bf16[1,96,1024]{2,1,0:T(8,128)(2,1)S(1)}, u32[]{:S(2)}, u32[]{:S(2)}) collective-permute-start(bf16[1,96,1024]{2,1,0:T(8,128)(2,1)S(1)} %get-tuple-element.194), channel_id=1, source_target_pairs={{0,4},{1,5},{2,6},{3,7},{4,0},{5,1},{6,2},{7,3},{8,12},{9,13},{10,... | collective-permute-start | bytes 589832 | tf_op jit(solution)/shard_map/ppermute | solution.py:23
  76.6 6.4 %collective-permute-done.18 = bf16[2,96,640]{2,1,0:T(8,128)(2,1)S(1)} collective-permute-done((bf16[2,96,640]{2,1,0:T(8,128)(2,1)S(1)}, bf16[2,96,640]{2,1,0:T(8,128)(2,1)S(1)}, u32[]{:S(2)}, u32[]{:S(2)}) %collective-permute-start.18) | collective-permute-done | bytes 245792 | tf_op jit(solution)/shard_map/ppermute | solution.py:23
  83.1 2.3 %collective-permute-done.17 = bf16[2,128,768]{2,1,0:T(8,128)(2,1)S(1)} collective-permute-done((bf16[2,128,768]{2,1,0:T(8,128)(2,1)S(1)}, bf16[2,128,768]{2,1,0:T(8,128)(2,1)S(1)}, u32[]{:S(2)}, u32[]{:S(2)}) %collective-permute-start.17) | collective-permute-done | bytes 393248 | tf_op jit(solution)/shard_map/ppermute | solution.py:23
  86.5 1.6 %collective-permute-start.26 = (bf16[1,96,1024]{2,1,0:T(8,128)(2,1)S(1)}, bf16[1,96,1024]{2,1,0:T(8,128)(2,1)S(1)}, u32[]{:S(2)}, u32[]{:S(2)}) collective-permute-start(bf16[1,96,1024]{2,1,0:T(8,128)(2,1)S(1)} %add_convert_fusion.6), channel_id=1, source_target_pairs={{0,16},{8,24},{16,0},{24,8},{1,17},{9,25},{17,1},{25,9},{2,18},{10... | collective-permute-start | bytes 589832 | tf_op jit(solution)/shard_map/ppermute | solution.py:23
  88.8 4.2 %collective-permute-done.21 = bf16[1,96,640]{2,1,0:T(8,128)(2,1)S(1)} collective-permute-done((bf16[1,96,640]{2,1,0:T(8,128)(2,1)S(1)}, bf16[1,96,640]{2,1,0:T(8,128)(2,1)S(1)}, u32[]{:S(2)}, u32[]{:S(2)}) %collective-permute-start.21) | collective-permute-done | bytes 122912 | tf_op jit(solution)/shard_map/ppermute | solution.py:23
  96.6 1.6 %collective-permute-start.29 = (bf16[2,96,768]{2,1,0:T(8,128)(2,1)S(1)}, bf16[2,96,768]{2,1,0:T(8,128)(2,1)S(1)}, u32[]{:S(2)}, u32[]{:S(2)}) collective-permute-start(bf16[2,96,768]{2,1,0:T(8,128)(2,1)S(1)} %pad_maximum_fusion.1), channel_id=1, source_target_pairs={{0,16},{8,24},{16,0},{24,8},{1,17},{9,25},{17,1},{25,9},{2,18},{10... | collective-permute-start | bytes 884744 | tf_op jit(solution)/shard_map/ppermute | solution.py:23
  101.0 1.9 %collective-permute-done.25.refs_3_ = bf16[96,640]{1,0:T(8,128)(2,1)S(1)} collective-permute-done((bf16[96,640]{1,0:T(8,128)(2,1)S(1)}, bf16[96,640]{1,0:T(8,128)(2,1)S(1)}, u32[]{:S(2)}, u32[]{:S(2)}) %collective-permute-start.25) | collective-permute-done | bytes 122912 | tf_op jit(solution)/shard_map/ppermute | solution.py:23
  107.5 1.7 %up_final.1 = (f32[96,3072]{1,0:T(8,128)}, f32[96,768]{1,0:T(8,128)}, f32[96]{0:T(128)}, f32[96]{0:T(128)}, f32[96]{0:T(128)}, /*index=5*/f32[96]{0:T(128)}, f32[384]{0:T(512)}) custom-call(bf16[96,1024]{1,0:T(8,128)(2,1)S(1)} %bitcast.35, bf16[96,1024]{1,0:T(8,128)(2,1)S(1)} %bitcast.37, bf16[2,96,1024]{2,1,0:T(8,128)(2,1)S(1)} %collective-permute-done.27.refs_2_), custom_call_target="tpu_custom_call" | custom-call | tf_op jit(solution)/shard_map/up_final/pallas_call | solution.py:514
  (98 shorter events, 30.8 us)
Async XLA Ops:
  0.6 9.5 %collective-permute-start = (bf16[128,768]{1,0:T(8,128)(2,1)}, bf16[128,768]{1,0:T(8,128)(2,1)S(1)}, u32[]{:S(2)}, u32[]{:S(2)}) collective-permute-start(bf16[128,768]{1,0:T(8,128)(2,1)} %bitcast.22), channel_id=1, source_target_pairs={{0,8},{8,0},{16,24},{24,16},{1,9},{9,1},{17,25},{25,17},{2,10},{10... | collective-permute-start | bytes 589832 | tf_op jit(solution)/shard_map/ppermute | solution.py:23
  3.6 12.2 %collective-permute-start.1 = (bf16[128,768]{1,0:T(8,128)(2,1)}, bf16[128,768]{1,0:T(8,128)(2,1)S(1)}, u32[]{:S(2)}, u32[]{:S(2)}) collective-permute-start(bf16[128,768]{1,0:T(8,128)(2,1)} %bitcast.23), channel_id=1, source_target_pairs={{0,16},{8,24},{16,0},{24,8},{1,17},{9,25},{17,1},{25,9},{2,18},{10... | collective-permute-start | bytes 589832 | tf_op jit(solution)/shard_map/ppermute | solution.py:23
  5.2 10.7 %collective-permute-start.2 = (bf16[128,768]{1,0:T(8,128)(2,1)}, bf16[128,768]{1,0:T(8,128)(2,1)S(1)}, u32[]{:S(2)}, u32[]{:S(2)}) collective-permute-start(bf16[128,768]{1,0:T(8,128)(2,1)} %bitcast.24), channel_id=1, source_target_pairs={{0,24},{8,16},{16,8},{24,0},{1,25},{9,17},{17,9},{25,1},{2,26},{10... | collective-permute-start | bytes 589832 | tf_op jit(solution)/shard_map/ppermute | solution.py:23
  5.2 16.2 %collective-permute-start.3 = (bf16[128,768]{1,0:T(8,128)(2,1)}, bf16[128,768]{1,0:T(8,128)(2,1)S(1)}, u32[]{:S(2)}, u32[]{:S(2)}) collective-permute-start(bf16[128,768]{1,0:T(8,128)(2,1)} %bitcast.29), channel_id=1, source_target_pairs={{0,8},{8,0},{16,24},{24,16},{1,9},{9,1},{17,25},{25,17},{2,10},{10... | collective-permute-start | bytes 589832 | tf_op jit(solution)/shard_map/ppermute | solution.py:23
  7.1 15.7 %collective-permute-start.4 = (bf16[128,768]{1,0:T(8,128)(2,1)}, bf16[128,768]{1,0:T(8,128)(2,1)S(1)}, u32[]{:S(2)}, u32[]{:S(2)}) collective-permute-start(bf16[128,768]{1,0:T(8,128)(2,1)} %bitcast.30), channel_id=1, source_target_pairs={{0,16},{8,24},{16,0},{24,8},{1,17},{9,25},{17,1},{25,9},{2,18},{10... | collective-permute-start | bytes 589832 | tf_op jit(solution)/shard_map/ppermute | solution.py:23
  10.1 12.7 %collective-permute-start.5 = (bf16[128,768]{1,0:T(8,128)(2,1)}, bf16[128,768]{1,0:T(8,128)(2,1)S(1)}, u32[]{:S(2)}, u32[]{:S(2)}) collective-permute-start(bf16[128,768]{1,0:T(8,128)(2,1)} %bitcast.31), channel_id=1, source_target_pairs={{0,24},{8,16},{16,8},{24,0},{1,25},{9,17},{17,9},{25,1},{2,26},{10... | collective-permute-start | bytes 589832 | tf_op jit(solution)/shard_map/ppermute | solution.py:23
  22.9 8.2 %collective-permute-start.6 = (bf16[256,384]{1,0:T(8,128)(2,1)S(1)}, bf16[256,384]{1,0:T(8,128)(2,1)S(1)}, u32[]{:S(2)}, u32[]{:S(2)}) collective-permute-start(bf16[256,384]{1,0:T(8,128)(2,1)S(1)} %get-tuple-element.110.refs_1_.refs_4_), channel_id=1, source_target_pairs={{0,8},{8,0},{16,24},{24,16},{1,9},{9,1},{17,25},{25,17},{2,10},{10... | collective-permute-start | bytes 589832 | tf_op jit(solution)/shard_map/ppermute | solution.py:23
  24.1 9.7 %collective-permute-start.7 = (bf16[256,384]{1,0:T(8,128)(2,1)S(1)}, bf16[256,384]{1,0:T(8,128)(2,1)S(1)}, u32[]{:S(2)}, u32[]{:S(2)}) collective-permute-start(bf16[256,384]{1,0:T(8,128)(2,1)S(1)} %get-tuple-element.110.refs_1_.refs_4_), channel_id=1, source_target_pairs={{0,16},{8,24},{16,0},{24,8},{1,17},{9,25},{17,1},{25,9},{2,18},{10... | collective-permute-start | bytes 589832 | tf_op jit(solution)/shard_map/ppermute | solution.py:23
  24.9 8.9 %collective-permute-start.8 = (bf16[256,384]{1,0:T(8,128)(2,1)S(1)}, bf16[256,384]{1,0:T(8,128)(2,1)S(1)}, u32[]{:S(2)}, u32[]{:S(2)}) collective-permute-start(bf16[256,384]{1,0:T(8,128)(2,1)S(1)} %get-tuple-element.110.refs_1_.refs_4_), channel_id=1, source_target_pairs={{0,24},{8,16},{16,8},{24,0},{1,25},{9,17},{17,9},{25,1},{2,26},{10... | collective-permute-start | bytes 589832 | tf_op jit(solution)/shard_map/ppermute | solution.py:23
  39.7 7.4 %collective-permute-start.10 = (bf16[128,384]{1,0:T(8,128)(2,1)S(1)}, bf16[128,384]{1,0:T(8,128)(2,1)S(1)}, u32[]{:S(2)}, u32[]{:S(2)}) collective-permute-start(bf16[128,384]{1,0:T(8,128)(2,1)S(1)} %get-tuple-element.122), channel_id=1, source_target_pairs={{0,16},{8,24},{16,0},{24,8},{1,17},{9,25},{17,1},{25,9},{2,18},{10... | collective-permute-start | bytes 294920 | tf_op jit(solution)/shard_map/ppermute | solution.py:23
  50.9 11.3 %collective-permute-start.16 = (bf16[2,96,768]{2,1,0:T(8,128)(2,1)S(1)}, bf16[2,96,768]{2,1,0:T(8,128)(2,1)S(1)}, u32[]{:S(2)}, u32[]{:S(2)}) collective-permute-start(bf16[2,96,768]{2,1,0:T(8,128)(2,1)S(1)} %get-tuple-element.141), channel_id=1, source_target_pairs={{0,2},{1,3},{2,0},{3,1},{4,6},{5,7},{6,4},{7,5},{8,10},{9,11},{10,... | collective-permute-start | bytes 884744 | tf_op jit(solution)/shard_map/ppermute | solution.py:23
  53.0 18.5 %collective-permute-start.15 = (bf16[2,96,1024]{2,1,0:T(8,128)(2,1)S(1)}, bf16[2,96,1024]{2,1,0:T(8,128)(2,1)S(1)}, u32[]{:S(2)}, u32[]{:S(2)}) collective-permute-start(bf16[2,96,1024]{2,1,0:T(8,128)(2,1)S(1)} %get-tuple-element.150), channel_id=1, source_target_pairs={{0,2},{1,3},{2,0},{3,1},{4,6},{5,7},{6,4},{7,5},{8,10},{9,11},{10,... | collective-permute-start | bytes 1179656 | tf_op jit(solution)/shard_map/ppermute | solution.py:23
  61.8 9.8 %collective-permute-start.14 = (bf16[4,96,640]{2,1,0:T(8,128)(2,1)S(1)}, bf16[4,96,640]{2,1,0:T(8,128)(2,1)S(1)}, u32[]{:S(2)}, u32[]{:S(2)}) collective-permute-start(bf16[4,96,640]{2,1,0:T(8,128)(2,1)S(1)} %get-tuple-element.148), channel_id=1, source_target_pairs={{0,1},{1,0},{2,3},{3,2},{4,5},{5,4},{6,7},{7,6},{8,9},{9,8},{10,11... | collective-permute-start | bytes 1474568 | tf_op jit(solution)/shard_map/ppermute | solution.py:23
  62.2 13.6 %collective-permute-start.19 = (bf16[1,96,768]{2,1,0:T(8,128)(2,1)S(1)}, bf16[1,96,768]{2,1,0:T(8,128)(2,1)S(1)}, u32[]{:S(2)}, u32[]{:S(2)}) collective-permute-start(bf16[1,96,768]{2,1,0:T(8,128)(2,1)S(1)} %get-tuple-element.196), channel_id=1, source_target_pairs={{0,4},{1,5},{2,6},{3,7},{4,0},{5,1},{6,2},{7,3},{8,12},{9,13},{10,... | collective-permute-start | bytes 442376 | tf_op jit(solution)/shard_map/ppermute | solution.py:23
  71.7 11.3 %collective-permute-start.18 = (bf16[2,96,640]{2,1,0:T(8,128)(2,1)S(1)}, bf16[2,96,640]{2,1,0:T(8,128)(2,1)S(1)}, u32[]{:S(2)}, u32[]{:S(2)}) collective-permute-start(bf16[2,96,640]{2,1,0:T(8,128)(2,1)S(1)} %get-tuple-element.159), channel_id=1, source_target_pairs={{0,2},{1,3},{2,0},{3,1},{4,6},{5,7},{6,4},{7,5},{8,10},{9,11},{10,... | collective-permute-start | bytes 737288 | tf_op jit(solution)/shard_map/ppermute | solution.py:23
  71.8 14.6 %collective-permute-start.22 = (bf16[1,96,1024]{2,1,0:T(8,128)(2,1)S(1)}, bf16[1,96,1024]{2,1,0:T(8,128)(2,1)S(1)}, u32[]{:S(2)}, u32[]{:S(2)}) collective-permute-start(bf16[1,96,1024]{2,1,0:T(8,128)(2,1)S(1)} %get-tuple-element.194), channel_id=1, source_target_pairs={{0,4},{1,5},{2,6},{3,7},{4,0},{5,1},{6,2},{7,3},{8,12},{9,13},{10,... | collective-permute-start | bytes 589832 | tf_op jit(solution)/shard_map/ppermute | solution.py:23
  75.8 9.6 %collective-permute-start.17 = (bf16[2,128,768]{2,1,0:T(8,128)(2,1)S(1)}, bf16[2,128,768]{2,1,0:T(8,128)(2,1)S(1)}, u32[]{:S(2)}, u32[]{:S(2)}) collective-permute-start(bf16[2,128,768]{2,1,0:T(8,128)(2,1)S(1)} %get-tuple-element.158), channel_id=1, source_target_pairs={{0,16},{8,24},{16,0},{24,8},{1,17},{9,25},{17,1},{25,9},{2,18},{10... | collective-permute-start | bytes 1179656 | tf_op jit(solution)/shard_map/ppermute | solution.py:23
  85.5 9.8 %collective-permute-start.28 = (bf16[1,96,768]{2,1,0:T(8,128)(2,1)S(1)}, bf16[1,96,768]{2,1,0:T(8,128)(2,1)S(1)}, u32[]{:S(2)}, u32[]{:S(2)}) collective-permute-start(bf16[1,96,768]{2,1,0:T(8,128)(2,1)S(1)} %add_convert_fusion.9), channel_id=1, source_target_pairs={{0,8},{8,0},{16,24},{24,16},{1,9},{9,1},{17,25},{25,17},{2,10},{10... | collective-permute-start | bytes 442376 | tf_op jit(solution)/shard_map/ppermute | solution.py:23
  86.5 10.1 %collective-permute-start.26 = (bf16[1,96,1024]{2,1,0:T(8,128)(2,1)S(1)}, bf16[1,96,1024]{2,1,0:T(8,128)(2,1)S(1)}, u32[]{:S(2)}, u32[]{:S(2)}) collective-permute-start(bf16[1,96,1024]{2,1,0:T(8,128)(2,1)S(1)} %add_convert_fusion.6), channel_id=1, source_target_pairs={{0,16},{8,24},{16,0},{24,8},{1,17},{9,25},{17,1},{25,9},{2,18},{10... | collective-permute-start | bytes 589832 | tf_op jit(solution)/shard_map/ppermute | solution.py:23
  88.1 10.1 %collective-permute-start.20 = (bf16[128,768]{1,0:T(8,128)(2,1)S(1)}, bf16[128,768]{1,0:T(8,128)(2,1)S(1)}, u32[]{:S(2)}, u32[]{:S(2)}) collective-permute-start(bf16[128,768]{1,0:T(8,128)(2,1)S(1)} %fusion.10), channel_id=1, source_target_pairs={{0,8},{8,0},{16,24},{24,16},{1,9},{9,1},{17,25},{25,17},{2,10},{10... | collective-permute-start | bytes 589832 | tf_op jit(solution)/shard_map/ppermute | solution.py:23
  93.0 7.1 %collective-permute-start.23 = (bf16[96,640]{1,0:T(8,128)(2,1)S(1)}, bf16[96,640]{1,0:T(8,128)(2,1)S(1)}, u32[]{:S(2)}, u32[]{:S(2)}) collective-permute-start(bf16[96,640]{1,0:T(8,128)(2,1)S(1)} %fusion.13.refs_0_), channel_id=1, source_target_pairs={{0,8},{8,0},{16,24},{24,16},{1,9},{9,1},{17,25},{25,17},{2,10},{10... | collective-permute-start | bytes 368648 | tf_op jit(solution)/shard_map/ppermute | solution.py:23
  95.2 7.7 %collective-permute-start.25 = (bf16[96,640]{1,0:T(8,128)(2,1)S(1)}, bf16[96,640]{1,0:T(8,128)(2,1)S(1)}, u32[]{:S(2)}, u32[]{:S(2)}) collective-permute-start(bf16[96,640]{1,0:T(8,128)(2,1)S(1)} %fusion.13.refs_0_), channel_id=1, source_target_pairs={{0,24},{8,16},{16,8},{24,0},{1,25},{9,17},{17,9},{25,1},{2,26},{10... | collective-permute-start | bytes 368648 | tf_op jit(solution)/shard_map/ppermute | solution.py:23
  96.6 8.5 %collective-permute-start.29 = (bf16[2,96,768]{2,1,0:T(8,128)(2,1)S(1)}, bf16[2,96,768]{2,1,0:T(8,128)(2,1)S(1)}, u32[]{:S(2)}, u32[]{:S(2)}) collective-permute-start(bf16[2,96,768]{2,1,0:T(8,128)(2,1)S(1)} %pad_maximum_fusion.1), channel_id=1, source_target_pairs={{0,16},{8,24},{16,0},{24,8},{1,17},{9,25},{17,1},{25,9},{2,18},{10... | collective-permute-start | bytes 884744 | tf_op jit(solution)/shard_map/ppermute | solution.py:23
  98.2 9.3 %collective-permute-start.27 = (bf16[2,96,1024]{2,1,0:T(8,128)(2,1)S(1)}, bf16[2,96,1024]{2,1,0:T(8,128)(2,1)S(1)}, u32[]{:S(2)}, u32[]{:S(2)}) collective-permute-start(bf16[2,96,1024]{2,1,0:T(8,128)(2,1)S(1)} %pad_maximum_fusion), channel_id=1, source_target_pairs={{0,8},{8,0},{16,24},{24,16},{1,9},{9,1},{17,25},{25,17},{2,10},{10... | collective-permute-start | bytes 1179656 | tf_op jit(solution)/shard_map/ppermute | solution.py:23
  (19 other events, 122.4 us)

commit v3 on v2

--- a/solution.py
+++ b/solution.py
@@ -25,19 +25,6 @@
 
 def gather_seq(value, size):
     return [value] + [exchange(value, "seq", size, k) for k in range(1, size)]
-
-
-def gather_steps(value, size, steps):
-    arrays, ks = [value], [[0]]
-    held = value[None]
-    for step in steps:
-        got = exchange(held, "seq", size, step)
-        ks.append([k ^ step for part in ks for k in part])
-        arrays.append(got)
-        if step != steps[-1]:
-            held = jnp.concatenate([held, got], 0)
-    arrays = [a if len(k) > 1 else a.reshape(value.shape) for a, k in zip(arrays, ks)]
-    return arrays, ks
 
 
 def norm_parts(values):
@@ -79,11 +66,21 @@
     return jax.ShapeDtypeStruct(shape, dtype)
 
 
+HOPS = {"d": "far", "u": "near", "a": "near"}
+GATHER = {"d": None, "u": None, "a": None}
+DH = (1, 2)
+ORDER = "pq af c1 c2 c3 lo pm fa up dn d0 u0 bw d1 u1 bo a0 h1 d2 a1 u2 d3 d4 ou a2 h2 u3 u4 a3 a4".split()
+
+
 def flat(ref):
     return ref[...].reshape(1, -1)
 
 
 def make(S, NB):
+    near_first = [2 ** i for i in range(NB.bit_length() - 1)]
+    far_first = near_first[:1] + near_first[:0:-1]
+    hops = {k: near_first if v == "near" else far_first for k, v in HOPS.items()}
+
     def rel_row(row, t):
         s = lax.axis_index("seq")
         parts = [row[:, i * t:(i + 1) * t] for i in range(S)]
@@ -112,19 +109,13 @@
                 bq_o[2:3, :] = jnp.concatenate(
                     [pack[2:3, p * cs:(p + 1) * cs], zero, pack[3:4, p * cs:(p + 1) * cs], zero], 1)
 
-    def prep_mlp_kernel(win, wout, wdown, bout, ln2g, ln2b, bin_, bdown, win_o, wout_o, wdn_o, pack_o):
+    def prep_mlp_kernel(win, wout, wdown, bin_, win_o, wout_o, wdn_o, bin_o):
         D = wout.shape[0]
         FF = win.shape[1]
         cs = D // S
         FJ = FF // (NB * S)
         s = lax.axis_index("seq")
         vin = flat(bin_)
-        pack_o[3:4, :] = flat(bout)
-        pack_o[4:5, :] = flat(ln2g)
-        pack_o[5:6, :] = flat(ln2b)
-        pack_o[7:8, :] = flat(bdown)
-        for c in range(FF // D):
-            pack_o[8 + c:9 + c, :] = vin[:, c * D:(c + 1) * D]
         for m in range(S):
             wout_o[m * cs:(m + 1) * cs, :] = wout[pl.ds(pl.multiple_of((s ^ m) * cs, 16), cs), :]
         for i in range(NB):
@@ -135,11 +126,11 @@
                 for i in range(NB):
                     at = (i * S + p) * FJ
                     win_o[:, i * FJ:(i + 1) * FJ] = win[:, at:at + FJ]
-                pack_o[6:7, :] = jnp.concatenate(
-                    [vin[:, (i * S + p) * FJ:(i * S + p + 1) * FJ] for i in range(NB)], 1)
+                    bin_o[:, i * FJ:(i + 1) * FJ] = vin[:, at:at + FJ]
 
     def attn_fwd_kernel(*refs):
-        xs, (row_ref, col_ref, pack, wq_ref, attn_o, qkv_o, lse_o) = refs[:S], refs[S:]
+        xs, (row_ref, col_ref, pack, wq_ref, qkv_o, lse_o, attn_o) = refs[:S], refs[S:S + 7]
+        near_o, far_o = refs[S + 7:2 * S + 6], refs[2 * S + 6:]
         t, D = xs[0].shape
         L = S * t
         cs = D // S
@@ -148,63 +139,84 @@
             h1 = (unit * pack[0:1, :] + pack[1:2, :]).astype(BF)
             qkv_o[k * t:(k + 1) * t, :] = (dot(h1, wq_ref[...]) + pack[2:3, :3 * cs]).astype(BF)
         row = row_ref[0:1, :]
-        outs = [[] for _ in range(S)]
-        for h in range(cs // HEAD_DIM):
-            at = h * HEAD_DIM
-            keys = qkv_o[:, cs + at:cs + at + HEAD_DIM]
-            vals = qkv_o[:, 2 * cs + at:2 * cs + at + HEAD_DIM]
-            for k in range(S):
-                q = qkv_o[k * t:(k + 1) * t, at:at + HEAD_DIM]
-                sc = dot(q, keys, 1, 1) * (HEAD_DIM ** -0.5)
-                sc = jnp.where(col_ref[k * t:(k + 1) * t, :1] == row, sc, -1e30)
-                top = jnp.max(sc, axis=-1, keepdims=True)
-                ex = jnp.exp(sc - top)
-                total = jnp.sum(ex, axis=-1, keepdims=True)
-                pr = (ex * (1.0 / total)).astype(BF)
-                outs[k].append(dot(pr, vals).astype(BF))
-                lse_o[k * t:(k + 1) * t, h:h + 1] = top + jnp.log(total)
+        heads = cs // HEAD_DIM
+        outs = [[None] * heads for _ in range(S)]
+        def part(c, h, rows=slice(None)):
+            return qkv_o[rows, c * cs + h * HEAD_DIM:c * cs + (h + 1) * HEAD_DIM]
+        def soft(sc, rows, h):
+            sc = jnp.where(col_ref[rows, :1] == row, sc, -1e30)
+            top = jnp.max(sc, axis=-1, keepdims=True)
+            ex = jnp.exp(sc - top)
+            total = jnp.sum(ex, axis=-1, keepdims=True)
+            lse_o[rows, h:h + 1] = top + jnp.log(total)
+            return (ex * (1.0 / total)).astype(BF)
+        def put(o, h, n):
+            o = o.astype(BF)
+            for r in range(o.shape[0] // t):
+                outs[n + r][h] = o[r * t:(r + 1) * t]
+        Q = 256
+        todo = [(h, n) for h in range(heads) for n in range(L // Q)]
+        def score(h, n):
+            return dot(part(0, h, slice(n * Q, (n + 1) * Q)) * BF(HEAD_DIM ** -0.5), part(1, h), 1, 1)
+        nxt = score(*todo[0])
+        prev = None
+        for i, (h, n) in enumerate(todo):
+            cur = nxt
+            if i + 1 < len(todo):
+                nxt = score(*todo[i + 1])
+            pr = soft(cur, slice(n * Q, (n + 1) * Q), h)
+            if prev is not None:
+                put(dot(prev[0], part(2, prev[1])), prev[1], prev[2])
+            prev = (pr, h, n * Q // t)
+        put(dot(prev[0], part(2, prev[1])), prev[1], prev[2])
         blocks = [jnp.concatenate(o, 1) for o in outs]
-        half = S // 2
-        for k in range(half):
-            attn_o[k * t:(k + 1) * t, :] = jnp.concatenate([blocks[k], blocks[k + half]], 1)
-
-    def order():
-        bits = NB.bit_length() - 1
-        return [int(format(p, "b").zfill(bits)[::-1], 2) for p in range(NB)]
-
-    def store_blocks(scr, keep_o, send_o, b):
-        for p, m in enumerate(order()):
+        for k in range(S):
+            attn_o[k * t:(k + 1) * t, :] = blocks[k]
+        for m in range(1, S):
+            near_o[m - 1][...] = fold(blocks[m])
+            far_o[m - 1][...] = fold(jnp.concatenate([blocks[k ^ m] for k in range(1, S)], 0))
+
+    def fold(block):
+        half = block.shape[0] // 2
+        return jnp.concatenate([block[:half], block[half:]], 1)
+
+    def unfold(block):
+        half = block.shape[1] // 2
+        return jnp.concatenate([block[:, :half], block[:, half:]], 0)
+
+    def order(steps):
+        ms = [0]
+        for step in reversed(steps):
+            ms = ms + [m ^ step for m in ms]
+        return ms
+
+    def store_blocks(scr, keep_o, send_o, b, steps):
+        for p, m in enumerate(order(steps)):
             o, at = (keep_o, p) if p < NB // 2 else (send_o, p - NB // 2)
             o[at] = scr[b ^ m].astype(BF)
 
     def up_kernel(*refs):
-        xs, ats, cots = refs[:S], refs[S:2 * S], refs[2 * S:3 * S]
-        (wout, pack, win, attn_all, h2_o, slope_o, keep_o, send_o, act_s, cot_s, gw_s) = refs[3 * S:]
+        xs, (own,), nears, fars, cots = refs[:S], refs[S:S + 1], refs[S + 1:2 * S], refs[2 * S:3 * S - 1], refs[3 * S - 1:4 * S - 1]
+        (wout, bout, g_ref, b_ref, win, bin_ref, attn_all, h2_o, slope_o, keep_o, send_o,
+         act_s, cot_s, gw_s) = refs[4 * S - 1:]
         t, D = xs[0].shape
         cs = D // S
         FJ = win.shape[1] // NB
-        half = S // 2
         b = lax.axis_index("batch")
+        attn_all[:t, :] = jnp.concatenate([own[:t, :]] + [unfold(r[...]) for r in nears], 1)
+        attn_all[t:, :] = jnp.concatenate([own[t:, :]] + [unfold(r[...]) for r in fars], 1)
         for k in range(S):
-            pieces = []
-            for m in range(S):
-                j = k ^ m
-                lo, hi = (j % half) * t, (j // half) * cs
-                pieces.append(ats[m][lo:lo + t, hi:hi + cs])
-            attn_all[k * t:(k + 1) * t, :] = jnp.concatenate(pieces, 1)
-        for k in range(S):
-            rows = slice(k * t, (k + 1) * t)
-            x1 = xs[k][...].astype(F32) + dot(attn_all[rows, :], wout[...]) + pack[3:4, :]
-            unit, _ = norm_parts(x1)
-            h2 = (unit * pack[4:5, :] + pack[5:6, :]).astype(BF)
-            h2_o[rows, :] = h2
-            u = dot(h2, win[...]) + pack[6:7, :]
-            act, slope = gelu_both(u)
-            act_s[rows, :] = act.astype(BF)
-            slope_o[rows, :] = slope
-            cot_s[rows, :] = cots[k][...]
+            cot_s[k * t:(k + 1) * t, :] = cots[k][...]
+        x = jnp.concatenate([x[...].astype(F32) for x in xs], 0)
+        x1 = x + dot(attn_all[...], wout[...]) + flat(bout)
+        unit, _ = norm_parts(x1)
+        h2 = (unit * flat(g_ref) + flat(b_ref)).astype(BF)
+        h2_o[...] = h2
+        act, slope = gelu_both(dot(h2, win[...]) + bin_ref[...])
+        act_s[...] = act.astype(BF)
+        slope_o[...] = slope
         gw_s[...] = dot(act_s[...], cot_s[...], 0, 0).reshape(NB, FJ, D)
-        store_blocks(gw_s, keep_o, send_o, b)
+        store_blocks(gw_s, keep_o, send_o, b, hops["d"])
 
     def down_kernel(*refs):
         cots, boths = refs[:S], refs[S:2 * S]
@@ -215,13 +227,12 @@
         NF = slope.shape[1]
         s = lax.axis_index("seq")
         b = lax.axis_index("batch")
-        gbin = jnp.zeros((1, NF), F32)
         for k in range(S):
-            rows = slice(k * t, (k + 1) * t)
-            du = (dot(cots[k][...], wdn[...], 1, 1) * slope[rows, :]).astype(BF)
-            du_s[rows, :] = du
-            da_s[rows, :] = boths[k][:, cs:]
-            gbin = gbin + jnp.sum(du.astype(F32), axis=0, keepdims=True)
+            da_s[k * t:(k + 1) * t, :] = boths[k][:, cs:]
+        cot = jnp.concatenate([c[...] for c in cots], 0)
+        du = (dot(cot, wdn[...], 1, 1) * slope[...]).astype(BF)
+        du_s[...] = du
+        gbin = jnp.sum(du.astype(F32), axis=0, keepdims=True)
         gw_s[:, :, :NF] = dot(h2[...], du_s[...], 0, 0).reshape(NB, R, NF)
         go = dot(attn_all[...], da_s[...], 0, 0)
         per = NB // S
@@ -229,7 +240,7 @@
             for j in range(per):
                 gw_s[(s ^ m) * per + j, :, NF:NF + cs] = go[m * cs + j * R:m * cs + (j + 1) * R, :]
         gw_s[:, :, NF + cs:] = columns([vec[:4, :], gbin], gw_s.shape[2] - NF - cs)
-        store_blocks(gw_s, keep_o, send_o, b)
+        store_blocks(gw_s, keep_o, send_o, b, hops["u"])
 
     def columns(rows, width):
         rows = jnp.concatenate(rows, 0)
@@ -238,35 +249,33 @@
         return jnp.transpose(rows)[:, :width].reshape(NB, D // NB, width)
 
     def local_kernel(*refs):
-        x_ref, ats, refs = refs[0], refs[1:1 + S], refs[1 + S:]
-        cot_ref, wout, pack, win, wdown = refs[:5]
-        refs = refs[5:]
-        out_o, dx1_o, vec_o = refs[0], refs[1], refs[2]
-        both = refs[3:3 + S]
+        x_ref, own, nears, refs = refs[0], refs[1], refs[2:1 + S], refs[1 + S:]
+        cot_ref, wout, bout, g_ref, b_ref, win, bin_ref, wdown = refs[:8]
+        act_o, x1_o, dx1_o, vec_o = refs[8:12]
+        both = refs[12:]
         t, D = x_ref.shape
         FF = win.shape[1]
         cs = D // S
         s = lax.axis_index("seq")
-        half = S // 2
-        attn = jnp.concatenate(
-            [ats[m][(m % half) * t:(m % half + 1) * t, (m // half) * cs:(m // half + 1) * cs] for m in range(S)], 1)
-        x1 = x_ref[...].astype(F32) + dot(attn, wout[...]) + pack[3:4, :]
+        heads = [wout[pl.ds(pl.multiple_of((s ^ m) * cs, 16), cs), :] for m in range(S)]
+        attn = [own[:t, :]] + [unfold(r[...]) for r in nears]
+        x1 = x_ref[...].astype(F32) + flat(bout)
+        for m in range(S):
+            x1 = x1 + dot(attn[m], heads[m])
         unit, scale = norm_parts(x1)
-        h2 = (unit * pack[4:5, :] + pack[5:6, :]).astype(BF)
+        h2 = (unit * flat(g_ref) + flat(b_ref)).astype(BF)
         cot = cot_ref[...]
-        C = D
-        mixed = jnp.zeros((t, D), F32)
+        bias_in = flat(bin_ref)
+        x1_o[...] = x1
         dh2 = jnp.zeros((t, D), F32)
-        for c in range(FF // C):
-            cols = slice(c * C, (c + 1) * C)
-            u = dot(h2, win[:, cols]) + pack[8 + c:9 + c, :]
-            act, slope = gelu_both(u)
-            mixed = mixed + dot(act.astype(BF), wdown[cols, :])
+        for c in range(FF // D):
+            cols = slice(c * D, (c + 1) * D)
+            act, slope = gelu_both(dot(h2, win[:, cols]) + bias_in[:, cols])
+            act_o[:, cols] = act.astype(BF)
             du = (dot(cot, wdown[cols, :], 1, 1) * slope).astype(BF)
             dh2 = dh2 + dot(du, win[:, cols], 1, 1)
-        out_o[...] = (x1 + mixed + pack[7:8, :]).astype(BF)
         dy = cot.astype(F32)
-        dx1 = dy + norm_back(dh2, unit, scale, pack[4:5, :])
+        dx1 = dy + norm_back(dh2, unit, scale, flat(g_ref))
         dx1_o[...] = dx1
         da = dx1.astype(BF)
         vec_o[...] = jnp.concatenate([
@@ -275,7 +284,6 @@
             jnp.sum(dh2, axis=0, keepdims=True),
             jnp.sum(dy, axis=0, keepdims=True),
             jnp.zeros((4, D), F32)], 0)
-        dattn = dot(da, wout[...], 1, 1).astype(BF)
         parts = [da[:, i * cs:(i + 1) * cs] for i in range(S)]
         bit = 1
         while bit < S:
@@ -283,7 +291,10 @@
             parts = [jnp.where(on, parts[i ^ bit], parts[i]) for i in range(S)]
             bit *= 2
         for k in range(S):
-            both[k][...] = jnp.concatenate([dattn[:, k * cs:(k + 1) * cs], parts[k]], 1)
+            both[k][...] = jnp.concatenate([dot(da, heads[k], 1, 1).astype(BF), parts[k]], 1)
+
+    def out_kernel(x1_ref, act, wdown, bdown, out_o):
+        out_o[...] = (x1_ref[...] + dot(act[...], wdown[...]) + flat(bdown)).astype(BF)
 
     def attn_bwd_kernel(*refs):
         xs, boths = refs[:S], refs[S:2 * S]
@@ -299,26 +310,50 @@
         row = row_ref[0:1, :]
         dattn = jnp.concatenate([r[:, :cs] for r in boths], 0)
         dattn_t = jnp.transpose(dattn)
-        q_t = jnp.transpose(qkv[:, :cs])
-        for h in range(cs // HEAD_DIM):
+        q_t = jnp.transpose(qkv[:, :cs] * BF(scale))
+        Q = 512
+        heads = cs // HEAD_DIM
+        todo = [(h, n) for h in range(heads) for n in range(L // Q)]
+
+        def part(c, h, rows=slice(None)):
+            return qkv[rows, c * cs + h * HEAD_DIM:c * cs + (h + 1) * HEAD_DIM]
+
+        def products(h, n):
+            rows = slice(n * Q, (n + 1) * Q)
+            return (dot(part(0, h, rows) * BF(scale), part(1, h), 1, 1),
+                    dot(dattn[rows, h * HEAD_DIM:(h + 1) * HEAD_DIM], part(2, h), 1, 1))
+
+        def slopes(sc, dp, h, n):
+            rows = slice(n * Q, (n + 1) * Q)
+            sc = jnp.where(col_ref[rows, :1] == row, sc, -1e30)
+            p = jnp.exp(sc - lse[rows, h:h + 1])
+            inner = jnp.sum(p * dp, axis=-1, keepdims=True)
+            return p.astype(BF), (p * (dp - inner)).astype(BF)
+
+        dk = [jnp.zeros((HEAD_DIM, L), F32) for _ in range(heads)]
+        dv = [jnp.zeros((HEAD_DIM, L), F32) for _ in range(heads)]
+
+        def gradients(p, ds, h, n):
+            rows = slice(n * Q, (n + 1) * Q)
             at = h * HEAD_DIM
-            keys = qkv[:, cs + at:cs + at + HEAD_DIM]
-            vals = qkv[:, 2 * cs + at:2 * cs + at + HEAD_DIM]
-            dk = jnp.zeros((HEAD_DIM, L), F32)
-            dv = jnp.zeros((HEAD_DIM, L), F32)
-            for k in range(S):
-                rows = slice(k * t, (k + 1) * t)
-                sc = dot(qkv[rows, at:at + HEAD_DIM], keys, 1, 1) * scale
-                sc = jnp.where(col_ref[rows, :1] == row, sc, -1e30)
-                p = jnp.exp(sc - lse[rows, h:h + 1])
-                dp = dot(dattn[rows, at:at + HEAD_DIM], vals, 1, 1)
-                inner = jnp.sum(p * dp, axis=-1, keepdims=True)
-                ds = (p * (dp - inner)).astype(BF)
-                dqkv_s[rows, at:at + HEAD_DIM] = (dot(ds, keys) * scale).astype(BF)
-                dk = dk + dot(q_t[at:at + HEAD_DIM, rows], ds)
-                dv = dv + dot(dattn_t[at:at + HEAD_DIM, rows], p.astype(BF))
-            dqkv_s[:, cs + at:cs + at + HEAD_DIM] = jnp.transpose((dk * scale).astype(BF))
-            dqkv_s[:, 2 * cs + at:2 * cs + at + HEAD_DIM] = jnp.transpose(dv.astype(BF))
+            dqkv_s[rows, at:at + HEAD_DIM] = dot(ds, part(1, h) * BF(scale)).astype(BF)
+            dk[h] = dk[h] + dot(q_t[at:at + HEAD_DIM, rows], ds)
+            dv[h] = dv[h] + dot(dattn_t[at:at + HEAD_DIM, rows], p)
+            if n == L // Q - 1:
+                dqkv_s[:, cs + at:cs + at + HEAD_DIM] = jnp.transpose(dk[h].astype(BF))
+                dqkv_s[:, 2 * cs + at:2 * cs + at + HEAD_DIM] = jnp.transpose(dv[h].astype(BF))
+
+        ahead = products(*todo[0])
+        behind = None
+        for i, at in enumerate(todo):
+            now = ahead
+            if i + 1 < len(todo):
+                ahead = products(*todo[i + 1])
+            p, ds = slopes(*now, *at)
+            if behind is not None:
+                gradients(*behind)
+            behind = (p, ds) + at
+        gradients(*behind)
         bsum = jnp.sum(dqkv_s[...].astype(F32), axis=0, keepdims=True)
         gg = jnp.zeros((1, D), F32)
         gb = jnp.zeros((1, D), F32)
@@ -331,10 +366,10 @@
             gb = gb + jnp.sum(dh1, axis=0, keepdims=True)
             if k == 0:
                 own_o[...] = dh1
-            elif k == 1:
+            elif k == DH[1]:
                 next_o[...] = dh1
             else:
-                away_o[k - 2] = dh1.astype(BF)
+                away_o[int(k != DH[0])] = dh1.astype(BF)
         gw = dot(h1_s[...], dqkv_s[...], 0, 0)
         gw_s[:, :, :3 * cs] = gw.reshape(NB, R, 3 * cs)
         zero = jnp.zeros((1, cs), F32)
@@ -344,7 +379,7 @@
         first = jnp.concatenate([wide[:, 2 * i * R:(2 * i + 1) * R] for i in range(NB)], 1)
         second = jnp.concatenate([wide[:, (2 * i + 1) * R:(2 * i + 2) * R] for i in range(NB)], 1)
         gw_s[:, :, 3 * cs:] = columns([gg, gb, first, second], gw_s.shape[2] - 3 * cs)
-        store_blocks(gw_s, keep_o, send_o, b)
+        store_blocks(gw_s, keep_o, send_o, b, hops["a"])
 
     def down_final_kernel(ks, *refs):
         parts, (wdn_o,) = refs[:-1], refs[-1:]
@@ -415,112 +450,201 @@
         x_own = tokens.reshape(t, D)
         cot_own = cotangent.reshape(t, D)
 
-        xs = gather_seq(x_own, S)
-        at = lax.broadcasted_iota(jnp.int32, (8, D), 0)
-        seg_wide = jnp.pad(segments.astype(F32), ((0, 0), (0, D - L)))
-        pack1 = seg_wide
-        for i, v in enumerate((ln1_gain, ln1_bias, bias_qv[:D], bias_qv[D:])):
-            pack1 = jnp.where(at == i, v[None, :], pack1)
-        wq_s, pack1, seg_row, seg_col = call(
-            prep_qkv_kernel,
-            [sds((D, 3 * cs), BF), sds((8, D), F32), sds((8, L), F32), sds((L, 128), F32)],
-            [w_qkv, pack1], "prep_qkv")
-        cots = gather_seq(cot_own, S)
-        attn, qkv, lse = call(
-            attn_fwd_kernel,
-            [sds((L // 2, 2 * cs), BF), sds((L, 3 * cs), BF), sds((L, 128), F32)],
-            [*xs, seg_row, seg_col, pack1, wq_s], "attn_fwd", flops=2 * L * D * 3 * cs)
-        attn, *cots = lax.optimization_barrier((attn, *cots))
-        ats = gather_seq(attn, S)
-        w_in_late, _ = lax.optimization_barrier((w_in, attn))
-        win_s, wout_s, wdn_s, pack = call(
-            prep_mlp_kernel,
-            [sds((D, NF), BF), sds((D, D), BF), sds((NF, D), BF), sds((16, D), F32)],
-            [w_in_late, w_out, w_down, bias_out, ln2_gain, ln2_bias, bias_in, bias_down], "prep_mlp")
-
-        def halve(keep, send, step, after=()):
-            got = exchange(send, "batch", NB, step)
-            got, keep, after = lax.optimization_barrier((got, keep, after))
-            n = keep.shape[0]
-            total = lambda lo, hi: (keep[lo:hi].astype(F32) + got[lo:hi].astype(F32)).astype(BF)
-            if n == 1:
-                return total(0, 1)
-            return total(0, n // 2), total(n // 2, n)
-
-        out, dx1, vec, *both = pl.pallas_call(
-            local_kernel,
-            out_shape=[sds((t, D), BF), sds((t, D), F32), sds((8, D), F32)] + [sds((t, 2 * cs), BF)] * S,
-            name="local",
-            cost_estimate=pl.CostEstimate(flops=2 * t * D * FF * 4, bytes_accessed=10 * MIB, transcendentals=0),
-            compiler_params=pltpu.CompilerParams(vmem_limit_bytes=40 * MIB),
-        )(x_own, *ats, cot_own, wout_s, pack, w_in, w_down)
-        boths = [both[0]] + [exchange(both[k], "seq", S, k) for k in range(1, S)]
-        ats = lax.optimization_barrier((*ats, dx1))[:S]
-        attn_all, h2, slope, keep_d, send_d = pl.pallas_call(
-            up_kernel,
-            out_shape=[sds((L, D), BF), sds((L, D), BF), sds((L, NF), F32),
-                       sds((NB // 2, FJ, D), BF), sds((NB // 2, FJ, D), BF)],
-            scratch_shapes=[pltpu.VMEM((L, NF), BF), pltpu.VMEM((L, D), BF),
-                            pltpu.VMEM((NB, FJ, D), F32)],
-            name="up",
-            compiler_params=pltpu.CompilerParams(vmem_limit_bytes=32 * MIB),
-        )(*xs, *ats, *cots, wout_s, pack, win_s)
-        send_d, *boths = lax.optimization_barrier((send_d, *boths))
         wide_u, wide_a = -(-(NF + cs + 8) // 128) * 128, -(-(3 * cs + 8) // 128) * 128
-        keep_u, send_u = pl.pallas_call(
-            down_kernel,
-            out_shape=[sds((NB // 2, R, wide_u), BF), sds((NB // 2, R, wide_u), BF)],
-            scratch_shapes=[pltpu.VMEM((L, NF), BF), pltpu.VMEM((L, cs), BF), pltpu.VMEM((NB, R, wide_u), F32)],
-            name="down",
-            compiler_params=pltpu.CompilerParams(vmem_limit_bytes=32 * MIB),
-        )(*cots, *boths, h2, slope, wdn_s, attn_all, vec)
-        kd, sd = halve(keep_d, send_d, 1)
-        kd, sd, send_u = lax.optimization_barrier((kd, sd, send_u))
-        ku, su = halve(keep_u, send_u, 1, sd)
-        qkv, su = lax.optimization_barrier((qkv, su))
-        own, beside, away, keep_a, send_a = pl.pallas_call(
-            attn_bwd_kernel,
-            out_shape=[sds((t, D), F32), sds((t, D), F32), sds((S - 2, t, D), BF),
-                       sds((NB // 2, R, wide_a), BF), sds((NB // 2, R, wide_a), BF)],
-            scratch_shapes=[pltpu.VMEM((L, D), BF), pltpu.VMEM((L, 3 * cs), BF), pltpu.VMEM((NB, R, wide_a), F32)],
-            name="attn_bwd",
-            cost_estimate=pl.CostEstimate(flops=2 * L * D * D * 4, bytes_accessed=10 * MIB, transcendentals=0),
-            compiler_params=pltpu.CompilerParams(vmem_limit_bytes=40 * MIB),
-        )(*xs, *boths, seg_row, seg_col, pack1, wq_s, qkv, lse)
-        kd, sd = halve(kd, sd, 2, keep_a)
-        ku, su = halve(ku, su, 2, sd)
-        ka, sa = halve(keep_a, send_a, 1, su)
-        away, sa = lax.optimization_barrier((away, sa))
-        got = exchange(away, "seq", S, 2)
-        kd = halve(kd, sd, 4, sa)
-        ka, sa = halve(ka, sa, 2, kd)
-        got, sa = lax.optimization_barrier((got, sa))
-        beside = exchange((beside + got[1].astype(F32)).astype(BF), "seq", S, 1)
-        dh1 = own + got[0].astype(F32) + beside.astype(F32)
-        kd, sa = lax.optimization_barrier((kd, sa))
-        down, ks_d = gather_steps(kd[0], S, (1, 2))
-        ku = halve(ku, su, 4, sa)
-        up, ks_u = gather_steps(ku[0], S, (2, 1))
-        ka = halve(ka, sa, 4, ku)
-        att = gather_seq(ka[0], S)
-        ks_a = [[k] for k in range(S)]
-        unit1, scale1 = norm_parts(x_own.astype(F32))
-        d_tokens = (dx1 + norm_back(dh1, unit1, scale1, ln1_gain)).reshape(tokens.shape)
-
-        o_wdn, = pl.pallas_call(
-            functools.partial(down_final_kernel, ks_d), out_shape=[sds((S * FJ, D), F32)], name="down_final",
-            compiler_params=pltpu.CompilerParams(vmem_limit_bytes=24 * MIB))(*down)
         vec_out = sds((R,), F32)
-        o_win, o_wout, o_bout, o_ln2g, o_ln2b, o_bdn, o_bin = pl.pallas_call(
-            functools.partial(up_final_kernel, ks_u),
-            out_shape=[sds((R, FF), F32), sds((R, D), F32)] + [vec_out] * 4 + [sds((S * FJ,), F32)],
-            scratch_shapes=[pltpu.VMEM((S, R, wide_u), F32)], name="up_final",
-            compiler_params=pltpu.CompilerParams(vmem_limit_bytes=24 * MIB))(*up)
-        o_wqkv, o_ln1g, o_ln1b, o_bqv = pl.pallas_call(
-            functools.partial(att_final_kernel, ks_a),
-            out_shape=[sds((R, 3 * D), F32), vec_out, vec_out, sds((2 * R,), F32)],
-            scratch_shapes=[pltpu.VMEM((S, R, wide_a), F32)], name="att_final",
-            compiler_params=pltpu.CompilerParams(vmem_limit_bytes=24 * MIB))(*att)
+        v = {}
+        token = [None]
+
+        def wait(*names):
+            vals = tuple(v[n] for n in names)
+            if token[0] is not None:
+                vals, _ = lax.optimization_barrier((vals, token[0]))
+            return vals
+
+        def kernel(body, outs, args, name, scratch=(), limit=24, us=1):
+            return pl.pallas_call(
+                body, out_shape=outs, scratch_shapes=list(scratch), name=name,
+                cost_estimate=pl.CostEstimate(flops=us * 10**9, bytes_accessed=us * 2 * 10**6, transcendentals=0),
+                compiler_params=pltpu.CompilerParams(vmem_limit_bytes=limit * MIB))(*args)
+
+        def prep_qkv():
+            at = lax.broadcasted_iota(jnp.int32, (8, D), 0)
+            pack1 = jnp.pad(segments.astype(F32), ((0, 0), (0, D - L)))
+            for i, vec in enumerate((ln1_gain, ln1_bias, bias_qv[:D], bias_qv[D:])):
+                pack1 = jnp.where(at == i, vec[None, :], pack1)
+            v["wq"], v["pack1"], v["row"], v["col"] = kernel(
+                prep_qkv_kernel, [sds((D, 3 * cs), BF), sds((8, D), F32), sds((8, L), F32), sds((L, 128), F32)],
+                [w_qkv, pack1], "prep_qkv")
+            cot_late, _ = lax.optimization_barrier((cot_own, v["col"]))
+            v["cots"] = tuple(gather_seq(cot_late, S))
+
+        def attn_fwd():
+            near, far = sds((t // 2, 2 * cs), BF), sds(((L - t) // 2, 2 * cs), BF)
+            v["qkv"], v["lse"], v["attn"], *sends = kernel(
+                attn_fwd_kernel,
+                [sds((L, 3 * cs), BF), sds((L, 128), F32), sds((L, cs), BF)] + [near] * (S - 1) + [far] * (S - 1),
+                v["xs"] + wait("row", "col", "pack1", "wq"), "attn_fwd", us=6)
+            v["nears"] = tuple(exchange(sends[m - 1], "seq", S, m) for m in range(1, S))
+            far_sends, _ = lax.optimization_barrier((tuple(sends[S - 1:]), sends[0]))
+            v["fars"] = tuple(exchange(far_sends[m - 1], "seq", S, m) for m in range(1, S))
+            token[0] = v["attn"]
+
+        def cots(*ks):
+            def run():
+                got = list(v["cots"])
+                vals, _ = lax.optimization_barrier((tuple(got[k] for k in ks), token[0]))
+                for k, g in zip(ks, vals):
+                    got[k] = g
+                v["cots"] = tuple(got)
+                token[0] = got[ks[-1]]
+            return run
+
+        def prep_mlp():
+            (w,) = wait("w_in")
+            v["win_s"], v["wout_s"], v["wdn_s"], v["bin_s"] = kernel(
+                prep_mlp_kernel, [sds((D, NF), BF), sds((D, D), BF), sds((NF, D), BF), sds((1, NF), F32)],
+                [w, w_out, w_down, bias_in], "prep_mlp")
+            token[0] = v["bin_s"]
+
+        def local():
+            (nears,) = wait("nears")
+            v["act"], v["x1"], v["dx1"], v["vec"], *both = kernel(
+                local_kernel,
+                [sds((t, FF), BF), sds((t, D), F32), sds((t, D), F32), sds((8, D), F32)]
+                + [sds((t, 2 * cs), BF)] * S,
+                (x_own, v["attn"]) + nears + (cot_own, w_out, bias_out, ln2_gain, ln2_bias, w_in, bias_in, w_down),
+                "local", limit=20, us=5)
+            v["nears"] = nears
+            v["boths"] = (both[0],) + tuple(exchange(both[k], "seq", S, k) for k in range(1, S))
+            token[0] = v["dx1"]
+
+        def fars():
+            (v["fars"],) = wait("fars")
+            token[0] = v["fars"][0]
+
+        def up():
+            nears, fars, cots = wait("nears", "fars", "cots")
+            v["cots"] = cots
+            v["attn_all"], v["h2"], v["slope"], v["d_keep"], v["d_send"] = kernel(
+                up_kernel,
+                [sds((L, D), BF), sds((L, D), BF), sds((L, NF), F32),
+                 sds((NB // 2, FJ, D), BF), sds((NB // 2, FJ, D), BF)],
+                v["xs"] + (v["attn"],) + nears + fars + cots
+                + (v["wout_s"], bias_out, ln2_gain, ln2_bias, v["win_s"], v["bin_s"]), "up",
+                [pltpu.VMEM((L, NF), BF), pltpu.VMEM((L, D), BF), pltpu.VMEM((NB, FJ, D), F32)], 32)
+            v["d_got"] = exchange(v["d_send"], "batch", NB, 1)
+            token[0] = v["d_keep"]
+
+        def both():
+            (v["boths"],) = wait("boths")
+            token[0] = v["boths"][1]
+
+        def down():
+            boths, h2 = wait("boths", "h2")
+            v["u_keep"], v["u_send"] = kernel(
+                down_kernel, [sds((NB // 2, R, wide_u), BF), sds((NB // 2, R, wide_u), BF)],
+                v["cots"] + boths + (h2, v["slope"], v["wdn_s"], v["attn_all"], v["vec"]), "down",
+                [pltpu.VMEM((L, NF), BF), pltpu.VMEM((L, cs), BF), pltpu.VMEM((NB, R, wide_u), F32)], 32)
+            v["u_got"] = exchange(v["u_send"], "batch", NB, 1)
+            token[0] = v["u_keep"]
+
+        def attn_bwd():
+            boths, qkv = wait("boths", "qkv")
+            v["own"], v["beside"], away, v["a_keep"], v["a_send"] = kernel(
+                attn_bwd_kernel,
+                [sds((t, D), F32), sds((t, D), F32), sds((S - 2, t, D), BF),
+                 sds((NB // 2, R, wide_a), BF), sds((NB // 2, R, wide_a), BF)],
+                v["xs"] + boths + (v["row"], v["col"], v["pack1"], v["wq"], qkv, v["lse"]), "attn_bwd",
+                [pltpu.VMEM((L, D), BF), pltpu.VMEM((L, 3 * cs), BF), pltpu.VMEM((NB, R, wide_a), F32)], 32)
+            v["a_got"] = exchange(v["a_send"], "batch", NB, 1)
+            v["h_got"] = exchange(away, "seq", S, DH[0])
+            token[0] = v["a_keep"]
+
+        def halve(name, level):
+            def run():
+                got, keep = wait(name + "_got", name + "_keep")
+                n = keep.shape[0]
+                total = lambda lo, hi: (keep[lo:hi].astype(F32) + got[lo:hi].astype(F32)).astype(BF)
+                if n > 1:
+                    v[name + "_keep"], send = total(0, n // 2), total(n // 2, n)
+                    v[name + "_got"] = exchange(send, "batch", NB, hops[name][level + 1])
+                    token[0] = send
+                    return
+                mine = total(0, 1)[0]
+                token[0] = mine
+                if GATHER[name] is None:
+                    v[name + "_all"] = gather_seq(mine, S)
+                    v[name + "_ks"] = [[k] for k in range(S)]
+                else:
+                    first, second = GATHER[name]
+                    v[name + "_all"] = [mine, exchange(mine, "seq", S, first)]
+                    v[name + "_ks"] = [[0], [first], [second, first ^ second]]
+            return run
+
+        def spread(name):
+            def run():
+                if GATHER[name] is None:
+                    return
+                (parts,) = wait(name + "_all")
+                pair = jnp.stack(parts)
+                v[name + "_all"] = list(parts) + [exchange(pair, "seq", S, GATHER[name][1])]
+                token[0] = pair
+            return run
+
+        def d_final():
+            (parts,) = wait("d_all")
+            v["o_wdn"], = kernel(
+                functools.partial(down_final_kernel, v["d_ks"]), [sds((S * FJ, D), F32)], parts, "down_final")
+            token[0] = v["o_wdn"]
+
+        def u_final():
+            (parts,) = wait("u_all")
+            v["o_u"] = kernel(
+                functools.partial(up_final_kernel, v["u_ks"]),
+                [sds((R, FF), F32), sds((R, D), F32)] + [vec_out] * 4 + [sds((S * FJ,), F32)],
+                parts, "up_final", [pltpu.VMEM((S, R, wide_u), F32)])
+            token[0] = v["o_u"][0]
+
+        def a_final():
+            (parts,) = wait("a_all")
+            v["o_a"] = kernel(
+                functools.partial(att_final_kernel, v["a_ks"]),
+                [sds((R, 3 * D), F32), vec_out, vec_out, sds((2 * R,), F32)],
+                parts, "att_final", [pltpu.VMEM((S, R, wide_a), F32)])
+            token[0] = v["o_a"][0]
+
+        def h_first():
+            (got,) = wait("h_got")
+            beside = (v["beside"] + got[1].astype(F32)).astype(BF)
+            v["own"] = v["own"] + got[0].astype(F32)
+            v["h_got"] = exchange(beside, "seq", S, DH[1])
+            token[0] = beside
+
+        def h_last():
+            (got,) = wait("h_got")
+            unit1, scale1 = norm_parts(x_own.astype(F32))
+            dh1 = v["own"] + got.astype(F32)
+            v["d_tokens"] = v["dx1"] + norm_back(dh1, unit1, scale1, ln1_gain)
+            token[0] = v["d_tokens"]
+
+        def forward_out():
+            x1, act = wait("x1", "act")
+            v["out"], = kernel(out_kernel, [sds((t, D), BF)], [x1, act, w_down, bias_down], "out")
+            token[0] = v["out"]
+
+        v["xs"] = tuple(gather_seq(x_own, S))
+        v["w_in"] = w_in
+        steps = dict(
+            pq=prep_qkv, af=attn_fwd, c1=cots(1), c2=cots(2), c3=cots(3), fa=fars, pm=prep_mlp, lo=local, up=up, bo=both,
+            dn=down, bw=attn_bwd, d0=halve("d", 0), d1=halve("d", 1), d2=halve("d", 2), d3=spread("d"), d4=d_final,
+            u0=halve("u", 0), u1=halve("u", 1), u2=halve("u", 2), u3=spread("u"), u4=u_final,
+            a0=halve("a", 0), a1=halve("a", 1), a2=halve("a", 2), a3=spread("a"), a4=a_final,
+            h1=h_first, h2=h_last, ou=forward_out)
+        for name in ORDER:
+            steps[name]()
+        out, d_tokens, o_wdn = v["out"], v["d_tokens"].reshape(tokens.shape), v["o_wdn"]
+        o_win, o_wout, o_bout, o_ln2g, o_ln2b, o_bdn, o_bin = v["o_u"]
+        o_wqkv, o_ln1g, o_ln1b, o_bqv = v["o_a"]
         return (out.reshape(tokens.shape), d_tokens, o_ln1g, o_ln1b, o_wqkv, o_bqv, o_wout, o_bout,
                 o_ln2g, o_ln2b, o_win, o_bin, o_wdn, o_bdn)
     return shards

time: 110 us -> 97 us (0.88)
  waiting for transfers between devices: 29 us -> 17.4 us
  starting transfers between devices: 38.1 us -> 45.9 us
  Pallas kernels: 30.7 us -> 25.5 us
  local copies, waits for them, and re-layouts: 6.43 us -> 2.85 us
    ppermute x30 -> x35, waiting for transfers between devices: 29 us -> 17.4 us  [exchange(): return lax.ppermute(value, axis, [(j, j ^ step) for j in range(size)])]
    ppermute x30 -> x35, starting transfers between devices: 38.1 us -> 45.9 us  [exchange(): return lax.ppermute(value, axis, [(j, j ^ step) for j in range(size)])]
    pallas_call x10 -> x11, Pallas kernels: 30.7 us -> 25.5 us  [kernel(): pl.pallas_call(body, out_shape=outs, scratch_shapes=list(scratch), name=n...]
    unnamed x26 -> x28, local copies, waits for them, and re-layouts: 5.65 us -> 2.06 us
  transfers between devices with their start and end apart: 30 -> 35, of which waited for: 12 -> 9; matrix products, arithmetic and copies ran while one was open for 4% -> 5% of each run, Pallas kernels for 21% -> 25%
where the time goes in v3:
time: 97 us; the launch traced here: 96.7 us
  starting transfers between devices  45.9 us (47%)
  Pallas kernels  25.5 us (26%)
  waiting for transfers between devices  17.4 us (18%)
  other arithmetic  4.01 us (4%)
  local copies, waits for them, and re-layouts  2.85 us (3%)
  between operations  1.06 us (1%)
    ppermute x35, starting transfers between devices, exchange(): return lax.ppermute(value, axis, [(j, j ^ step) for j in range(size)])  45.9 us
    pallas_call x11, Pallas kernels, kernel(): pl.pallas_call(body, out_shape=outs, scratch_shapes=list(scratch), name=n...  25.5 us
    ppermute x35, waiting for transfers between devices, exchange(): return lax.ppermute(value, axis, [(j, j ^ step) for j in range(size)])  17.4 us
    unnamed x28, local copies, waits for them, and re-layouts  2.06 us
  transfers between devices with their start and end apart: 35, of which 9 were waited for; matrix products, arithmetic and copies ran while one was open for 5% of the time, Pallas kernels for 25%

profile of v3, /device:TPU:0, one launch (start us, length us, event | category | flops | bytes accessed | tf_op | source)
XLA Modules:
  0.0 96.7 jit_solution(13712748404861098432)
XLA Ops:
  0.6 3.0 %collective-permute-start = (bf16[128,768]{1,0:T(8,128)(2,1)}, bf16[128,768]{1,0:T(8,128)(2,1)S(1)}, u32[]{:S(2)}, u32[]{:S(2)}) collective-permute-start(bf16[128,768]{1,0:T(8,128)(2,1)} %bitcast.23), channel_id=1, source_target_pairs={{0,8},{8,0},{16,24},{24,16},{1,9},{9,1},{17,25},{25,17},{2,10},{10... | collective-permute-start | bytes 589832 | tf_op jit(solution)/shard_map/ppermute | solution.py:23
  3.6 1.5 %collective-permute-start.1 = (bf16[128,768]{1,0:T(8,128)(2,1)}, bf16[128,768]{1,0:T(8,128)(2,1)S(1)}, u32[]{:S(2)}, u32[]{:S(2)}) collective-permute-start(bf16[128,768]{1,0:T(8,128)(2,1)} %bitcast.24), channel_id=1, source_target_pairs={{0,16},{8,24},{16,0},{24,8},{1,17},{9,25},{17,1},{25,9},{2,18},{10... | collective-permute-start | bytes 589832 | tf_op jit(solution)/shard_map/ppermute | solution.py:23
  7.5 2.0 %copy-done.8 = bf16[768,2304]{1,0:T(8,128)(2,1)S(1)} copy-done((bf16[768,2304]{1,0:T(8,128)(2,1)S(1)}, bf16[768,2304]{1,0:T(8,128)(2,1)}, u32[]{:S(2)}) %copy-start.8) | copy-done | bytes 3538968
  9.8 2.1 %collective-permute-start.8 = (bf16[128,768]{1,0:T(8,128)(2,1)S(1)}, bf16[128,768]{1,0:T(8,128)(2,1)S(1)}, u32[]{:S(2)}, u32[]{:S(2)}) collective-permute-start(bf16[128,768]{1,0:T(8,128)(2,1)S(1)} %bitcast.32), channel_id=1, source_target_pairs={{0,8},{8,0},{16,24},{24,16},{1,9},{9,1},{17,25},{25,17},{2,10},{10... | collective-permute-start | bytes 589832 | tf_op jit(solution)/shard_map/ppermute | solution.py:23
  12.0 1.5 %collective-permute-start.7 = (bf16[128,768]{1,0:T(8,128)(2,1)S(1)}, bf16[128,768]{1,0:T(8,128)(2,1)S(1)}, u32[]{:S(2)}, u32[]{:S(2)}) collective-permute-start(bf16[128,768]{1,0:T(8,128)(2,1)S(1)} %bitcast.33), channel_id=1, source_target_pairs={{0,16},{8,24},{16,0},{24,8},{1,17},{9,25},{17,1},{25,9},{2,18},{10... | collective-permute-start | bytes 589832 | tf_op jit(solution)/shard_map/ppermute | solution.py:23
  15.4 2.9 %attn_fwd.1 = (bf16[512,576]{1,0:T(8,128)(2,1)S(1)}, f32[512,128]{1,0:T(8,128)S(1)}, bf16[512,192]{1,0:T(8,128)(2,1)S(1)}, bf16[64,384]{1,0:T(8,128)(2,1)S(1)}, ...) custom-call(bf16[128,768]{1,0:T(8,128)(2,1)S(1)} %bitcast.26, ...), custom_call_target="tpu_custom_call" | custom-call | flops 6000000000 | bytes 12000000 | tf_op jit(solution)/shard_map/attn_fwd/pallas_call | solution.py:465
  23.8 1.7 %collective-permute-start.10 = (bf16[192,384]{1,0:T(8,128)(2,1)S(1)}, bf16[192,384]{1,0:T(8,128)(2,1)S(1)}, u32[]{:S(2)}, u32[]{:S(2)}) collective-permute-start(bf16[192,384]{1,0:T(8,128)(2,1)S(1)} %get-tuple-element.151), channel_id=1, source_target_pairs={{0,16},{8,24},{16,0},{24,8},{1,17},{9,25},{17,1},{25,9},{2,18},{10... | collective-permute-start | bytes 442376 | tf_op jit(solution)/shard_map/ppermute | solution.py:23
  27.4 5.0 %local.1 = (bf16[128,3072]{1,0:T(8,128)(2,1)S(1)}, f32[128,768]{1,0:T(8,128)S(1)}, f32[128,768]{1,0:T(8,128)S(1)}, f32[8,768]{1,0:T(8,128)S(1)}, bf16[128,384]{1...) custom-call(bf16[128,768]{1,0:T(8,128)(2,1)S(1)} %bitcast.27, ...), custom_call_target="tpu_custom_call" | custom-call | flops 5000000000 | bytes 10000000 | tf_op jit(solution)/shard_map/local/pallas_call | solution.py:465
  37.1 3.6 %up.1 = (bf16[512,768]{1,0:T(8,128)(2,1)S(1)}, bf16[512,768]{1,0:T(8,128)(2,1)S(1)}, f32[512,768]{1,0:T(8,128)S(1)}, bf16[4,96,768]{2,1,0:T(8,128)(2,1)S(1)}, bf16[4,96,768]{2,1,0:T(8,128)(2,1)S(1)}) custom-call(bf16[128,768]{1,0:T(8,128)(2,1)S(1)} %bitcast.28, bf16[128,768]{1,0:T(8,128)(2,1)S(1)} %collective-permute-done.refs_1_, ...), custom_call_target="tpu_custom_call" | custom-call | flops 1000000000 | bytes 2000000 | tf_op jit(solution)/shard_map/up/pallas_call | solution.py:465
  40.8 1.9 %down.1 = (bf16[4,96,1024]{2,1,0:T(8,128)(2,1)S(1)}, bf16[4,96,1024]{2,1,0:T(8,128)(2,1)S(1)}) custom-call(bf16[128,768]{1,0:T(8,128)(2,1)S(1)} %bitcast.37, bf16[128,768]{1,0:T(8,128)(2,1)S(1)} %collective-permute-done.8.refs_12_.refs_1_, bf16[128,768]{1,0:T(8,128)(2,1)S(1)} %collective-permute-done.7.refs_13_.refs_2_, ...), custom_call_target="tpu_custom_call" | custom-call | flops 1000000000 | bytes 2000000 | tf_op jit(solution)/shard_map/down/pallas_call | solution.py:465
  43.8 2.8 %collective-permute-start.16 = (bf16[2,96,768]{2,1,0:T(8,128)(2,1)S(1)}, bf16[2,96,768]{2,1,0:T(8,128)(2,1)S(1)}, u32[]{:S(2)}, u32[]{:S(2)}) collective-permute-start(bf16[2,96,768]{2,1,0:T(8,128)(2,1)S(1)} %get-tuple-element.252), channel_id=1, source_target_pairs={{0,4},{1,5},{2,6},{3,7},{4,0},{5,1},{6,2},{7,3},{8,12},{9,13},{10,... | collective-permute-start | bytes 884744 | tf_op jit(solution)/shard_map/ppermute | solution.py:23
  46.9 1.6 %collective-permute-start.24 = (bf16[2,96,1024]{2,1,0:T(8,128)(2,1)S(1)}, bf16[2,96,1024]{2,1,0:T(8,128)(2,1)S(1)}, u32[]{:S(2)}, u32[]{:S(2)}) collective-permute-start(bf16[2,96,1024]{2,1,0:T(8,128)(2,1)S(1)} %get-tuple-element.250), channel_id=1, source_target_pairs={{0,2},{1,3},{2,0},{3,1},{4,6},{5,7},{6,4},{7,5},{8,10},{9,11},{10,... | collective-permute-start | bytes 1179656 | tf_op jit(solution)/shard_map/ppermute | solution.py:23
  48.6 4.9 %attn_bwd.1 = (f32[128,768]{1,0:T(8,128)S(1)}, f32[128,768]{1,0:T(8,128)S(1)}, bf16[2,128,768]{2,1,0:T(8,128)(2,1)S(1)}, bf16[4,96,640]{2,1,0:T(8,128)(2,1)S(1)}, bf16[4,96,640]{2,1,0:T(8,128)(2,1)S(1)}) custom-call(bf16[128,768]{1,0:T(8,128)(2,1)S(1)} %bitcast.29, bf16[128,768]{1,0:T(8,128)(2,1)S(1)} %collective-permute-done.refs_1_, ...), custom_call_target="tpu_custom_call" | custom-call | flops 1000000000 | bytes 2000000 | tf_op jit(solution)/shard_map/attn_bwd/pallas_call | solution.py:465
  54.9 5.3 %collective-permute-done.16 = bf16[2,96,768]{2,1,0:T(8,128)(2,1)S(1)} collective-permute-done((bf16[2,96,768]{2,1,0:T(8,128)(2,1)S(1)}, bf16[2,96,768]{2,1,0:T(8,128)(2,1)S(1)}, u32[]{:S(2)}, u32[]{:S(2)}) %collective-permute-start.16) | collective-permute-done | bytes 294944 | tf_op jit(solution)/shard_map/ppermute | solution.py:23
  61.0 2.5 %collective-permute-done.24 = bf16[2,96,1024]{2,1,0:T(8,128)(2,1)S(1)} collective-permute-done((bf16[2,96,1024]{2,1,0:T(8,128)(2,1)S(1)}, bf16[2,96,1024]{2,1,0:T(8,128)(2,1)S(1)}, u32[]{:S(2)}, u32[]{:S(2)}) %collective-permute-start.24) | collective-permute-done | bytes 393248 | tf_op jit(solution)/shard_map/ppermute | solution.py:23
  63.7 2.0 %collective-permute-start.25 = (bf16[1,96,1024]{2,1,0:T(8,128)(2,1)S(1)}, bf16[1,96,1024]{2,1,0:T(8,128)(2,1)S(1)}, u32[]{:S(2)}, u32[]{:S(2)}) collective-permute-start(bf16[1,96,1024]{2,1,0:T(8,128)(2,1)S(1)} %get-tuple-element.256), channel_id=1, source_target_pairs={{0,4},{1,5},{2,6},{3,7},{4,0},{5,1},{6,2},{7,3},{8,12},{9,13},{10,... | collective-permute-start | bytes 589832 | tf_op jit(solution)/shard_map/ppermute | solution.py:23
  65.8 2.5 %collective-permute-start.26 = (bf16[2,96,640]{2,1,0:T(8,128)(2,1)S(1)}, bf16[2,96,640]{2,1,0:T(8,128)(2,1)S(1)}, u32[]{:S(2)}, u32[]{:S(2)}) collective-permute-start(bf16[2,96,640]{2,1,0:T(8,128)(2,1)S(1)} %get-tuple-element.254), channel_id=1, source_target_pairs={{0,2},{1,3},{2,0},{3,1},{4,6},{5,7},{6,4},{7,5},{8,10},{9,11},{10,... | collective-permute-start | bytes 737288 | tf_op jit(solution)/shard_map/ppermute | solution.py:23
  72.0 3.5 %collective-permute-done.26 = bf16[2,96,640]{2,1,0:T(8,128)(2,1)S(1)} collective-permute-done((bf16[2,96,640]{2,1,0:T(8,128)(2,1)S(1)}, bf16[2,96,640]{2,1,0:T(8,128)(2,1)S(1)}, u32[]{:S(2)}, u32[]{:S(2)}) %collective-permute-start.26) | collective-permute-done | bytes 245792 | tf_op jit(solution)/shard_map/ppermute | solution.py:23
  75.5 2.0 %collective-permute-start.27 = (bf16[128,768]{1,0:T(8,128)(2,1)S(1)}, bf16[128,768]{1,0:T(8,128)(2,1)S(1)}, u32[]{:S(2)}, u32[]{:S(2)}) collective-permute-start(bf16[128,768]{1,0:T(8,128)(2,1)S(1)} %fusion.11), channel_id=1, source_target_pairs={{0,16},{8,24},{16,0},{24,8},{1,17},{9,25},{17,1},{25,9},{2,18},{10... | collective-permute-start | bytes 589832 | tf_op jit(solution)/shard_map/ppermute | solution.py:23
  77.6 2.5 %collective-permute-start.28 = (bf16[1,96,640]{2,1,0:T(8,128)(2,1)S(1)}, bf16[1,96,640]{2,1,0:T(8,128)(2,1)S(1)}, u32[]{:S(2)}, u32[]{:S(2)}) collective-permute-start(bf16[1,96,640]{2,1,0:T(8,128)(2,1)S(1)} %get-tuple-element.260), channel_id=1, source_target_pairs={{0,4},{1,5},{2,6},{3,7},{4,0},{5,1},{6,2},{7,3},{8,12},{9,13},{10,... | collective-permute-start | bytes 368648 | tf_op jit(solution)/shard_map/ppermute | solution.py:23
  81.6 2.2 %collective-permute-start.34 = (bf16[96,1024]{1,0:T(8,128)(2,1)S(1)}, bf16[96,1024]{1,0:T(8,128)(2,1)S(1)}, u32[]{:S(2)}, u32[]{:S(2)}) collective-permute-start(bf16[96,1024]{1,0:T(8,128)(2,1)S(1)} %fusion.12.refs_0_), channel_id=1, source_target_pairs={{0,24},{8,16},{16,8},{24,0},{1,25},{9,17},{17,9},{25,1},{2,26},{10... | collective-permute-start | bytes 589832 | tf_op jit(solution)/shard_map/ppermute | solution.py:23
  84.9 1.7 %out.1 = bf16[128,768]{1,0:T(8,128)(2,1)} custom-call(f32[128,768]{1,0:T(8,128)S(1)} %get-tuple-element.221.x1_ref, bf16[128,3072]{1,0:T(8,128)(2,1)S(1)} %get-tuple-element.222.act, bf16[3072,768]{1,0:T(8,128)(2,1)S(1)} %bitcast.22, f32[768]{0:T(1024)S(1)} %copy-done.7), custom_call_target="tpu_custom_call" | custom-call | flops 1000000000 | bytes 2000000 | tf_op jit(solution)/shard_map/out/pallas_call | solution.py:465
  88.2 2.3 %collective-permute-start.31 = (bf16[96,640]{1,0:T(8,128)(2,1)S(1)}, bf16[96,640]{1,0:T(8,128)(2,1)S(1)}, u32[]{:S(2)}, u32[]{:S(2)}) collective-permute-start(bf16[96,640]{1,0:T(8,128)(2,1)S(1)} %fusion.14.refs_0_), channel_id=1, source_target_pairs={{0,24},{8,16},{16,8},{24,0},{1,25},{9,17},{17,9},{25,1},{2,26},{10... | collective-permute-start | bytes 368648 | tf_op jit(solution)/shard_map/ppermute | solution.py:23
  92.6 1.7 %up_final.1 = (f32[96,3072]{1,0:T(8,128)}, f32[96,768]{1,0:T(8,128)}, f32[96]{0:T(128)}, f32[96]{0:T(128)}, f32[96]{0:T(128)}, /*index=5*/f32[96]{0:T(128)}, f32[384]{0:T(512)}) custom-call(bf16[96,1024]{1,0:T(8,128)(2,1)S(1)} %fusion.12.refs_0_, bf16[96,1024]{1,0:T(8,128)(2,1)S(1)} %collective-permute-done.32.refs_1_, ...), custom_call_target="tpu_custom_call" | custom-call | flops 1000000000 | bytes 2000000 | tf_op jit(solution)/shard_map/up_final/pallas_call | solution.py:465
  (111 shorter events, 32.7 us)
Async XLA Ops:
  0.6 12.9 %collective-permute-start = (bf16[128,768]{1,0:T(8,128)(2,1)}, bf16[128,768]{1,0:T(8,128)(2,1)S(1)}, u32[]{:S(2)}, u32[]{:S(2)}) collective-permute-start(bf16[128,768]{1,0:T(8,128)(2,1)} %bitcast.23), channel_id=1, source_target_pairs={{0,8},{8,0},{16,24},{24,16},{1,9},{9,1},{17,25},{25,17},{2,10},{10... | collective-permute-start | bytes 589832 | tf_op jit(solution)/shard_map/ppermute | solution.py:23
  3.6 10.8 %collective-permute-start.1 = (bf16[128,768]{1,0:T(8,128)(2,1)}, bf16[128,768]{1,0:T(8,128)(2,1)S(1)}, u32[]{:S(2)}, u32[]{:S(2)}) collective-permute-start(bf16[128,768]{1,0:T(8,128)(2,1)} %bitcast.24), channel_id=1, source_target_pairs={{0,16},{8,24},{16,0},{24,8},{1,17},{9,25},{17,1},{25,9},{2,18},{10... | collective-permute-start | bytes 589832 | tf_op jit(solution)/shard_map/ppermute | solution.py:23
  5.2 10.2 %collective-permute-start.2 = (bf16[128,768]{1,0:T(8,128)(2,1)}, bf16[128,768]{1,0:T(8,128)(2,1)S(1)}, u32[]{:S(2)}, u32[]{:S(2)}) collective-permute-start(bf16[128,768]{1,0:T(8,128)(2,1)} %bitcast.25), channel_id=1, source_target_pairs={{0,24},{8,16},{16,8},{24,0},{1,25},{9,17},{17,9},{25,1},{2,26},{10... | collective-permute-start | bytes 589832 | tf_op jit(solution)/shard_map/ppermute | solution.py:23
  9.8 10.6 %collective-permute-start.8 = (bf16[128,768]{1,0:T(8,128)(2,1)S(1)}, bf16[128,768]{1,0:T(8,128)(2,1)S(1)}, u32[]{:S(2)}, u32[]{:S(2)}) collective-permute-start(bf16[128,768]{1,0:T(8,128)(2,1)S(1)} %bitcast.32), channel_id=1, source_target_pairs={{0,8},{8,0},{16,24},{24,16},{1,9},{9,1},{17,25},{25,17},{2,10},{10... | collective-permute-start | bytes 589832 | tf_op jit(solution)/shard_map/ppermute | solution.py:23
  12.0 11.0 %collective-permute-start.7 = (bf16[128,768]{1,0:T(8,128)(2,1)S(1)}, bf16[128,768]{1,0:T(8,128)(2,1)S(1)}, u32[]{:S(2)}, u32[]{:S(2)}) collective-permute-start(bf16[128,768]{1,0:T(8,128)(2,1)S(1)} %bitcast.33), channel_id=1, source_target_pairs={{0,16},{8,24},{16,0},{24,8},{1,17},{9,25},{17,1},{25,9},{2,18},{10... | collective-permute-start | bytes 589832 | tf_op jit(solution)/shard_map/ppermute | solution.py:23
  13.5 10.3 %collective-permute-start.6 = (bf16[128,768]{1,0:T(8,128)(2,1)S(1)}, bf16[128,768]{1,0:T(8,128)(2,1)S(1)}, u32[]{:S(2)}, u32[]{:S(2)}) collective-permute-start(bf16[128,768]{1,0:T(8,128)(2,1)S(1)} %bitcast.34), channel_id=1, source_target_pairs={{0,24},{8,16},{16,8},{24,0},{1,25},{9,17},{17,9},{25,1},{2,26},{10... | collective-permute-start | bytes 589832 | tf_op jit(solution)/shard_map/ppermute | solution.py:23
  18.3 8.4 %collective-permute-start.3 = (bf16[64,384]{1,0:T(8,128)(2,1)S(1)}, bf16[64,384]{1,0:T(8,128)(2,1)S(1)}, u32[]{:S(2)}, u32[]{:S(2)}) collective-permute-start(bf16[64,384]{1,0:T(8,128)(2,1)S(1)} %get-tuple-element.135), channel_id=1, source_target_pairs={{0,8},{8,0},{16,24},{24,16},{1,9},{9,1},{17,25},{25,17},{2,10},{10... | collective-permute-start | bytes 147464 | tf_op jit(solution)/shard_map/ppermute | solution.py:23
  23.8 10.8 %collective-permute-start.10 = (bf16[192,384]{1,0:T(8,128)(2,1)S(1)}, bf16[192,384]{1,0:T(8,128)(2,1)S(1)}, u32[]{:S(2)}, u32[]{:S(2)}) collective-permute-start(bf16[192,384]{1,0:T(8,128)(2,1)S(1)} %get-tuple-element.151), channel_id=1, source_target_pairs={{0,16},{8,24},{16,0},{24,8},{1,17},{9,25},{17,1},{25,9},{2,18},{10... | collective-permute-start | bytes 442376 | tf_op jit(solution)/shard_map/ppermute | solution.py:23
  25.5 11.6 %collective-permute-start.11 = (bf16[192,384]{1,0:T(8,128)(2,1)S(1)}, bf16[192,384]{1,0:T(8,128)(2,1)S(1)}, u32[]{:S(2)}, u32[]{:S(2)}) collective-permute-start(bf16[192,384]{1,0:T(8,128)(2,1)S(1)} %get-tuple-element.152), channel_id=1, source_target_pairs={{0,24},{8,16},{16,8},{24,0},{1,25},{9,17},{17,9},{25,1},{2,26},{10... | collective-permute-start | bytes 442376 | tf_op jit(solution)/shard_map/ppermute | solution.py:23
  26.7 10.3 %collective-permute-start.9 = (bf16[192,384]{1,0:T(8,128)(2,1)S(1)}, bf16[192,384]{1,0:T(8,128)(2,1)S(1)}, u32[]{:S(2)}, u32[]{:S(2)}) collective-permute-start(bf16[192,384]{1,0:T(8,128)(2,1)S(1)} %get-tuple-element.150), channel_id=1, source_target_pairs={{0,8},{8,0},{16,24},{24,16},{1,9},{9,1},{17,25},{25,17},{2,10},{10... | collective-permute-start | bytes 442376 | tf_op jit(solution)/shard_map/ppermute | solution.py:23
  43.8 16.4 %collective-permute-start.16 = (bf16[2,96,768]{2,1,0:T(8,128)(2,1)S(1)}, bf16[2,96,768]{2,1,0:T(8,128)(2,1)S(1)}, u32[]{:S(2)}, u32[]{:S(2)}) collective-permute-start(bf16[2,96,768]{2,1,0:T(8,128)(2,1)S(1)} %get-tuple-element.252), channel_id=1, source_target_pairs={{0,4},{1,5},{2,6},{3,7},{4,0},{5,1},{6,2},{7,3},{8,12},{9,13},{10,... | collective-permute-start | bytes 884744 | tf_op jit(solution)/shard_map/ppermute | solution.py:23
  46.9 16.6 %collective-permute-start.24 = (bf16[2,96,1024]{2,1,0:T(8,128)(2,1)S(1)}, bf16[2,96,1024]{2,1,0:T(8,128)(2,1)S(1)}, u32[]{:S(2)}, u32[]{:S(2)}) collective-permute-start(bf16[2,96,1024]{2,1,0:T(8,128)(2,1)S(1)} %get-tuple-element.250), channel_id=1, source_target_pairs={{0,2},{1,3},{2,0},{3,1},{4,6},{5,7},{6,4},{7,5},{8,10},{9,11},{10,... | collective-permute-start | bytes 1179656 | tf_op jit(solution)/shard_map/ppermute | solution.py:23
  53.4 12.3 %collective-permute-start.20 = (bf16[4,96,640]{2,1,0:T(8,128)(2,1)S(1)}, bf16[4,96,640]{2,1,0:T(8,128)(2,1)S(1)}, u32[]{:S(2)}, u32[]{:S(2)}) collective-permute-start(bf16[4,96,640]{2,1,0:T(8,128)(2,1)S(1)} %get-tuple-element.205), channel_id=1, source_target_pairs={{0,1},{1,0},{2,3},{3,2},{4,5},{5,4},{6,7},{7,6},{8,9},{9,8},{10,11... | collective-permute-start | bytes 1474568 | tf_op jit(solution)/shard_map/ppermute | solution.py:23
  53.5 14.8 %collective-permute-start.19 = (bf16[2,128,768]{2,1,0:T(8,128)(2,1)S(1)}, bf16[2,128,768]{2,1,0:T(8,128)(2,1)S(1)}, u32[]{:S(2)}, u32[]{:S(2)}) collective-permute-start(bf16[2,128,768]{2,1,0:T(8,128)(2,1)S(1)} %get-tuple-element.204), channel_id=1, source_target_pairs={{0,8},{8,0},{16,24},{24,16},{1,9},{9,1},{17,25},{25,17},{2,10},{10... | collective-permute-start | bytes 1179656 | tf_op jit(solution)/shard_map/ppermute | solution.py:23
  63.7 13.9 %collective-permute-start.25 = (bf16[1,96,1024]{2,1,0:T(8,128)(2,1)S(1)}, bf16[1,96,1024]{2,1,0:T(8,128)(2,1)S(1)}, u32[]{:S(2)}, u32[]{:S(2)}) collective-permute-start(bf16[1,96,1024]{2,1,0:T(8,128)(2,1)S(1)} %get-tuple-element.256), channel_id=1, source_target_pairs={{0,4},{1,5},{2,6},{3,7},{4,0},{5,1},{6,2},{7,3},{8,12},{9,13},{10,... | collective-permute-start | bytes 589832 | tf_op jit(solution)/shard_map/ppermute | solution.py:23
  65.8 9.7 %collective-permute-start.26 = (bf16[2,96,640]{2,1,0:T(8,128)(2,1)S(1)}, bf16[2,96,640]{2,1,0:T(8,128)(2,1)S(1)}, u32[]{:S(2)}, u32[]{:S(2)}) collective-permute-start(bf16[2,96,640]{2,1,0:T(8,128)(2,1)S(1)} %get-tuple-element.254), channel_id=1, source_target_pairs={{0,2},{1,3},{2,0},{3,1},{4,6},{5,7},{6,4},{7,5},{8,10},{9,11},{10,... | collective-permute-start | bytes 737288 | tf_op jit(solution)/shard_map/ppermute | solution.py:23
  68.5 11.7 %collective-permute-start.21 = (bf16[96,768]{1,0:T(8,128)(2,1)S(1)}, bf16[96,768]{1,0:T(8,128)(2,1)S(1)}, u32[]{:S(2)}, u32[]{:S(2)}) collective-permute-start(bf16[96,768]{1,0:T(8,128)(2,1)S(1)} %fusion.13.refs_0_), channel_id=1, source_target_pairs={{0,8},{8,0},{16,24},{24,16},{1,9},{9,1},{17,25},{25,17},{2,10},{10... | collective-permute-start | bytes 442376 | tf_op jit(solution)/shard_map/ppermute | solution.py:23
  69.8 10.5 %collective-permute-start.22 = (bf16[96,768]{1,0:T(8,128)(2,1)S(1)}, bf16[96,768]{1,0:T(8,128)(2,1)S(1)}, u32[]{:S(2)}, u32[]{:S(2)}) collective-permute-start(bf16[96,768]{1,0:T(8,128)(2,1)S(1)} %fusion.13.refs_0_), channel_id=1, source_target_pairs={{0,16},{8,24},{16,0},{24,8},{1,17},{9,25},{17,1},{25,9},{2,18},{10... | collective-permute-start | bytes 442376 | tf_op jit(solution)/shard_map/ppermute | solution.py:23
  70.6 10.9 %collective-permute-start.23 = (bf16[96,768]{1,0:T(8,128)(2,1)S(1)}, bf16[96,768]{1,0:T(8,128)(2,1)S(1)}, u32[]{:S(2)}, u32[]{:S(2)}) collective-permute-start(bf16[96,768]{1,0:T(8,128)(2,1)S(1)} %fusion.13.refs_0_), channel_id=1, source_target_pairs={{0,24},{8,16},{16,8},{24,0},{1,25},{9,17},{17,9},{25,1},{2,26},{10... | collective-permute-start | bytes 442376 | tf_op jit(solution)/shard_map/ppermute | solution.py:23
  75.5 11.2 %collective-permute-start.27 = (bf16[128,768]{1,0:T(8,128)(2,1)S(1)}, bf16[128,768]{1,0:T(8,128)(2,1)S(1)}, u32[]{:S(2)}, u32[]{:S(2)}) collective-permute-start(bf16[128,768]{1,0:T(8,128)(2,1)S(1)} %fusion.11), channel_id=1, source_target_pairs={{0,16},{8,24},{16,0},{24,8},{1,17},{9,25},{17,1},{25,9},{2,18},{10... | collective-permute-start | bytes 589832 | tf_op jit(solution)/shard_map/ppermute | solution.py:23
  77.6 8.9 %collective-permute-start.28 = (bf16[1,96,640]{2,1,0:T(8,128)(2,1)S(1)}, bf16[1,96,640]{2,1,0:T(8,128)(2,1)S(1)}, u32[]{:S(2)}, u32[]{:S(2)}) collective-permute-start(bf16[1,96,640]{2,1,0:T(8,128)(2,1)S(1)} %get-tuple-element.260), channel_id=1, source_target_pairs={{0,4},{1,5},{2,6},{3,7},{4,0},{5,1},{6,2},{7,3},{8,12},{9,13},{10,... | collective-permute-start | bytes 368648 | tf_op jit(solution)/shard_map/ppermute | solution.py:23
  80.4 12.2 %collective-permute-start.33 = (bf16[96,1024]{1,0:T(8,128)(2,1)S(1)}, bf16[96,1024]{1,0:T(8,128)(2,1)S(1)}, u32[]{:S(2)}, u32[]{:S(2)}) collective-permute-start(bf16[96,1024]{1,0:T(8,128)(2,1)S(1)} %fusion.12.refs_0_), channel_id=1, source_target_pairs={{0,16},{8,24},{16,0},{24,8},{1,17},{9,25},{17,1},{25,9},{2,18},{10... | collective-permute-start | bytes 589832 | tf_op jit(solution)/shard_map/ppermute | solution.py:23
  81.6 11.0 %collective-permute-start.34 = (bf16[96,1024]{1,0:T(8,128)(2,1)S(1)}, bf16[96,1024]{1,0:T(8,128)(2,1)S(1)}, u32[]{:S(2)}, u32[]{:S(2)}) collective-permute-start(bf16[96,1024]{1,0:T(8,128)(2,1)S(1)} %fusion.12.refs_0_), channel_id=1, source_target_pairs={{0,24},{8,16},{16,8},{24,0},{1,25},{9,17},{17,9},{25,1},{2,26},{10... | collective-permute-start | bytes 589832 | tf_op jit(solution)/shard_map/ppermute | solution.py:23
  86.8 8.6 %collective-permute-start.30 = (bf16[96,640]{1,0:T(8,128)(2,1)S(1)}, bf16[96,640]{1,0:T(8,128)(2,1)S(1)}, u32[]{:S(2)}, u32[]{:S(2)}) collective-permute-start(bf16[96,640]{1,0:T(8,128)(2,1)S(1)} %fusion.14.refs_0_), channel_id=1, source_target_pairs={{0,16},{8,24},{16,0},{24,8},{1,17},{9,25},{17,1},{25,9},{2,18},{10... | collective-permute-start | bytes 368648 | tf_op jit(solution)/shard_map/ppermute | solution.py:23
  (25 other events, 214.3 us)

commit v4 on v3

--- a/solution.py
+++ b/solution.py
@@ -69,7 +69,7 @@
 HOPS = {"d": "far", "u": "near", "a": "near"}
 GATHER = {"d": None, "u": None, "a": None}
 DH = (1, 2)
-ORDER = "pq af c1 c2 c3 lo pm fa up dn d0 u0 bw d1 u1 bo a0 h1 d2 a1 u2 d3 d4 ou a2 h2 u3 u4 a3 a4".split()
+ORDER = "pq cs t2 t1 af fs c1 pm c2 c3 lo fa up dn d0 u0 bw ou d1 u1 a0 h1 d2 h2 a1 u2 d3 d4 a2 u3 u4 a3 a4".split()
 
 
 def flat(ref):
@@ -91,23 +91,15 @@
             bit *= 2
         return jnp.concatenate(parts, 1)
 
-    def prep_qkv_kernel(wqkv, pack, wq_o, bq_o, row_o, col_o):
+    def prep_qkv_kernel(wqkv, wq_o):
         D = wqkv.shape[0]
         cs = D // S
-        L = row_o.shape[1]
-        s = lax.axis_index("seq")
-        row = rel_row(pack[4:5, :L], L // S)
-        row_o[...] = jnp.broadcast_to(row, row_o.shape)
-        col_o[...] = jnp.transpose(jnp.broadcast_to(row, (128, L)))
-        bq_o[0:2, :] = pack[0:2, :]
+        s = lax.axis_index("seq")
         for p in range(S):
             @pl.when(s == p)
             def _(p=p):
                 for c in range(3):
                     wq_o[:, c * cs:(c + 1) * cs] = wqkv[:, c * D + p * cs:c * D + (p + 1) * cs]
-                zero = jnp.zeros((1, cs), F32)
-                bq_o[2:3, :] = jnp.concatenate(
-                    [pack[2:3, p * cs:(p + 1) * cs], zero, pack[3:4, p * cs:(p + 1) * cs], zero], 1)
 
     def prep_mlp_kernel(win, wout, wdown, bin_, win_o, wout_o, wdn_o, bin_o):
         D = wout.shape[0]
@@ -128,23 +120,41 @@
                     win_o[:, i * FJ:(i + 1) * FJ] = win[:, at:at + FJ]
                     bin_o[:, i * FJ:(i + 1) * FJ] = vin[:, at:at + FJ]
 
+    def turn_kernel(w, o):
+        rows, cols = w.shape
+        step = min(rows, cols)
+        for i in range(0, rows, step):
+            for j in range(0, cols, step):
+                o[j:j + step, i:i + step] = jnp.transpose(w[i:i + step, j:j + step])
+
     def attn_fwd_kernel(*refs):
-        xs, (row_ref, col_ref, pack, wq_ref, qkv_o, lse_o, attn_o) = refs[:S], refs[S:S + 7]
-        near_o, far_o = refs[S + 7:2 * S + 6], refs[2 * S + 6:]
+        xs, (seg_ref, g_ref, b_ref, bqv, wq_ref) = refs[:S], refs[S:S + 5]
+        qkv_o, lse_o, row_o, col_o, attn_o = refs[S + 5:S + 10]
+        near_o, far_o, bias_s = refs[S + 10:2 * S + 9], refs[2 * S + 9:3 * S + 8], refs[3 * S + 8]
         t, D = xs[0].shape
         L = S * t
         cs = D // S
+        s = lax.axis_index("seq")
+        gain, shift, bias = flat(g_ref), flat(b_ref), flat(bqv)
+        for p in range(S):
+            @pl.when(s == p)
+            def _(p=p):
+                zero = jnp.zeros((1, cs), F32)
+                bias_s[...] = jnp.concatenate(
+                    [bias[:, p * cs:(p + 1) * cs], zero, bias[:, D + p * cs:D + (p + 1) * cs]], 1)
+        row = rel_row(seg_ref[...], t).astype(F32)
+        row_o[...] = jnp.broadcast_to(row, row_o.shape)
+        col_o[...] = jnp.transpose(jnp.broadcast_to(row, (128, L)))
         for k in range(S):
             unit, _ = norm_parts(xs[k][...].astype(F32))
-            h1 = (unit * pack[0:1, :] + pack[1:2, :]).astype(BF)
-            qkv_o[k * t:(k + 1) * t, :] = (dot(h1, wq_ref[...]) + pack[2:3, :3 * cs]).astype(BF)
-        row = row_ref[0:1, :]
+            h1 = (unit * gain + shift).astype(BF)
+            qkv_o[k * t:(k + 1) * t, :] = (dot(h1, wq_ref[...]) + bias_s[...]).astype(BF)
         heads = cs // HEAD_DIM
         outs = [[None] * heads for _ in range(S)]
         def part(c, h, rows=slice(None)):
             return qkv_o[rows, c * cs + h * HEAD_DIM:c * cs + (h + 1) * HEAD_DIM]
         def soft(sc, rows, h):
-            sc = jnp.where(col_ref[rows, :1] == row, sc, -1e30)
+            sc = jnp.where(col_o[rows, :1] == row, sc, -1e30)
             top = jnp.max(sc, axis=-1, keepdims=True)
             ex = jnp.exp(sc - top)
             total = jnp.sum(ex, axis=-1, keepdims=True)
@@ -250,9 +260,9 @@
 
     def local_kernel(*refs):
         x_ref, own, nears, refs = refs[0], refs[1], refs[2:1 + S], refs[1 + S:]
-        cot_ref, wout, bout, g_ref, b_ref, win, bin_ref, wdown = refs[:8]
-        act_o, x1_o, dx1_o, vec_o = refs[8:12]
-        both = refs[12:]
+        cot_ref, wout, bout, g_ref, b_ref, win, bin_ref, win_t, wdown_t = refs[:9]
+        act_o, x1_o, dx1_o, vec_o = refs[9:13]
+        both = refs[13:]
         t, D = x_ref.shape
         FF = win.shape[1]
         cs = D // S
@@ -272,8 +282,8 @@
             cols = slice(c * D, (c + 1) * D)
             act, slope = gelu_both(dot(h2, win[:, cols]) + bias_in[:, cols])
             act_o[:, cols] = act.astype(BF)
-            du = (dot(cot, wdown[cols, :], 1, 1) * slope).astype(BF)
-            dh2 = dh2 + dot(du, win[:, cols], 1, 1)
+            du = (dot(cot, wdown_t[:, cols]) * slope).astype(BF)
+            dh2 = dh2 + dot(du, win_t[cols, :])
         dy = cot.astype(F32)
         dx1 = dy + norm_back(dh2, unit, scale, flat(g_ref))
         dx1_o[...] = dx1
@@ -298,8 +308,8 @@
 
     def attn_bwd_kernel(*refs):
         xs, boths = refs[:S], refs[S:2 * S]
-        row_ref, col_ref, pack, wq, qkv, lse = refs[2 * S:2 * S + 6]
-        own_o, next_o, away_o, keep_o, send_o, h1_s, dqkv_s, gw_s = refs[2 * S + 6:]
+        row_ref, col_ref, g_ref, b_ref, wq, qkv, lse = refs[2 * S:2 * S + 7]
+        own_o, next_o, away_o, keep_o, send_o, h1_s, dqkv_s, gw_s = refs[2 * S + 7:]
         t, D = xs[0].shape
         L = S * t
         cs = D // S
@@ -360,7 +370,7 @@
         for k in range(S):
             rows = slice(k * t, (k + 1) * t)
             unit, _ = norm_parts(xs[k][...].astype(F32))
-            h1_s[rows, :] = (unit * pack[0:1, :] + pack[1:2, :]).astype(BF)
+            h1_s[rows, :] = (unit * flat(g_ref) + flat(b_ref)).astype(BF)
             dh1 = dot(dqkv_s[rows, :], wq[...], 1, 1)
             gg = gg + jnp.sum(dh1 * unit, axis=0, keepdims=True)
             gb = gb + jnp.sum(dh1, axis=0, keepdims=True)
@@ -468,26 +478,28 @@
                 compiler_params=pltpu.CompilerParams(vmem_limit_bytes=limit * MIB))(*args)
 
         def prep_qkv():
-            at = lax.broadcasted_iota(jnp.int32, (8, D), 0)
-            pack1 = jnp.pad(segments.astype(F32), ((0, 0), (0, D - L)))
-            for i, vec in enumerate((ln1_gain, ln1_bias, bias_qv[:D], bias_qv[D:])):
-                pack1 = jnp.where(at == i, vec[None, :], pack1)
-            v["wq"], v["pack1"], v["row"], v["col"] = kernel(
-                prep_qkv_kernel, [sds((D, 3 * cs), BF), sds((8, D), F32), sds((8, L), F32), sds((L, 128), F32)],
-                [w_qkv, pack1], "prep_qkv")
-            cot_late, _ = lax.optimization_barrier((cot_own, v["col"]))
-            v["cots"] = tuple(gather_seq(cot_late, S))
+            v["wq"], = kernel(prep_qkv_kernel, [sds((D, 3 * cs), BF)], [w_qkv], "prep_qkv", us=8)
+            token[0] = v["wq"]
 
         def attn_fwd():
             near, far = sds((t // 2, 2 * cs), BF), sds(((L - t) // 2, 2 * cs), BF)
-            v["qkv"], v["lse"], v["attn"], *sends = kernel(
+            v["qkv"], v["lse"], v["row"], v["col"], v["attn"], *sends = kernel(
                 attn_fwd_kernel,
-                [sds((L, 3 * cs), BF), sds((L, 128), F32), sds((L, cs), BF)] + [near] * (S - 1) + [far] * (S - 1),
-                v["xs"] + wait("row", "col", "pack1", "wq"), "attn_fwd", us=6)
+                [sds((L, 3 * cs), BF), sds((L, 128), F32), sds((8, L), F32), sds((L, 128), F32), sds((L, cs), BF)]
+                + [near] * (S - 1) + [far] * (S - 1),
+                v["xs"] + (segments, ln1_gain, ln1_bias, bias_qv) + wait("wq"), "attn_fwd",
+                [pltpu.VMEM((1, 3 * cs), F32)], us=6)
             v["nears"] = tuple(exchange(sends[m - 1], "seq", S, m) for m in range(1, S))
-            far_sends, _ = lax.optimization_barrier((tuple(sends[S - 1:]), sends[0]))
-            v["fars"] = tuple(exchange(far_sends[m - 1], "seq", S, m) for m in range(1, S))
+            v["far_sends"] = tuple(sends[S - 1:])
             token[0] = v["attn"]
+
+        def cots_send():
+            (cot,) = wait("cot")
+            v["cots"] = tuple(gather_seq(cot, S))
+
+        def fars_send():
+            (sends,) = wait("far_sends")
+            v["fars"] = tuple(exchange(sends[m - 1], "seq", S, m) for m in range(1, S))
 
         def cots(*ks):
             def run():
@@ -499,6 +511,15 @@
                 token[0] = got[ks[-1]]
             return run
 
+        def turn(name, source):
+            def run():
+                w = v[source]
+                if token[0] is not None:
+                    w, _ = lax.optimization_barrier((w, token[0]))
+                v[name], = kernel(turn_kernel, [sds(w.shape[::-1], BF)], [w], name, us=2)
+                token[0] = v[name]
+            return run
+
         def prep_mlp():
             (w,) = wait("w_in")
             v["win_s"], v["wout_s"], v["wdn_s"], v["bin_s"] = kernel(
@@ -512,7 +533,7 @@
                 local_kernel,
                 [sds((t, FF), BF), sds((t, D), F32), sds((t, D), F32), sds((8, D), F32)]
                 + [sds((t, 2 * cs), BF)] * S,
-                (x_own, v["attn"]) + nears + (cot_own, w_out, bias_out, ln2_gain, ln2_bias, w_in, bias_in, w_down),
+                (x_own, v["attn"]) + nears + (cot_own, w_out, bias_out, ln2_gain, ln2_bias, w_in, bias_in, v["win_t"], v["wdown_t"]),
                 "local", limit=20, us=5)
             v["nears"] = nears
             v["boths"] = (both[0],) + tuple(exchange(both[k], "seq", S, k) for k in range(1, S))
@@ -554,7 +575,7 @@
                 attn_bwd_kernel,
                 [sds((t, D), F32), sds((t, D), F32), sds((S - 2, t, D), BF),
                  sds((NB // 2, R, wide_a), BF), sds((NB // 2, R, wide_a), BF)],
-                v["xs"] + boths + (v["row"], v["col"], v["pack1"], v["wq"], qkv, v["lse"]), "attn_bwd",
+                v["xs"] + boths + (v["row"], v["col"], ln1_gain, ln1_bias, v["wq"], qkv, v["lse"]), "attn_bwd",
                 [pltpu.VMEM((L, D), BF), pltpu.VMEM((L, 3 * cs), BF), pltpu.VMEM((NB, R, wide_a), F32)], 32)
             v["a_got"] = exchange(v["a_send"], "batch", NB, 1)
             v["h_got"] = exchange(away, "seq", S, DH[0])
@@ -633,9 +654,9 @@
             token[0] = v["out"]
 
         v["xs"] = tuple(gather_seq(x_own, S))
-        v["w_in"] = w_in
+        v["w_in"], v["w_down"], v["cot"] = w_in, w_down, cot_own
         steps = dict(
-            pq=prep_qkv, af=attn_fwd, c1=cots(1), c2=cots(2), c3=cots(3), fa=fars, pm=prep_mlp, lo=local, up=up, bo=both,
+            pq=prep_qkv, af=attn_fwd, cs=cots_send, fs=fars_send, c1=cots(1), c2=cots(2), c3=cots(3), fa=fars, pm=prep_mlp, t1=turn("wdown_t", "w_down"), t2=turn("win_t", "w_in"), lo=local, up=up, bo=both,
             dn=down, bw=attn_bwd, d0=halve("d", 0), d1=halve("d", 1), d2=halve("d", 2), d3=spread("d"), d4=d_final,
             u0=halve("u", 0), u1=halve("u", 1), u2=halve("u", 2), u3=spread("u"), u4=u_final,
             a0=halve("a", 0), a1=halve("a", 1), a2=halve("a", 2), a3=spread("a"), a4=a_final,

time: 97 us -> 94.7 us (0.976)
  Pallas kernels: 25.5 us -> 27.3 us
  starting transfers between devices: 45.9 us -> 44.3 us
  other arithmetic: 4.01 us -> 2.46 us
  waiting for transfers between devices: 17.4 us -> 16.4 us
    pallas_call x11 -> x13, Pallas kernels: 25.5 us -> 27.3 us  [kernel(): pl.pallas_call(body, out_shape=outs, scratch_shapes=list(scratch), name=n...]
    ppermute x35, starting transfers between devices: 45.9 us -> 44.3 us  [exchange(): return lax.ppermute(value, axis, [(j, j ^ step) for j in range(size)])]
    unnamed x28 -> x30, local copies, waits for them, and re-layouts: 2.06 us -> 3.12 us
    ppermute x35, waiting for transfers between devices: 17.4 us -> 16.4 us  [exchange(): return lax.ppermute(value, axis, [(j, j ^ step) for j in range(size)])]
  transfers between devices with their start and end apart: 35 -> 35, of which waited for: 9 -> 9; matrix products, arithmetic and copies ran while one was open for 5% -> 3% of each run, Pallas kernels for 25% -> 27%
where the time goes in v4:
time: 94.7 us; the launch traced here: 94.5 us
  starting transfers between devices  44.3 us (47%)
  Pallas kernels  27.3 us (29%)
  waiting for transfers between devices  16.4 us (17%)
  local copies, waits for them, and re-layouts  3.12 us (3%)
  other arithmetic  2.46 us (3%)
  between operations  0.99 us (1%)
    ppermute x35, starting transfers between devices, exchange(): return lax.ppermute(value, axis, [(j, j ^ step) for j in range(size)])  44.3 us
    pallas_call x13, Pallas kernels, kernel(): pl.pallas_call(body, out_shape=outs, scratch_shapes=list(scratch), name=n...  27.3 us
    ppermute x35, waiting for transfers between devices, exchange(): return lax.ppermute(value, axis, [(j, j ^ step) for j in range(size)])  16.4 us
    unnamed x30, local copies, waits for them, and re-layouts  3.12 us
  transfers between devices with their start and end apart: 35, of which 9 were waited for; matrix products, arithmetic and copies ran while one was open for 3% of the time, Pallas kernels for 27%

profile of v4, /device:TPU:0, one launch (start us, length us, event | category | flops | bytes accessed | tf_op | source)
XLA Modules:
  0.0 94.5 jit_solution(6050229496357576854)
XLA Ops:
  0.7 3.0 %collective-permute-start = (bf16[128,768]{1,0:T(8,128)(2,1)}, bf16[128,768]{1,0:T(8,128)(2,1)S(1)}, u32[]{:S(2)}, u32[]{:S(2)}) collective-permute-start(bf16[128,768]{1,0:T(8,128)(2,1)} %bitcast.21), channel_id=1, source_target_pairs={{0,8},{8,0},{16,24},{24,16},{1,9},{9,1},{17,25},{25,17},{2,10},{10... | collective-permute-start | bytes 589832 | tf_op jit(solution)/shard_map/ppermute | solution.py:23
  3.7 1.5 %collective-permute-start.1 = (bf16[128,768]{1,0:T(8,128)(2,1)}, bf16[128,768]{1,0:T(8,128)(2,1)S(1)}, u32[]{:S(2)}, u32[]{:S(2)}) collective-permute-start(bf16[128,768]{1,0:T(8,128)(2,1)} %bitcast.22), channel_id=1, source_target_pairs={{0,16},{8,24},{16,0},{24,8},{1,17},{9,25},{17,1},{25,9},{2,18},{10... | collective-permute-start | bytes 589832 | tf_op jit(solution)/shard_map/ppermute | solution.py:23
  5.2 2.0 %copy-done.11 = bf16[768,2304]{1,0:T(8,128)(2,1)S(1)} copy-done((bf16[768,2304]{1,0:T(8,128)(2,1)S(1)}, bf16[768,2304]{1,0:T(8,128)(2,1)}, u32[]{:S(2)}) %copy-start.11) | copy-done | bytes 3538968
  7.4 2.1 %collective-permute-start.8 = (bf16[128,768]{1,0:T(8,128)(2,1)S(1)}, bf16[128,768]{1,0:T(8,128)(2,1)S(1)}, u32[]{:S(2)}, u32[]{:S(2)}) collective-permute-start(bf16[128,768]{1,0:T(8,128)(2,1)S(1)} %bitcast.28), channel_id=1, source_target_pairs={{0,8},{8,0},{16,24},{24,16},{1,9},{9,1},{17,25},{25,17},{2,10},{10... | collective-permute-start | bytes 589832 | tf_op jit(solution)/shard_map/ppermute | solution.py:23
  9.5 1.5 %collective-permute-start.7 = (bf16[128,768]{1,0:T(8,128)(2,1)S(1)}, bf16[128,768]{1,0:T(8,128)(2,1)S(1)}, u32[]{:S(2)}, u32[]{:S(2)}) collective-permute-start(bf16[128,768]{1,0:T(8,128)(2,1)S(1)} %bitcast.29), channel_id=1, source_target_pairs={{0,16},{8,24},{16,0},{24,8},{1,17},{9,25},{17,1},{25,9},{2,18},{10... | collective-permute-start | bytes 589832 | tf_op jit(solution)/shard_map/ppermute | solution.py:23
  16.3 3.0 %attn_fwd.1 = (bf16[512,576]{1,0:T(8,128)(2,1)S(1)}, f32[512,128]{1,0:T(8,128)S(1)}, f32[8,512]{1,0:T(8,128)S(1)}, f32[512,128]{1,0:T(8,128)S(1)}, bf16[512,192]...) custom-call(bf16[128,768]{1,0:T(8,128)(2,1)S(1)} %bitcast.24, ...), custom_call_target="tpu_custom_call" | custom-call | flops 6000000000 | bytes 12000000 | tf_op jit(solution)/shard_map/attn_fwd/pallas_call | solution.py:475
  20.1 1.6 %collective-permute-start.4 = (bf16[64,384]{1,0:T(8,128)(2,1)S(1)}, bf16[64,384]{1,0:T(8,128)(2,1)S(1)}, u32[]{:S(2)}, u32[]{:S(2)}) collective-permute-start(bf16[64,384]{1,0:T(8,128)(2,1)S(1)} %get-tuple-element.136), channel_id=1, source_target_pairs={{0,16},{8,24},{16,0},{24,8},{1,17},{9,25},{17,1},{25,9},{2,18},{10... | collective-permute-start | bytes 147464 | tf_op jit(solution)/shard_map/ppermute | solution.py:23
  27.6 4.0 %local.1 = (bf16[128,3072]{1,0:T(8,128)(2,1)S(1)}, f32[128,768]{1,0:T(8,128)S(1)}, f32[128,768]{1,0:T(8,128)S(1)}, f32[8,768]{1,0:T(8,128)S(1)}, bf16[128,384]{1...) custom-call(bf16[128,768]{1,0:T(8,128)(2,1)S(1)} %bitcast.25, ...), custom_call_target="tpu_custom_call" | custom-call | flops 5000000000 | bytes 10000000 | tf_op jit(solution)/shard_map/local/pallas_call | solution.py:475
  31.6 1.5 %collective-permute-start.10 = (bf16[128,384]{1,0:T(8,128)(2,1)S(1)}, bf16[128,384]{1,0:T(8,128)(2,1)S(1)}, u32[]{:S(2)}, u32[]{:S(2)}) collective-permute-start(bf16[128,384]{1,0:T(8,128)(2,1)S(1)} %get-tuple-element.151), channel_id=1, source_target_pairs={{0,16},{8,24},{16,0},{24,8},{1,17},{9,25},{17,1},{25,9},{2,18},{10... | collective-permute-start | bytes 294920 | tf_op jit(solution)/shard_map/ppermute | solution.py:23
  35.3 3.6 %up.1 = (bf16[512,768]{1,0:T(8,128)(2,1)S(1)}, bf16[512,768]{1,0:T(8,128)(2,1)S(1)}, f32[512,768]{1,0:T(8,128)S(1)}, bf16[4,96,768]{2,1,0:T(8,128)(2,1)S(1)}, bf16[4,96,768]{2,1,0:T(8,128)(2,1)S(1)}) custom-call(bf16[128,768]{1,0:T(8,128)(2,1)S(1)} %bitcast.26, bf16[128,768]{1,0:T(8,128)(2,1)S(1)} %collective-permute-done.refs_1_, ...), custom_call_target="tpu_custom_call" | custom-call | flops 1000000000 | bytes 2000000 | tf_op jit(solution)/shard_map/up/pallas_call | solution.py:475
  39.0 1.9 %down.1 = (bf16[4,96,1024]{2,1,0:T(8,128)(2,1)S(1)}, bf16[4,96,1024]{2,1,0:T(8,128)(2,1)S(1)}) custom-call(bf16[128,768]{1,0:T(8,128)(2,1)S(1)} %bitcast.33, bf16[128,768]{1,0:T(8,128)(2,1)S(1)} %collective-permute-done.8.refs_12_.refs_1_, bf16[128,768]{1,0:T(8,128)(2,1)S(1)} %collective-permute-done.7.refs_13_.refs_2_, ...), custom_call_target="tpu_custom_call" | custom-call | flops 1000000000 | bytes 2000000 | tf_op jit(solution)/shard_map/down/pallas_call | solution.py:475
  41.9 2.7 %collective-permute-start.20 = (bf16[2,96,768]{2,1,0:T(8,128)(2,1)S(1)}, bf16[2,96,768]{2,1,0:T(8,128)(2,1)S(1)}, u32[]{:S(2)}, u32[]{:S(2)}) collective-permute-start(bf16[2,96,768]{2,1,0:T(8,128)(2,1)S(1)} %get-tuple-element.254), channel_id=1, source_target_pairs={{0,4},{1,5},{2,6},{3,7},{4,0},{5,1},{6,2},{7,3},{8,12},{9,13},{10,... | collective-permute-start | bytes 884744 | tf_op jit(solution)/shard_map/ppermute | solution.py:23
  44.8 1.6 %collective-permute-start.19 = (bf16[2,96,1024]{2,1,0:T(8,128)(2,1)S(1)}, bf16[2,96,1024]{2,1,0:T(8,128)(2,1)S(1)}, u32[]{:S(2)}, u32[]{:S(2)}) collective-permute-start(bf16[2,96,1024]{2,1,0:T(8,128)(2,1)S(1)} %get-tuple-element.252), channel_id=1, source_target_pairs={{0,2},{1,3},{2,0},{3,1},{4,6},{5,7},{6,4},{7,5},{8,10},{9,11},{10,... | collective-permute-start | bytes 1179656 | tf_op jit(solution)/shard_map/ppermute | solution.py:23
  46.4 5.2 %attn_bwd.1 = (f32[128,768]{1,0:T(8,128)S(1)}, f32[128,768]{1,0:T(8,128)S(1)}, bf16[2,128,768]{2,1,0:T(8,128)(2,1)S(1)}, bf16[4,96,640]{2,1,0:T(8,128)(2,1)S(1)}, bf16[4,96,640]{2,1,0:T(8,128)(2,1)S(1)}) custom-call(bf16[128,768]{1,0:T(8,128)(2,1)S(1)} %bitcast.27, bf16[128,768]{1,0:T(8,128)(2,1)S(1)} %collective-permute-done.refs_1_, ...), custom_call_target="tpu_custom_call" | custom-call | flops 1000000000 | bytes 2000000 | tf_op jit(solution)/shard_map/attn_bwd/pallas_call | solution.py:475
  54.5 3.7 %collective-permute-done.20 = bf16[2,96,768]{2,1,0:T(8,128)(2,1)S(1)} collective-permute-done((bf16[2,96,768]{2,1,0:T(8,128)(2,1)S(1)}, bf16[2,96,768]{2,1,0:T(8,128)(2,1)S(1)}, u32[]{:S(2)}, u32[]{:S(2)}) %collective-permute-start.20) | collective-permute-done | bytes 294944 | tf_op jit(solution)/shard_map/ppermute | solution.py:23
  58.9 2.6 %collective-permute-done.19 = bf16[2,96,1024]{2,1,0:T(8,128)(2,1)S(1)} collective-permute-done((bf16[2,96,1024]{2,1,0:T(8,128)(2,1)S(1)}, bf16[2,96,1024]{2,1,0:T(8,128)(2,1)S(1)}, u32[]{:S(2)}, u32[]{:S(2)}) %collective-permute-start.19) | collective-permute-done | bytes 393248 | tf_op jit(solution)/shard_map/ppermute | solution.py:23
  61.7 2.1 %collective-permute-start.28 = (bf16[1,96,1024]{2,1,0:T(8,128)(2,1)S(1)}, bf16[1,96,1024]{2,1,0:T(8,128)(2,1)S(1)}, u32[]{:S(2)}, u32[]{:S(2)}) collective-permute-start(bf16[1,96,1024]{2,1,0:T(8,128)(2,1)S(1)} %get-tuple-element.258), channel_id=1, source_target_pairs={{0,4},{1,5},{2,6},{3,7},{4,0},{5,1},{6,2},{7,3},{8,12},{9,13},{10,... | collective-permute-start | bytes 589832 | tf_op jit(solution)/shard_map/ppermute | solution.py:23
  63.9 2.5 %collective-permute-start.23 = (bf16[2,96,640]{2,1,0:T(8,128)(2,1)S(1)}, bf16[2,96,640]{2,1,0:T(8,128)(2,1)S(1)}, u32[]{:S(2)}, u32[]{:S(2)}) collective-permute-start(bf16[2,96,640]{2,1,0:T(8,128)(2,1)S(1)} %get-tuple-element.256), channel_id=1, source_target_pairs={{0,2},{1,3},{2,0},{3,1},{4,6},{5,7},{6,4},{7,5},{8,10},{9,11},{10,... | collective-permute-start | bytes 737288 | tf_op jit(solution)/shard_map/ppermute | solution.py:23
  69.9 3.5 %collective-permute-done.21 = bf16[128,768]{1,0:T(8,128)(2,1)S(1)} collective-permute-done((bf16[128,768]{1,0:T(8,128)(2,1)S(1)}, bf16[128,768]{1,0:T(8,128)(2,1)S(1)}, u32[]{:S(2)}, u32[]{:S(2)}) %collective-permute-start.21) | collective-permute-done | bytes 196640 | tf_op jit(solution)/shard_map/ppermute | solution.py:23
  73.4 1.7 %collective-permute-start.27 = (bf16[96,768]{1,0:T(8,128)(2,1)S(1)}, bf16[96,768]{1,0:T(8,128)(2,1)S(1)}, u32[]{:S(2)}, u32[]{:S(2)}) collective-permute-start(bf16[96,768]{1,0:T(8,128)(2,1)S(1)} %fusion.13.refs_0_), channel_id=1, source_target_pairs={{0,24},{8,16},{16,8},{24,0},{1,25},{9,17},{17,9},{25,1},{2,26},{10... | collective-permute-start | bytes 442376 | tf_op jit(solution)/shard_map/ppermute | solution.py:23
  78.7 1.7 %collective-permute-start.34 = (bf16[96,1024]{1,0:T(8,128)(2,1)S(1)}, bf16[96,1024]{1,0:T(8,128)(2,1)S(1)}, u32[]{:S(2)}, u32[]{:S(2)}) collective-permute-start(bf16[96,1024]{1,0:T(8,128)(2,1)S(1)} %fusion.12.refs_0_), channel_id=1, source_target_pairs={{0,24},{8,16},{16,8},{24,0},{1,25},{9,17},{17,9},{25,1},{2,26},{10... | collective-permute-start | bytes 589832 | tf_op jit(solution)/shard_map/ppermute | solution.py:23
  85.2 1.6 %collective-permute-start.31 = (bf16[96,640]{1,0:T(8,128)(2,1)S(1)}, bf16[96,640]{1,0:T(8,128)(2,1)S(1)}, u32[]{:S(2)}, u32[]{:S(2)}) collective-permute-start(bf16[96,640]{1,0:T(8,128)(2,1)S(1)} %fusion.14.refs_0_), channel_id=1, source_target_pairs={{0,24},{8,16},{16,8},{24,0},{1,25},{9,17},{17,9},{25,1},{2,26},{10... | collective-permute-start | bytes 368648 | tf_op jit(solution)/shard_map/ppermute | solution.py:23
  86.8 2.3 %collective-permute-done.33.refs_2_ = bf16[96,1024]{1,0:T(8,128)(2,1)S(1)} collective-permute-done((bf16[96,1024]{1,0:T(8,128)(2,1)S(1)}, bf16[96,1024]{1,0:T(8,128)(2,1)S(1)}, u32[]{:S(2)}, u32[]{:S(2)}) %collective-permute-start.33) | collective-permute-done | bytes 196640 | tf_op jit(solution)/shard_map/ppermute | solution.py:23
  89.6 1.7 %up_final.1 = (f32[96,3072]{1,0:T(8,128)}, f32[96,768]{1,0:T(8,128)}, f32[96]{0:T(128)}, f32[96]{0:T(128)}, f32[96]{0:T(128)}, /*index=5*/f32[96]{0:T(128)}, f32[384]{0:T(512)}) custom-call(bf16[96,1024]{1,0:T(8,128)(2,1)S(1)} %fusion.12.refs_0_, bf16[96,1024]{1,0:T(8,128)(2,1)S(1)} %collective-permute-done.32.refs_1_, ...), custom_call_target="tpu_custom_call" | custom-call | flops 1000000000 | bytes 2000000 | tf_op jit(solution)/shard_map/up_final/pallas_call | solution.py:475
  (106 shorter events, 34.7 us)
Async XLA Ops:
  0.7 14.1 %collective-permute-start = (bf16[128,768]{1,0:T(8,128)(2,1)}, bf16[128,768]{1,0:T(8,128)(2,1)S(1)}, u32[]{:S(2)}, u32[]{:S(2)}) collective-permute-start(bf16[128,768]{1,0:T(8,128)(2,1)} %bitcast.21), channel_id=1, source_target_pairs={{0,8},{8,0},{16,24},{24,16},{1,9},{9,1},{17,25},{25,17},{2,10},{10... | collective-permute-start | bytes 589832 | tf_op jit(solution)/shard_map/ppermute | solution.py:23
  3.7 12.6 %collective-permute-start.1 = (bf16[128,768]{1,0:T(8,128)(2,1)}, bf16[128,768]{1,0:T(8,128)(2,1)S(1)}, u32[]{:S(2)}, u32[]{:S(2)}) collective-permute-start(bf16[128,768]{1,0:T(8,128)(2,1)} %bitcast.22), channel_id=1, source_target_pairs={{0,16},{8,24},{16,0},{24,8},{1,17},{9,25},{17,1},{25,9},{2,18},{10... | collective-permute-start | bytes 589832 | tf_op jit(solution)/shard_map/ppermute | solution.py:23
  5.2 11.1 %collective-permute-start.2 = (bf16[128,768]{1,0:T(8,128)(2,1)}, bf16[128,768]{1,0:T(8,128)(2,1)S(1)}, u32[]{:S(2)}, u32[]{:S(2)}) collective-permute-start(bf16[128,768]{1,0:T(8,128)(2,1)} %bitcast.23), channel_id=1, source_target_pairs={{0,24},{8,16},{16,8},{24,0},{1,25},{9,17},{17,9},{25,1},{2,26},{10... | collective-permute-start | bytes 589832 | tf_op jit(solution)/shard_map/ppermute | solution.py:23
  7.4 12.0 %collective-permute-start.8 = (bf16[128,768]{1,0:T(8,128)(2,1)S(1)}, bf16[128,768]{1,0:T(8,128)(2,1)S(1)}, u32[]{:S(2)}, u32[]{:S(2)}) collective-permute-start(bf16[128,768]{1,0:T(8,128)(2,1)S(1)} %bitcast.28), channel_id=1, source_target_pairs={{0,8},{8,0},{16,24},{24,16},{1,9},{9,1},{17,25},{25,17},{2,10},{10... | collective-permute-start | bytes 589832 | tf_op jit(solution)/shard_map/ppermute | solution.py:23
  9.5 14.4 %collective-permute-start.7 = (bf16[128,768]{1,0:T(8,128)(2,1)S(1)}, bf16[128,768]{1,0:T(8,128)(2,1)S(1)}, u32[]{:S(2)}, u32[]{:S(2)}) collective-permute-start(bf16[128,768]{1,0:T(8,128)(2,1)S(1)} %bitcast.29), channel_id=1, source_target_pairs={{0,16},{8,24},{16,0},{24,8},{1,17},{9,25},{17,1},{25,9},{2,18},{10... | collective-permute-start | bytes 589832 | tf_op jit(solution)/shard_map/ppermute | solution.py:23
  14.8 9.2 %collective-permute-start.6 = (bf16[128,768]{1,0:T(8,128)(2,1)S(1)}, bf16[128,768]{1,0:T(8,128)(2,1)S(1)}, u32[]{:S(2)}, u32[]{:S(2)}) collective-permute-start(bf16[128,768]{1,0:T(8,128)(2,1)S(1)} %bitcast.30), channel_id=1, source_target_pairs={{0,24},{8,16},{16,8},{24,0},{1,25},{9,17},{17,9},{25,1},{2,26},{10... | collective-permute-start | bytes 589832 | tf_op jit(solution)/shard_map/ppermute | solution.py:23
  24.0 10.3 %collective-permute-start.12 = (bf16[192,384]{1,0:T(8,128)(2,1)S(1)}, bf16[192,384]{1,0:T(8,128)(2,1)S(1)}, u32[]{:S(2)}, u32[]{:S(2)}) collective-permute-start(bf16[192,384]{1,0:T(8,128)(2,1)S(1)} %get-tuple-element.157), channel_id=1, source_target_pairs={{0,8},{8,0},{16,24},{24,16},{1,9},{9,1},{17,25},{25,17},{2,10},{10... | collective-permute-start | bytes 442376 | tf_op jit(solution)/shard_map/ppermute | solution.py:23
  25.2 10.0 %collective-permute-start.13 = (bf16[192,384]{1,0:T(8,128)(2,1)S(1)}, bf16[192,384]{1,0:T(8,128)(2,1)S(1)}, u32[]{:S(2)}, u32[]{:S(2)}) collective-permute-start(bf16[192,384]{1,0:T(8,128)(2,1)S(1)} %get-tuple-element.158), channel_id=1, source_target_pairs={{0,16},{8,24},{16,0},{24,8},{1,17},{9,25},{17,1},{25,9},{2,18},{10... | collective-permute-start | bytes 442376 | tf_op jit(solution)/shard_map/ppermute | solution.py:23
  26.3 9.0 %collective-permute-start.14 = (bf16[192,384]{1,0:T(8,128)(2,1)S(1)}, bf16[192,384]{1,0:T(8,128)(2,1)S(1)}, u32[]{:S(2)}, u32[]{:S(2)}) collective-permute-start(bf16[192,384]{1,0:T(8,128)(2,1)S(1)} %get-tuple-element.159), channel_id=1, source_target_pairs={{0,24},{8,16},{16,8},{24,0},{1,25},{9,17},{17,9},{25,1},{2,26},{10... | collective-permute-start | bytes 442376 | tf_op jit(solution)/shard_map/ppermute | solution.py:23
  41.9 16.3 %collective-permute-start.20 = (bf16[2,96,768]{2,1,0:T(8,128)(2,1)S(1)}, bf16[2,96,768]{2,1,0:T(8,128)(2,1)S(1)}, u32[]{:S(2)}, u32[]{:S(2)}) collective-permute-start(bf16[2,96,768]{2,1,0:T(8,128)(2,1)S(1)} %get-tuple-element.254), channel_id=1, source_target_pairs={{0,4},{1,5},{2,6},{3,7},{4,0},{5,1},{6,2},{7,3},{8,12},{9,13},{10,... | collective-permute-start | bytes 884744 | tf_op jit(solution)/shard_map/ppermute | solution.py:23
  44.8 16.8 %collective-permute-start.19 = (bf16[2,96,1024]{2,1,0:T(8,128)(2,1)S(1)}, bf16[2,96,1024]{2,1,0:T(8,128)(2,1)S(1)}, u32[]{:S(2)}, u32[]{:S(2)}) collective-permute-start(bf16[2,96,1024]{2,1,0:T(8,128)(2,1)S(1)} %get-tuple-element.252), channel_id=1, source_target_pairs={{0,2},{1,3},{2,0},{3,1},{4,6},{5,7},{6,4},{7,5},{8,10},{9,11},{10,... | collective-permute-start | bytes 1179656 | tf_op jit(solution)/shard_map/ppermute | solution.py:23
  51.7 12.1 %collective-permute-start.18 = (bf16[4,96,640]{2,1,0:T(8,128)(2,1)S(1)}, bf16[4,96,640]{2,1,0:T(8,128)(2,1)S(1)}, u32[]{:S(2)}, u32[]{:S(2)}) collective-permute-start(bf16[4,96,640]{2,1,0:T(8,128)(2,1)S(1)} %get-tuple-element.207), channel_id=1, source_target_pairs={{0,1},{1,0},{2,3},{3,2},{4,5},{5,4},{6,7},{7,6},{8,9},{9,8},{10,11... | collective-permute-start | bytes 1474568 | tf_op jit(solution)/shard_map/ppermute | solution.py:23
  51.8 14.7 %collective-permute-start.17 = (bf16[2,128,768]{2,1,0:T(8,128)(2,1)S(1)}, bf16[2,128,768]{2,1,0:T(8,128)(2,1)S(1)}, u32[]{:S(2)}, u32[]{:S(2)}) collective-permute-start(bf16[2,128,768]{2,1,0:T(8,128)(2,1)S(1)} %get-tuple-element.206), channel_id=1, source_target_pairs={{0,8},{8,0},{16,24},{24,16},{1,9},{9,1},{17,25},{25,17},{2,10},{10... | collective-permute-start | bytes 1179656 | tf_op jit(solution)/shard_map/ppermute | solution.py:23
  58.3 9.7 %collective-permute-start.22 = (bf16[1,96,768]{2,1,0:T(8,128)(2,1)S(1)}, bf16[1,96,768]{2,1,0:T(8,128)(2,1)S(1)}, u32[]{:S(2)}, u32[]{:S(2)}) collective-permute-start(bf16[1,96,768]{2,1,0:T(8,128)(2,1)S(1)} %get-tuple-element.260), channel_id=1, source_target_pairs={{0,2},{1,3},{2,0},{3,1},{4,6},{5,7},{6,4},{7,5},{8,10},{9,11},{10,... | collective-permute-start | bytes 442376 | tf_op jit(solution)/shard_map/ppermute | solution.py:23
  61.7 15.0 %collective-permute-start.28 = (bf16[1,96,1024]{2,1,0:T(8,128)(2,1)S(1)}, bf16[1,96,1024]{2,1,0:T(8,128)(2,1)S(1)}, u32[]{:S(2)}, u32[]{:S(2)}) collective-permute-start(bf16[1,96,1024]{2,1,0:T(8,128)(2,1)S(1)} %get-tuple-element.258), channel_id=1, source_target_pairs={{0,4},{1,5},{2,6},{3,7},{4,0},{5,1},{6,2},{7,3},{8,12},{9,13},{10,... | collective-permute-start | bytes 589832 | tf_op jit(solution)/shard_map/ppermute | solution.py:23
  63.9 12.4 %collective-permute-start.23 = (bf16[2,96,640]{2,1,0:T(8,128)(2,1)S(1)}, bf16[2,96,640]{2,1,0:T(8,128)(2,1)S(1)}, u32[]{:S(2)}, u32[]{:S(2)}) collective-permute-start(bf16[2,96,640]{2,1,0:T(8,128)(2,1)S(1)} %get-tuple-element.256), channel_id=1, source_target_pairs={{0,2},{1,3},{2,0},{3,1},{4,6},{5,7},{6,4},{7,5},{8,10},{9,11},{10,... | collective-permute-start | bytes 737288 | tf_op jit(solution)/shard_map/ppermute | solution.py:23
  68.1 10.0 %collective-permute-start.25 = (bf16[96,768]{1,0:T(8,128)(2,1)S(1)}, bf16[96,768]{1,0:T(8,128)(2,1)S(1)}, u32[]{:S(2)}, u32[]{:S(2)}) collective-permute-start(bf16[96,768]{1,0:T(8,128)(2,1)S(1)} %fusion.13.refs_0_), channel_id=1, source_target_pairs={{0,8},{8,0},{16,24},{24,16},{1,9},{9,1},{17,25},{25,17},{2,10},{10... | collective-permute-start | bytes 442376 | tf_op jit(solution)/shard_map/ppermute | solution.py:23
  68.9 9.7 %collective-permute-start.26 = (bf16[96,768]{1,0:T(8,128)(2,1)S(1)}, bf16[96,768]{1,0:T(8,128)(2,1)S(1)}, u32[]{:S(2)}, u32[]{:S(2)}) collective-permute-start(bf16[96,768]{1,0:T(8,128)(2,1)S(1)} %fusion.13.refs_0_), channel_id=1, source_target_pairs={{0,16},{8,24},{16,0},{24,8},{1,17},{9,25},{17,1},{25,9},{2,18},{10... | collective-permute-start | bytes 442376 | tf_op jit(solution)/shard_map/ppermute | solution.py:23
  73.4 7.6 %collective-permute-start.27 = (bf16[96,768]{1,0:T(8,128)(2,1)S(1)}, bf16[96,768]{1,0:T(8,128)(2,1)S(1)}, u32[]{:S(2)}, u32[]{:S(2)}) collective-permute-start(bf16[96,768]{1,0:T(8,128)(2,1)S(1)} %fusion.13.refs_0_), channel_id=1, source_target_pairs={{0,24},{8,16},{16,8},{24,0},{1,25},{9,17},{17,9},{25,1},{2,26},{10... | collective-permute-start | bytes 442376 | tf_op jit(solution)/shard_map/ppermute | solution.py:23
  76.8 8.4 %collective-permute-start.32 = (bf16[96,1024]{1,0:T(8,128)(2,1)S(1)}, bf16[96,1024]{1,0:T(8,128)(2,1)S(1)}, u32[]{:S(2)}, u32[]{:S(2)}) collective-permute-start(bf16[96,1024]{1,0:T(8,128)(2,1)S(1)} %fusion.12.refs_0_), channel_id=1, source_target_pairs={{0,8},{8,0},{16,24},{24,16},{1,9},{9,1},{17,25},{25,17},{2,10},{10... | collective-permute-start | bytes 589832 | tf_op jit(solution)/shard_map/ppermute | solution.py:23
  78.1 11.1 %collective-permute-start.33 = (bf16[96,1024]{1,0:T(8,128)(2,1)S(1)}, bf16[96,1024]{1,0:T(8,128)(2,1)S(1)}, u32[]{:S(2)}, u32[]{:S(2)}) collective-permute-start(bf16[96,1024]{1,0:T(8,128)(2,1)S(1)} %fusion.12.refs_0_), channel_id=1, source_target_pairs={{0,16},{8,24},{16,0},{24,8},{1,17},{9,25},{17,1},{25,9},{2,18},{10... | collective-permute-start | bytes 589832 | tf_op jit(solution)/shard_map/ppermute | solution.py:23
  78.7 10.9 %collective-permute-start.34 = (bf16[96,1024]{1,0:T(8,128)(2,1)S(1)}, bf16[96,1024]{1,0:T(8,128)(2,1)S(1)}, u32[]{:S(2)}, u32[]{:S(2)}) collective-permute-start(bf16[96,1024]{1,0:T(8,128)(2,1)S(1)} %fusion.12.refs_0_), channel_id=1, source_target_pairs={{0,24},{8,16},{16,8},{24,0},{1,25},{9,17},{17,9},{25,1},{2,26},{10... | collective-permute-start | bytes 589832 | tf_op jit(solution)/shard_map/ppermute | solution.py:23
  83.3 8.0 %collective-permute-start.29 = (bf16[96,640]{1,0:T(8,128)(2,1)S(1)}, bf16[96,640]{1,0:T(8,128)(2,1)S(1)}, u32[]{:S(2)}, u32[]{:S(2)}) collective-permute-start(bf16[96,640]{1,0:T(8,128)(2,1)S(1)} %fusion.14.refs_0_), channel_id=1, source_target_pairs={{0,8},{8,0},{16,24},{24,16},{1,9},{9,1},{17,25},{25,17},{2,10},{10... | collective-permute-start | bytes 368648 | tf_op jit(solution)/shard_map/ppermute | solution.py:23
  85.2 8.0 %collective-permute-start.31 = (bf16[96,640]{1,0:T(8,128)(2,1)S(1)}, bf16[96,640]{1,0:T(8,128)(2,1)S(1)}, u32[]{:S(2)}, u32[]{:S(2)}) collective-permute-start(bf16[96,640]{1,0:T(8,128)(2,1)S(1)} %fusion.14.refs_0_), channel_id=1, source_target_pairs={{0,24},{8,16},{16,8},{24,0},{1,25},{9,17},{17,9},{25,1},{2,26},{10... | collective-permute-start | bytes 368648 | tf_op jit(solution)/shard_map/ppermute | solution.py:23
  (26 other events, 135.8 us)

commit v5 on v4

--- a/solution.py
+++ b/solution.py
@@ -414,12 +414,12 @@
         NF = NB * FJ
         s = lax.axis_index("seq")
         for k, block in order_of(zip(parts, ks)):
-            scr[s ^ k] = block.astype(F32)
+            scr[s ^ k] = block
         for i in range(NB):
             win_o[:, i * S * FJ:(i + 1) * S * FJ] = jnp.concatenate(
-                [scr[p, :, i * FJ:(i + 1) * FJ] for p in range(S)], 1)
-        wo_o[...] = jnp.concatenate([scr[p, :, NF:NF + cs] for p in range(S)], 1)
-        vecs = [as_rows(scr[p, :, NF + cs:]) for p in range(S)]
+                [scr[p, :, i * FJ:(i + 1) * FJ] for p in range(S)], 1).astype(F32)
+        wo_o[...] = jnp.concatenate([scr[p, :, NF:NF + cs] for p in range(S)], 1).astype(F32)
+        vecs = [as_rows(scr[p, :, NF + cs:].astype(F32)) for p in range(S)]
         total = sum(vecs[1:], vecs[0])
         for i, o in enumerate((bo_o, g2_o, b2_o, bd_o)):
             o[...] = total[i:i + 1, :].reshape(R)
@@ -439,11 +439,12 @@
         cs = D // S
         s = lax.axis_index("seq")
         for k, block in order_of(zip(parts, ks)):
-            scr[s ^ k] = block.astype(F32)
+            scr[s ^ k] = block
         for c in range(3):
             wq_o[:, c * D:(c + 1) * D] = jnp.concatenate(
-                [scr[p, :, c * cs:(c + 1) * cs] for p in range(S)], 1)
-        total = as_rows(sum([scr[p, :, 3 * cs:] for p in range(1, S)], scr[0, :, 3 * cs:]))
+                [scr[p, :, c * cs:(c + 1) * cs] for p in range(S)], 1).astype(F32)
+        tails = [scr[p, :, 3 * cs:].astype(F32) for p in range(S)]
+        total = as_rows(sum(tails[1:], tails[0]))
         g1_o[...] = total[0:1, :].reshape(R)
         b1_o[...] = total[1:2, :].reshape(R)
         bqv_o[...] = jnp.concatenate([total[2:3, :], total[3:4, :]], 1).reshape(2 * R)
@@ -623,7 +624,7 @@
             v["o_u"] = kernel(
                 functools.partial(up_final_kernel, v["u_ks"]),
                 [sds((R, FF), F32), sds((R, D), F32)] + [vec_out] * 4 + [sds((S * FJ,), F32)],
-                parts, "up_final", [pltpu.VMEM((S, R, wide_u), F32)])
+                parts, "up_final", [pltpu.VMEM((S, R, wide_u), BF)])
             token[0] = v["o_u"][0]
 
         def a_final():
@@ -631,7 +632,7 @@
             v["o_a"] = kernel(
                 functools.partial(att_final_kernel, v["a_ks"]),
                 [sds((R, 3 * D), F32), vec_out, vec_out, sds((2 * R,), F32)],
-                parts, "att_final", [pltpu.VMEM((S, R, wide_a), F32)])
+                parts, "att_final", [pltpu.VMEM((S, R, wide_a), BF)])
             token[0] = v["o_a"][0]
 
         def h_first():

time: 94.7 us -> 94.6 us (level)
  no operation moved by 1% of the time
where the time goes in v5:
time: 94.6 us; the launch traced here: 94.4 us
  starting transfers between devices  44.3 us (47%)
  Pallas kernels  26.9 us (28%)
  waiting for transfers between devices  16.6 us (18%)
  local copies, waits for them, and re-layouts  3.12 us (3%)
  other arithmetic  2.46 us (3%)
  between operations  0.99 us (1%)
    ppermute x35, starting transfers between devices, exchange(): return lax.ppermute(value, axis, [(j, j ^ step) for j in range(size)])  44.3 us
    pallas_call x13, Pallas kernels, kernel(): pl.pallas_call(body, out_shape=outs, scratch_shapes=list(scratch), name=n...  26.9 us
    ppermute x35, waiting for transfers between devices, exchange(): return lax.ppermute(value, axis, [(j, j ^ step) for j in range(size)])  16.6 us
    unnamed x30, local copies, waits for them, and re-layouts  3.12 us
  transfers between devices with their start and end apart: 35, of which 9 were waited for; matrix products, arithmetic and copies ran while one was open for 3% of the time, Pallas kernels for 27%

profile of v5, /device:TPU:0, one launch (start us, length us, event | category | flops | bytes accessed | tf_op | source)
XLA Modules:
  0.0 94.4 jit_solution(14892670898827444377)
XLA Ops:
  0.7 3.0 %collective-permute-start = (bf16[128,768]{1,0:T(8,128)(2,1)}, bf16[128,768]{1,0:T(8,128)(2,1)S(1)}, u32[]{:S(2)}, u32[]{:S(2)}) collective-permute-start(bf16[128,768]{1,0:T(8,128)(2,1)} %bitcast.21), channel_id=1, source_target_pairs={{0,8},{8,0},{16,24},{24,16},{1,9},{9,1},{17,25},{25,17},{2,10},{10... | collective-permute-start | bytes 589832 | tf_op jit(solution)/shard_map/ppermute | solution.py:23
  3.7 1.5 %collective-permute-start.1 = (bf16[128,768]{1,0:T(8,128)(2,1)}, bf16[128,768]{1,0:T(8,128)(2,1)S(1)}, u32[]{:S(2)}, u32[]{:S(2)}) collective-permute-start(bf16[128,768]{1,0:T(8,128)(2,1)} %bitcast.22), channel_id=1, source_target_pairs={{0,16},{8,24},{16,0},{24,8},{1,17},{9,25},{17,1},{25,9},{2,18},{10... | collective-permute-start | bytes 589832 | tf_op jit(solution)/shard_map/ppermute | solution.py:23
  5.2 2.0 %copy-done.11 = bf16[768,2304]{1,0:T(8,128)(2,1)S(1)} copy-done((bf16[768,2304]{1,0:T(8,128)(2,1)S(1)}, bf16[768,2304]{1,0:T(8,128)(2,1)}, u32[]{:S(2)}) %copy-start.11) | copy-done | bytes 3538968
  7.4 2.1 %collective-permute-start.8 = (bf16[128,768]{1,0:T(8,128)(2,1)S(1)}, bf16[128,768]{1,0:T(8,128)(2,1)S(1)}, u32[]{:S(2)}, u32[]{:S(2)}) collective-permute-start(bf16[128,768]{1,0:T(8,128)(2,1)S(1)} %bitcast.28), channel_id=1, source_target_pairs={{0,8},{8,0},{16,24},{24,16},{1,9},{9,1},{17,25},{25,17},{2,10},{10... | collective-permute-start | bytes 589832 | tf_op jit(solution)/shard_map/ppermute | solution.py:23
  9.5 1.5 %collective-permute-start.7 = (bf16[128,768]{1,0:T(8,128)(2,1)S(1)}, bf16[128,768]{1,0:T(8,128)(2,1)S(1)}, u32[]{:S(2)}, u32[]{:S(2)}) collective-permute-start(bf16[128,768]{1,0:T(8,128)(2,1)S(1)} %bitcast.29), channel_id=1, source_target_pairs={{0,16},{8,24},{16,0},{24,8},{1,17},{9,25},{17,1},{25,9},{2,18},{10... | collective-permute-start | bytes 589832 | tf_op jit(solution)/shard_map/ppermute | solution.py:23
  14.8 1.5 %collective-permute-start.6 = (bf16[128,768]{1,0:T(8,128)(2,1)S(1)}, bf16[128,768]{1,0:T(8,128)(2,1)S(1)}, u32[]{:S(2)}, u32[]{:S(2)}) collective-permute-start(bf16[128,768]{1,0:T(8,128)(2,1)S(1)} %bitcast.30), channel_id=1, source_target_pairs={{0,24},{8,16},{16,8},{24,0},{1,25},{9,17},{17,9},{25,1},{2,26},{10... | collective-permute-start | bytes 589832 | tf_op jit(solution)/shard_map/ppermute | solution.py:23
  16.3 3.0 %attn_fwd.1 = (bf16[512,576]{1,0:T(8,128)(2,1)S(1)}, f32[512,128]{1,0:T(8,128)S(1)}, f32[8,512]{1,0:T(8,128)S(1)}, f32[512,128]{1,0:T(8,128)S(1)}, bf16[512,192]...) custom-call(bf16[128,768]{1,0:T(8,128)(2,1)S(1)} %bitcast.24, ...), custom_call_target="tpu_custom_call" | custom-call | flops 6000000000 | bytes 12000000 | tf_op jit(solution)/shard_map/attn_fwd/pallas_call | solution.py:476
  20.1 1.6 %collective-permute-start.4 = (bf16[64,384]{1,0:T(8,128)(2,1)S(1)}, bf16[64,384]{1,0:T(8,128)(2,1)S(1)}, u32[]{:S(2)}, u32[]{:S(2)}) collective-permute-start(bf16[64,384]{1,0:T(8,128)(2,1)S(1)} %get-tuple-element.136), channel_id=1, source_target_pairs={{0,16},{8,24},{16,0},{24,8},{1,17},{9,25},{17,1},{25,9},{2,18},{10... | collective-permute-start | bytes 147464 | tf_op jit(solution)/shard_map/ppermute | solution.py:23
  27.6 4.0 %local.1 = (bf16[128,3072]{1,0:T(8,128)(2,1)S(1)}, f32[128,768]{1,0:T(8,128)S(1)}, f32[128,768]{1,0:T(8,128)S(1)}, f32[8,768]{1,0:T(8,128)S(1)}, bf16[128,384]{1...) custom-call(bf16[128,768]{1,0:T(8,128)(2,1)S(1)} %bitcast.25, ...), custom_call_target="tpu_custom_call" | custom-call | flops 5000000000 | bytes 10000000 | tf_op jit(solution)/shard_map/local/pallas_call | solution.py:476
  31.6 1.5 %collective-permute-start.10 = (bf16[128,384]{1,0:T(8,128)(2,1)S(1)}, bf16[128,384]{1,0:T(8,128)(2,1)S(1)}, u32[]{:S(2)}, u32[]{:S(2)}) collective-permute-start(bf16[128,384]{1,0:T(8,128)(2,1)S(1)} %get-tuple-element.151), channel_id=1, source_target_pairs={{0,16},{8,24},{16,0},{24,8},{1,17},{9,25},{17,1},{25,9},{2,18},{10... | collective-permute-start | bytes 294920 | tf_op jit(solution)/shard_map/ppermute | solution.py:23
  35.3 3.6 %up.1 = (bf16[512,768]{1,0:T(8,128)(2,1)S(1)}, bf16[512,768]{1,0:T(8,128)(2,1)S(1)}, f32[512,768]{1,0:T(8,128)S(1)}, bf16[4,96,768]{2,1,0:T(8,128)(2,1)S(1)}, bf16[4,96,768]{2,1,0:T(8,128)(2,1)S(1)}) custom-call(bf16[128,768]{1,0:T(8,128)(2,1)S(1)} %bitcast.26, bf16[128,768]{1,0:T(8,128)(2,1)S(1)} %collective-permute-done.refs_1_, ...), custom_call_target="tpu_custom_call" | custom-call | flops 1000000000 | bytes 2000000 | tf_op jit(solution)/shard_map/up/pallas_call | solution.py:476
  39.0 1.9 %down.1 = (bf16[4,96,1024]{2,1,0:T(8,128)(2,1)S(1)}, bf16[4,96,1024]{2,1,0:T(8,128)(2,1)S(1)}) custom-call(bf16[128,768]{1,0:T(8,128)(2,1)S(1)} %bitcast.33, bf16[128,768]{1,0:T(8,128)(2,1)S(1)} %collective-permute-done.8.refs_12_.refs_1_, bf16[128,768]{1,0:T(8,128)(2,1)S(1)} %collective-permute-done.7.refs_13_.refs_2_, ...), custom_call_target="tpu_custom_call" | custom-call | flops 1000000000 | bytes 2000000 | tf_op jit(solution)/shard_map/down/pallas_call | solution.py:476
  41.9 2.7 %collective-permute-start.20 = (bf16[2,96,768]{2,1,0:T(8,128)(2,1)S(1)}, bf16[2,96,768]{2,1,0:T(8,128)(2,1)S(1)}, u32[]{:S(2)}, u32[]{:S(2)}) collective-permute-start(bf16[2,96,768]{2,1,0:T(8,128)(2,1)S(1)} %get-tuple-element.254), channel_id=1, source_target_pairs={{0,4},{1,5},{2,6},{3,7},{4,0},{5,1},{6,2},{7,3},{8,12},{9,13},{10,... | collective-permute-start | bytes 884744 | tf_op jit(solution)/shard_map/ppermute | solution.py:23
  44.8 1.6 %collective-permute-start.19 = (bf16[2,96,1024]{2,1,0:T(8,128)(2,1)S(1)}, bf16[2,96,1024]{2,1,0:T(8,128)(2,1)S(1)}, u32[]{:S(2)}, u32[]{:S(2)}) collective-permute-start(bf16[2,96,1024]{2,1,0:T(8,128)(2,1)S(1)} %get-tuple-element.252), channel_id=1, source_target_pairs={{0,2},{1,3},{2,0},{3,1},{4,6},{5,7},{6,4},{7,5},{8,10},{9,11},{10,... | collective-permute-start | bytes 1179656 | tf_op jit(solution)/shard_map/ppermute | solution.py:23
  46.4 5.2 %attn_bwd.1 = (f32[128,768]{1,0:T(8,128)S(1)}, f32[128,768]{1,0:T(8,128)S(1)}, bf16[2,128,768]{2,1,0:T(8,128)(2,1)S(1)}, bf16[4,96,640]{2,1,0:T(8,128)(2,1)S(1)}, bf16[4,96,640]{2,1,0:T(8,128)(2,1)S(1)}) custom-call(bf16[128,768]{1,0:T(8,128)(2,1)S(1)} %bitcast.27, bf16[128,768]{1,0:T(8,128)(2,1)S(1)} %collective-permute-done.refs_1_, ...), custom_call_target="tpu_custom_call" | custom-call | flops 1000000000 | bytes 2000000 | tf_op jit(solution)/shard_map/attn_bwd/pallas_call | solution.py:476
  54.5 3.7 %collective-permute-done.20 = bf16[2,96,768]{2,1,0:T(8,128)(2,1)S(1)} collective-permute-done((bf16[2,96,768]{2,1,0:T(8,128)(2,1)S(1)}, bf16[2,96,768]{2,1,0:T(8,128)(2,1)S(1)}, u32[]{:S(2)}, u32[]{:S(2)}) %collective-permute-start.20) | collective-permute-done | bytes 294944 | tf_op jit(solution)/shard_map/ppermute | solution.py:23
  58.9 2.6 %collective-permute-done.19 = bf16[2,96,1024]{2,1,0:T(8,128)(2,1)S(1)} collective-permute-done((bf16[2,96,1024]{2,1,0:T(8,128)(2,1)S(1)}, bf16[2,96,1024]{2,1,0:T(8,128)(2,1)S(1)}, u32[]{:S(2)}, u32[]{:S(2)}) %collective-permute-start.19) | collective-permute-done | bytes 393248 | tf_op jit(solution)/shard_map/ppermute | solution.py:23
  61.7 2.1 %collective-permute-start.28 = (bf16[1,96,1024]{2,1,0:T(8,128)(2,1)S(1)}, bf16[1,96,1024]{2,1,0:T(8,128)(2,1)S(1)}, u32[]{:S(2)}, u32[]{:S(2)}) collective-permute-start(bf16[1,96,1024]{2,1,0:T(8,128)(2,1)S(1)} %get-tuple-element.258), channel_id=1, source_target_pairs={{0,4},{1,5},{2,6},{3,7},{4,0},{5,1},{6,2},{7,3},{8,12},{9,13},{10,... | collective-permute-start | bytes 589832 | tf_op jit(solution)/shard_map/ppermute | solution.py:23
  63.9 2.5 %collective-permute-start.23 = (bf16[2,96,640]{2,1,0:T(8,128)(2,1)S(1)}, bf16[2,96,640]{2,1,0:T(8,128)(2,1)S(1)}, u32[]{:S(2)}, u32[]{:S(2)}) collective-permute-start(bf16[2,96,640]{2,1,0:T(8,128)(2,1)S(1)} %get-tuple-element.256), channel_id=1, source_target_pairs={{0,2},{1,3},{2,0},{3,1},{4,6},{5,7},{6,4},{7,5},{8,10},{9,11},{10,... | collective-permute-start | bytes 737288 | tf_op jit(solution)/shard_map/ppermute | solution.py:23
  69.9 3.5 %collective-permute-done.21 = bf16[128,768]{1,0:T(8,128)(2,1)S(1)} collective-permute-done((bf16[128,768]{1,0:T(8,128)(2,1)S(1)}, bf16[128,768]{1,0:T(8,128)(2,1)S(1)}, u32[]{:S(2)}, u32[]{:S(2)}) %collective-permute-start.21) | collective-permute-done | bytes 196640 | tf_op jit(solution)/shard_map/ppermute | solution.py:23
  73.4 1.7 %collective-permute-start.27 = (bf16[96,768]{1,0:T(8,128)(2,1)S(1)}, bf16[96,768]{1,0:T(8,128)(2,1)S(1)}, u32[]{:S(2)}, u32[]{:S(2)}) collective-permute-start(bf16[96,768]{1,0:T(8,128)(2,1)S(1)} %fusion.13.refs_0_), channel_id=1, source_target_pairs={{0,24},{8,16},{16,8},{24,0},{1,25},{9,17},{17,9},{25,1},{2,26},{10... | collective-permute-start | bytes 442376 | tf_op jit(solution)/shard_map/ppermute | solution.py:23
  78.7 1.7 %collective-permute-start.34 = (bf16[96,1024]{1,0:T(8,128)(2,1)S(1)}, bf16[96,1024]{1,0:T(8,128)(2,1)S(1)}, u32[]{:S(2)}, u32[]{:S(2)}) collective-permute-start(bf16[96,1024]{1,0:T(8,128)(2,1)S(1)} %fusion.12.refs_0_), channel_id=1, source_target_pairs={{0,24},{8,16},{16,8},{24,0},{1,25},{9,17},{17,9},{25,1},{2,26},{10... | collective-permute-start | bytes 589832 | tf_op jit(solution)/shard_map/ppermute | solution.py:23
  85.2 1.6 %collective-permute-start.31 = (bf16[96,640]{1,0:T(8,128)(2,1)S(1)}, bf16[96,640]{1,0:T(8,128)(2,1)S(1)}, u32[]{:S(2)}, u32[]{:S(2)}) collective-permute-start(bf16[96,640]{1,0:T(8,128)(2,1)S(1)} %fusion.14.refs_0_), channel_id=1, source_target_pairs={{0,24},{8,16},{16,8},{24,0},{1,25},{9,17},{17,9},{25,1},{2,26},{10... | collective-permute-start | bytes 368648 | tf_op jit(solution)/shard_map/ppermute | solution.py:23
  86.8 2.3 %collective-permute-done.33.refs_2_ = bf16[96,1024]{1,0:T(8,128)(2,1)S(1)} collective-permute-done((bf16[96,1024]{1,0:T(8,128)(2,1)S(1)}, bf16[96,1024]{1,0:T(8,128)(2,1)S(1)}, u32[]{:S(2)}, u32[]{:S(2)}) %collective-permute-start.33) | collective-permute-done | bytes 196640 | tf_op jit(solution)/shard_map/ppermute | solution.py:23
  (106 shorter events, 34.8 us)
Async XLA Ops:
  0.7 14.1 %collective-permute-start = (bf16[128,768]{1,0:T(8,128)(2,1)}, bf16[128,768]{1,0:T(8,128)(2,1)S(1)}, u32[]{:S(2)}, u32[]{:S(2)}) collective-permute-start(bf16[128,768]{1,0:T(8,128)(2,1)} %bitcast.21), channel_id=1, source_target_pairs={{0,8},{8,0},{16,24},{24,16},{1,9},{9,1},{17,25},{25,17},{2,10},{10... | collective-permute-start | bytes 589832 | tf_op jit(solution)/shard_map/ppermute | solution.py:23
  3.7 12.6 %collective-permute-start.1 = (bf16[128,768]{1,0:T(8,128)(2,1)}, bf16[128,768]{1,0:T(8,128)(2,1)S(1)}, u32[]{:S(2)}, u32[]{:S(2)}) collective-permute-start(bf16[128,768]{1,0:T(8,128)(2,1)} %bitcast.22), channel_id=1, source_target_pairs={{0,16},{8,24},{16,0},{24,8},{1,17},{9,25},{17,1},{25,9},{2,18},{10... | collective-permute-start | bytes 589832 | tf_op jit(solution)/shard_map/ppermute | solution.py:23
  5.2 11.1 %collective-permute-start.2 = (bf16[128,768]{1,0:T(8,128)(2,1)}, bf16[128,768]{1,0:T(8,128)(2,1)S(1)}, u32[]{:S(2)}, u32[]{:S(2)}) collective-permute-start(bf16[128,768]{1,0:T(8,128)(2,1)} %bitcast.23), channel_id=1, source_target_pairs={{0,24},{8,16},{16,8},{24,0},{1,25},{9,17},{17,9},{25,1},{2,26},{10... | collective-permute-start | bytes 589832 | tf_op jit(solution)/shard_map/ppermute | solution.py:23
  7.4 12.0 %collective-permute-start.8 = (bf16[128,768]{1,0:T(8,128)(2,1)S(1)}, bf16[128,768]{1,0:T(8,128)(2,1)S(1)}, u32[]{:S(2)}, u32[]{:S(2)}) collective-permute-start(bf16[128,768]{1,0:T(8,128)(2,1)S(1)} %bitcast.28), channel_id=1, source_target_pairs={{0,8},{8,0},{16,24},{24,16},{1,9},{9,1},{17,25},{25,17},{2,10},{10... | collective-permute-start | bytes 589832 | tf_op jit(solution)/shard_map/ppermute | solution.py:23
  9.5 14.4 %collective-permute-start.7 = (bf16[128,768]{1,0:T(8,128)(2,1)S(1)}, bf16[128,768]{1,0:T(8,128)(2,1)S(1)}, u32[]{:S(2)}, u32[]{:S(2)}) collective-permute-start(bf16[128,768]{1,0:T(8,128)(2,1)S(1)} %bitcast.29), channel_id=1, source_target_pairs={{0,16},{8,24},{16,0},{24,8},{1,17},{9,25},{17,1},{25,9},{2,18},{10... | collective-permute-start | bytes 589832 | tf_op jit(solution)/shard_map/ppermute | solution.py:23
  14.8 9.2 %collective-permute-start.6 = (bf16[128,768]{1,0:T(8,128)(2,1)S(1)}, bf16[128,768]{1,0:T(8,128)(2,1)S(1)}, u32[]{:S(2)}, u32[]{:S(2)}) collective-permute-start(bf16[128,768]{1,0:T(8,128)(2,1)S(1)} %bitcast.30), channel_id=1, source_target_pairs={{0,24},{8,16},{16,8},{24,0},{1,25},{9,17},{17,9},{25,1},{2,26},{10... | collective-permute-start | bytes 589832 | tf_op jit(solution)/shard_map/ppermute | solution.py:23
  24.0 10.3 %collective-permute-start.12 = (bf16[192,384]{1,0:T(8,128)(2,1)S(1)}, bf16[192,384]{1,0:T(8,128)(2,1)S(1)}, u32[]{:S(2)}, u32[]{:S(2)}) collective-permute-start(bf16[192,384]{1,0:T(8,128)(2,1)S(1)} %get-tuple-element.157), channel_id=1, source_target_pairs={{0,8},{8,0},{16,24},{24,16},{1,9},{9,1},{17,25},{25,17},{2,10},{10... | collective-permute-start | bytes 442376 | tf_op jit(solution)/shard_map/ppermute | solution.py:23
  25.2 10.0 %collective-permute-start.13 = (bf16[192,384]{1,0:T(8,128)(2,1)S(1)}, bf16[192,384]{1,0:T(8,128)(2,1)S(1)}, u32[]{:S(2)}, u32[]{:S(2)}) collective-permute-start(bf16[192,384]{1,0:T(8,128)(2,1)S(1)} %get-tuple-element.158), channel_id=1, source_target_pairs={{0,16},{8,24},{16,0},{24,8},{1,17},{9,25},{17,1},{25,9},{2,18},{10... | collective-permute-start | bytes 442376 | tf_op jit(solution)/shard_map/ppermute | solution.py:23
  26.3 9.0 %collective-permute-start.14 = (bf16[192,384]{1,0:T(8,128)(2,1)S(1)}, bf16[192,384]{1,0:T(8,128)(2,1)S(1)}, u32[]{:S(2)}, u32[]{:S(2)}) collective-permute-start(bf16[192,384]{1,0:T(8,128)(2,1)S(1)} %get-tuple-element.159), channel_id=1, source_target_pairs={{0,24},{8,16},{16,8},{24,0},{1,25},{9,17},{17,9},{25,1},{2,26},{10... | collective-permute-start | bytes 442376 | tf_op jit(solution)/shard_map/ppermute | solution.py:23
  41.9 16.3 %collective-permute-start.20 = (bf16[2,96,768]{2,1,0:T(8,128)(2,1)S(1)}, bf16[2,96,768]{2,1,0:T(8,128)(2,1)S(1)}, u32[]{:S(2)}, u32[]{:S(2)}) collective-permute-start(bf16[2,96,768]{2,1,0:T(8,128)(2,1)S(1)} %get-tuple-element.254), channel_id=1, source_target_pairs={{0,4},{1,5},{2,6},{3,7},{4,0},{5,1},{6,2},{7,3},{8,12},{9,13},{10,... | collective-permute-start | bytes 884744 | tf_op jit(solution)/shard_map/ppermute | solution.py:23
  44.8 16.8 %collective-permute-start.19 = (bf16[2,96,1024]{2,1,0:T(8,128)(2,1)S(1)}, bf16[2,96,1024]{2,1,0:T(8,128)(2,1)S(1)}, u32[]{:S(2)}, u32[]{:S(2)}) collective-permute-start(bf16[2,96,1024]{2,1,0:T(8,128)(2,1)S(1)} %get-tuple-element.252), channel_id=1, source_target_pairs={{0,2},{1,3},{2,0},{3,1},{4,6},{5,7},{6,4},{7,5},{8,10},{9,11},{10,... | collective-permute-start | bytes 1179656 | tf_op jit(solution)/shard_map/ppermute | solution.py:23
  51.7 12.1 %collective-permute-start.18 = (bf16[4,96,640]{2,1,0:T(8,128)(2,1)S(1)}, bf16[4,96,640]{2,1,0:T(8,128)(2,1)S(1)}, u32[]{:S(2)}, u32[]{:S(2)}) collective-permute-start(bf16[4,96,640]{2,1,0:T(8,128)(2,1)S(1)} %get-tuple-element.207), channel_id=1, source_target_pairs={{0,1},{1,0},{2,3},{3,2},{4,5},{5,4},{6,7},{7,6},{8,9},{9,8},{10,11... | collective-permute-start | bytes 1474568 | tf_op jit(solution)/shard_map/ppermute | solution.py:23
  51.8 14.7 %collective-permute-start.17 = (bf16[2,128,768]{2,1,0:T(8,128)(2,1)S(1)}, bf16[2,128,768]{2,1,0:T(8,128)(2,1)S(1)}, u32[]{:S(2)}, u32[]{:S(2)}) collective-permute-start(bf16[2,128,768]{2,1,0:T(8,128)(2,1)S(1)} %get-tuple-element.206), channel_id=1, source_target_pairs={{0,8},{8,0},{16,24},{24,16},{1,9},{9,1},{17,25},{25,17},{2,10},{10... | collective-permute-start | bytes 1179656 | tf_op jit(solution)/shard_map/ppermute | solution.py:23
  58.3 9.7 %collective-permute-start.22 = (bf16[1,96,768]{2,1,0:T(8,128)(2,1)S(1)}, bf16[1,96,768]{2,1,0:T(8,128)(2,1)S(1)}, u32[]{:S(2)}, u32[]{:S(2)}) collective-permute-start(bf16[1,96,768]{2,1,0:T(8,128)(2,1)S(1)} %get-tuple-element.260), channel_id=1, source_target_pairs={{0,2},{1,3},{2,0},{3,1},{4,6},{5,7},{6,4},{7,5},{8,10},{9,11},{10,... | collective-permute-start | bytes 442376 | tf_op jit(solution)/shard_map/ppermute | solution.py:23
  61.7 15.0 %collective-permute-start.28 = (bf16[1,96,1024]{2,1,0:T(8,128)(2,1)S(1)}, bf16[1,96,1024]{2,1,0:T(8,128)(2,1)S(1)}, u32[]{:S(2)}, u32[]{:S(2)}) collective-permute-start(bf16[1,96,1024]{2,1,0:T(8,128)(2,1)S(1)} %get-tuple-element.258), channel_id=1, source_target_pairs={{0,4},{1,5},{2,6},{3,7},{4,0},{5,1},{6,2},{7,3},{8,12},{9,13},{10,... | collective-permute-start | bytes 589832 | tf_op jit(solution)/shard_map/ppermute | solution.py:23
  63.9 12.4 %collective-permute-start.23 = (bf16[2,96,640]{2,1,0:T(8,128)(2,1)S(1)}, bf16[2,96,640]{2,1,0:T(8,128)(2,1)S(1)}, u32[]{:S(2)}, u32[]{:S(2)}) collective-permute-start(bf16[2,96,640]{2,1,0:T(8,128)(2,1)S(1)} %get-tuple-element.256), channel_id=1, source_target_pairs={{0,2},{1,3},{2,0},{3,1},{4,6},{5,7},{6,4},{7,5},{8,10},{9,11},{10,... | collective-permute-start | bytes 737288 | tf_op jit(solution)/shard_map/ppermute | solution.py:23
  68.1 10.0 %collective-permute-start.25 = (bf16[96,768]{1,0:T(8,128)(2,1)S(1)}, bf16[96,768]{1,0:T(8,128)(2,1)S(1)}, u32[]{:S(2)}, u32[]{:S(2)}) collective-permute-start(bf16[96,768]{1,0:T(8,128)(2,1)S(1)} %fusion.13.refs_0_), channel_id=1, source_target_pairs={{0,8},{8,0},{16,24},{24,16},{1,9},{9,1},{17,25},{25,17},{2,10},{10... | collective-permute-start | bytes 442376 | tf_op jit(solution)/shard_map/ppermute | solution.py:23
  68.9 9.7 %collective-permute-start.26 = (bf16[96,768]{1,0:T(8,128)(2,1)S(1)}, bf16[96,768]{1,0:T(8,128)(2,1)S(1)}, u32[]{:S(2)}, u32[]{:S(2)}) collective-permute-start(bf16[96,768]{1,0:T(8,128)(2,1)S(1)} %fusion.13.refs_0_), channel_id=1, source_target_pairs={{0,16},{8,24},{16,0},{24,8},{1,17},{9,25},{17,1},{25,9},{2,18},{10... | collective-permute-start | bytes 442376 | tf_op jit(solution)/shard_map/ppermute | solution.py:23
  73.4 7.6 %collective-permute-start.27 = (bf16[96,768]{1,0:T(8,128)(2,1)S(1)}, bf16[96,768]{1,0:T(8,128)(2,1)S(1)}, u32[]{:S(2)}, u32[]{:S(2)}) collective-permute-start(bf16[96,768]{1,0:T(8,128)(2,1)S(1)} %fusion.13.refs_0_), channel_id=1, source_target_pairs={{0,24},{8,16},{16,8},{24,0},{1,25},{9,17},{17,9},{25,1},{2,26},{10... | collective-permute-start | bytes 442376 | tf_op jit(solution)/shard_map/ppermute | solution.py:23
  76.8 8.4 %collective-permute-start.32 = (bf16[96,1024]{1,0:T(8,128)(2,1)S(1)}, bf16[96,1024]{1,0:T(8,128)(2,1)S(1)}, u32[]{:S(2)}, u32[]{:S(2)}) collective-permute-start(bf16[96,1024]{1,0:T(8,128)(2,1)S(1)} %fusion.12.refs_0_), channel_id=1, source_target_pairs={{0,8},{8,0},{16,24},{24,16},{1,9},{9,1},{17,25},{25,17},{2,10},{10... | collective-permute-start | bytes 589832 | tf_op jit(solution)/shard_map/ppermute | solution.py:23
  78.1 11.1 %collective-permute-start.33 = (bf16[96,1024]{1,0:T(8,128)(2,1)S(1)}, bf16[96,1024]{1,0:T(8,128)(2,1)S(1)}, u32[]{:S(2)}, u32[]{:S(2)}) collective-permute-start(bf16[96,1024]{1,0:T(8,128)(2,1)S(1)} %fusion.12.refs_0_), channel_id=1, source_target_pairs={{0,16},{8,24},{16,0},{24,8},{1,17},{9,25},{17,1},{25,9},{2,18},{10... | collective-permute-start | bytes 589832 | tf_op jit(solution)/shard_map/ppermute | solution.py:23
  78.7 10.9 %collective-permute-start.34 = (bf16[96,1024]{1,0:T(8,128)(2,1)S(1)}, bf16[96,1024]{1,0:T(8,128)(2,1)S(1)}, u32[]{:S(2)}, u32[]{:S(2)}) collective-permute-start(bf16[96,1024]{1,0:T(8,128)(2,1)S(1)} %fusion.12.refs_0_), channel_id=1, source_target_pairs={{0,24},{8,16},{16,8},{24,0},{1,25},{9,17},{17,9},{25,1},{2,26},{10... | collective-permute-start | bytes 589832 | tf_op jit(solution)/shard_map/ppermute | solution.py:23
  83.3 7.8 %collective-permute-start.29 = (bf16[96,640]{1,0:T(8,128)(2,1)S(1)}, bf16[96,640]{1,0:T(8,128)(2,1)S(1)}, u32[]{:S(2)}, u32[]{:S(2)}) collective-permute-start(bf16[96,640]{1,0:T(8,128)(2,1)S(1)} %fusion.14.refs_0_), channel_id=1, source_target_pairs={{0,8},{8,0},{16,24},{24,16},{1,9},{9,1},{17,25},{25,17},{2,10},{10... | collective-permute-start | bytes 368648 | tf_op jit(solution)/shard_map/ppermute | solution.py:23
  85.2 8.0 %collective-permute-start.31 = (bf16[96,640]{1,0:T(8,128)(2,1)S(1)}, bf16[96,640]{1,0:T(8,128)(2,1)S(1)}, u32[]{:S(2)}, u32[]{:S(2)}) collective-permute-start(bf16[96,640]{1,0:T(8,128)(2,1)S(1)} %fusion.14.refs_0_), channel_id=1, source_target_pairs={{0,24},{8,16},{16,8},{24,0},{1,25},{9,17},{17,9},{25,1},{2,26},{10... | collective-permute-start | bytes 368648 | tf_op jit(solution)/shard_map/ppermute | solution.py:23
  (26 other events, 135.8 us)

commit v6 on v5

--- a/solution.py
+++ b/solution.py
@@ -68,8 +68,8 @@
 
 HOPS = {"d": "far", "u": "near", "a": "near"}
 GATHER = {"d": None, "u": None, "a": None}
-DH = (1, 2)
-ORDER = "pq cs t2 t1 af fs c1 pm c2 c3 lo fa up dn d0 u0 bw ou d1 u1 a0 h1 d2 h2 a1 u2 d3 d4 a2 u3 u4 a3 a4".split()
+DH = (2, 1)
+ORDER = "pq cs t2 t1 af fs c1 pm c2 c3 lo fa up dn d0 u0 bw ou d1 u1 h1 a0 h2 d2 a1 u2 d3 d4 a2 h3 u3 u4 a3 a4".split()
 
 
 def flat(ref):
@@ -643,6 +643,10 @@
             token[0] = beside
 
         def h_last():
+            (v["h_got"],) = wait("h_got")
+            token[0] = v["h_got"]
+
+        def token_grad():
             (got,) = wait("h_got")
             unit1, scale1 = norm_parts(x_own.astype(F32))
             dh1 = v["own"] + got.astype(F32)
@@ -661,7 +665,7 @@
             dn=down, bw=attn_bwd, d0=halve("d", 0), d1=halve("d", 1), d2=halve("d", 2), d3=spread("d"), d4=d_final,
             u0=halve("u", 0), u1=halve("u", 1), u2=halve("u", 2), u3=spread("u"), u4=u_final,
             a0=halve("a", 0), a1=halve("a", 1), a2=halve("a", 2), a3=spread("a"), a4=a_final,
-            h1=h_first, h2=h_last, ou=forward_out)
+            h1=h_first, h2=h_last, h3=token_grad, ou=forward_out)
         for name in ORDER:
             steps[name]()
         out, d_tokens, o_wdn = v["out"], v["d_tokens"].reshape(tokens.shape), v["o_wdn"]

time: 94.6 us -> 92 us (0.973)
  waiting for transfers between devices: 16.6 us -> 14.8 us
    ppermute x35, waiting for transfers between devices: 16.6 us -> 14.8 us  [exchange(): return lax.ppermute(value, axis, [(j, j ^ step) for j in range(size)])]
  transfers between devices with their start and end apart: 35 -> 35, of which waited for: 9 -> 9; matrix products, arithmetic and copies ran while one was open for 3% -> 3% of each run, Pallas kernels for 27% -> 28%
where the time goes in v6:
time: 92 us; the launch traced here: 91.8 us
  starting transfers between devices  43.6 us (47%)
  Pallas kernels  26.8 us (29%)
  waiting for transfers between devices  14.8 us (16%)
  local copies, waits for them, and re-layouts  3.12 us (3%)
  other arithmetic  2.46 us (3%)
  between operations  0.96 us (1%)
    ppermute x35, starting transfers between devices, exchange(): return lax.ppermute(value, axis, [(j, j ^ step) for j in range(size)])  43.6 us
    pallas_call x13, Pallas kernels, kernel(): pl.pallas_call(body, out_shape=outs, scratch_shapes=list(scratch), name=n...  26.8 us
    ppermute x35, waiting for transfers between devices, exchange(): return lax.ppermute(value, axis, [(j, j ^ step) for j in range(size)])  14.8 us
    unnamed x30, local copies, waits for them, and re-layouts  3.12 us
  transfers between devices with their start and end apart: 35, of which 9 were waited for; matrix products, arithmetic and copies ran while one was open for 3% of the time, Pallas kernels for 28%

profile of v6, /device:TPU:0, one launch (start us, length us, event | category | flops | bytes accessed | tf_op | source)
XLA Modules:
  0.0 91.8 jit_solution(6245312773445590961)
XLA Ops:
  0.7 3.0 %collective-permute-start = (bf16[128,768]{1,0:T(8,128)(2,1)}, bf16[128,768]{1,0:T(8,128)(2,1)S(1)}, u32[]{:S(2)}, u32[]{:S(2)}) collective-permute-start(bf16[128,768]{1,0:T(8,128)(2,1)} %bitcast.21), channel_id=1, source_target_pairs={{0,8},{8,0},{16,24},{24,16},{1,9},{9,1},{17,25},{25,17},{2,10},{10... | collective-permute-start | bytes 589832 | tf_op jit(solution)/shard_map/ppermute | solution.py:23
  3.7 1.5 %collective-permute-start.1 = (bf16[128,768]{1,0:T(8,128)(2,1)}, bf16[128,768]{1,0:T(8,128)(2,1)S(1)}, u32[]{:S(2)}, u32[]{:S(2)}) collective-permute-start(bf16[128,768]{1,0:T(8,128)(2,1)} %bitcast.22), channel_id=1, source_target_pairs={{0,16},{8,24},{16,0},{24,8},{1,17},{9,25},{17,1},{25,9},{2,18},{10... | collective-permute-start | bytes 589832 | tf_op jit(solution)/shard_map/ppermute | solution.py:23
  5.2 2.0 %copy-done.11 = bf16[768,2304]{1,0:T(8,128)(2,1)S(1)} copy-done((bf16[768,2304]{1,0:T(8,128)(2,1)S(1)}, bf16[768,2304]{1,0:T(8,128)(2,1)}, u32[]{:S(2)}) %copy-start.11) | copy-done | bytes 3538968
  7.4 2.1 %collective-permute-start.8 = (bf16[128,768]{1,0:T(8,128)(2,1)S(1)}, bf16[128,768]{1,0:T(8,128)(2,1)S(1)}, u32[]{:S(2)}, u32[]{:S(2)}) collective-permute-start(bf16[128,768]{1,0:T(8,128)(2,1)S(1)} %bitcast.28), channel_id=1, source_target_pairs={{0,8},{8,0},{16,24},{24,16},{1,9},{9,1},{17,25},{25,17},{2,10},{10... | collective-permute-start | bytes 589832 | tf_op jit(solution)/shard_map/ppermute | solution.py:23
  9.5 1.5 %collective-permute-start.7 = (bf16[128,768]{1,0:T(8,128)(2,1)S(1)}, bf16[128,768]{1,0:T(8,128)(2,1)S(1)}, u32[]{:S(2)}, u32[]{:S(2)}) collective-permute-start(bf16[128,768]{1,0:T(8,128)(2,1)S(1)} %bitcast.29), channel_id=1, source_target_pairs={{0,16},{8,24},{16,0},{24,8},{1,17},{9,25},{17,1},{25,9},{2,18},{10... | collective-permute-start | bytes 589832 | tf_op jit(solution)/shard_map/ppermute | solution.py:23
  14.8 1.5 %collective-permute-start.6 = (bf16[128,768]{1,0:T(8,128)(2,1)S(1)}, bf16[128,768]{1,0:T(8,128)(2,1)S(1)}, u32[]{:S(2)}, u32[]{:S(2)}) collective-permute-start(bf16[128,768]{1,0:T(8,128)(2,1)S(1)} %bitcast.30), channel_id=1, source_target_pairs={{0,24},{8,16},{16,8},{24,0},{1,25},{9,17},{17,9},{25,1},{2,26},{10... | collective-permute-start | bytes 589832 | tf_op jit(solution)/shard_map/ppermute | solution.py:23
  16.3 3.0 %attn_fwd.1 = (bf16[512,576]{1,0:T(8,128)(2,1)S(1)}, f32[512,128]{1,0:T(8,128)S(1)}, f32[8,512]{1,0:T(8,128)S(1)}, f32[512,128]{1,0:T(8,128)S(1)}, bf16[512,192]...) custom-call(bf16[128,768]{1,0:T(8,128)(2,1)S(1)} %bitcast.24, ...), custom_call_target="tpu_custom_call" | custom-call | flops 6000000000 | bytes 12000000 | tf_op jit(solution)/shard_map/attn_fwd/pallas_call | solution.py:476
  20.1 1.6 %collective-permute-start.4 = (bf16[64,384]{1,0:T(8,128)(2,1)S(1)}, bf16[64,384]{1,0:T(8,128)(2,1)S(1)}, u32[]{:S(2)}, u32[]{:S(2)}) collective-permute-start(bf16[64,384]{1,0:T(8,128)(2,1)S(1)} %get-tuple-element.137), channel_id=1, source_target_pairs={{0,16},{8,24},{16,0},{24,8},{1,17},{9,25},{17,1},{25,9},{2,18},{10... | collective-permute-start | bytes 147464 | tf_op jit(solution)/shard_map/ppermute | solution.py:23
  27.6 4.0 %local.1 = (bf16[128,3072]{1,0:T(8,128)(2,1)S(1)}, f32[128,768]{1,0:T(8,128)S(1)}, f32[128,768]{1,0:T(8,128)S(1)}, f32[8,768]{1,0:T(8,128)S(1)}, bf16[128,384]{1...) custom-call(bf16[128,768]{1,0:T(8,128)(2,1)S(1)} %bitcast.25, ...), custom_call_target="tpu_custom_call" | custom-call | flops 5000000000 | bytes 10000000 | tf_op jit(solution)/shard_map/local/pallas_call | solution.py:476
  31.6 1.5 %collective-permute-start.10 = (bf16[128,384]{1,0:T(8,128)(2,1)S(1)}, bf16[128,384]{1,0:T(8,128)(2,1)S(1)}, u32[]{:S(2)}, u32[]{:S(2)}) collective-permute-start(bf16[128,384]{1,0:T(8,128)(2,1)S(1)} %get-tuple-element.152), channel_id=1, source_target_pairs={{0,16},{8,24},{16,0},{24,8},{1,17},{9,25},{17,1},{25,9},{2,18},{10... | collective-permute-start | bytes 294920 | tf_op jit(solution)/shard_map/ppermute | solution.py:23
  35.1 3.6 %up.1 = (bf16[512,768]{1,0:T(8,128)(2,1)S(1)}, bf16[512,768]{1,0:T(8,128)(2,1)S(1)}, f32[512,768]{1,0:T(8,128)S(1)}, bf16[4,96,768]{2,1,0:T(8,128)(2,1)S(1)}, bf16[4,96,768]{2,1,0:T(8,128)(2,1)S(1)}) custom-call(bf16[128,768]{1,0:T(8,128)(2,1)S(1)} %bitcast.26, bf16[128,768]{1,0:T(8,128)(2,1)S(1)} %collective-permute-done.refs_1_, ...), custom_call_target="tpu_custom_call" | custom-call | flops 1000000000 | bytes 2000000 | tf_op jit(solution)/shard_map/up/pallas_call | solution.py:476
  38.9 1.9 %down.1 = (bf16[4,96,1024]{2,1,0:T(8,128)(2,1)S(1)}, bf16[4,96,1024]{2,1,0:T(8,128)(2,1)S(1)}) custom-call(bf16[128,768]{1,0:T(8,128)(2,1)S(1)} %bitcast.33, bf16[128,768]{1,0:T(8,128)(2,1)S(1)} %collective-permute-done.8.refs_12_.refs_1_, bf16[128,768]{1,0:T(8,128)(2,1)S(1)} %collective-permute-done.7.refs_13_.refs_2_, ...), custom_call_target="tpu_custom_call" | custom-call | flops 1000000000 | bytes 2000000 | tf_op jit(solution)/shard_map/down/pallas_call | solution.py:476
  41.9 2.7 %collective-permute-start.19 = (bf16[2,96,768]{2,1,0:T(8,128)(2,1)S(1)}, bf16[2,96,768]{2,1,0:T(8,128)(2,1)S(1)}, u32[]{:S(2)}, u32[]{:S(2)}) collective-permute-start(bf16[2,96,768]{2,1,0:T(8,128)(2,1)S(1)} %get-tuple-element.256), channel_id=1, source_target_pairs={{0,4},{1,5},{2,6},{3,7},{4,0},{5,1},{6,2},{7,3},{8,12},{9,13},{10,... | collective-permute-start | bytes 884744 | tf_op jit(solution)/shard_map/ppermute | solution.py:23
  44.8 1.6 %collective-permute-start.18 = (bf16[2,96,1024]{2,1,0:T(8,128)(2,1)S(1)}, bf16[2,96,1024]{2,1,0:T(8,128)(2,1)S(1)}, u32[]{:S(2)}, u32[]{:S(2)}) collective-permute-start(bf16[2,96,1024]{2,1,0:T(8,128)(2,1)S(1)} %get-tuple-element.254), channel_id=1, source_target_pairs={{0,2},{1,3},{2,0},{3,1},{4,6},{5,7},{6,4},{7,5},{8,10},{9,11},{10,... | collective-permute-start | bytes 1179656 | tf_op jit(solution)/shard_map/ppermute | solution.py:23
  46.5 5.2 %attn_bwd.1 = (f32[128,768]{1,0:T(8,128)S(1)}, f32[128,768]{1,0:T(8,128)S(1)}, bf16[2,128,768]{2,1,0:T(8,128)(2,1)S(1)}, bf16[4,96,640]{2,1,0:T(8,128)(2,1)S(1)}, bf16[4,96,640]{2,1,0:T(8,128)(2,1)S(1)}) custom-call(bf16[128,768]{1,0:T(8,128)(2,1)S(1)} %bitcast.27, bf16[128,768]{1,0:T(8,128)(2,1)S(1)} %collective-permute-done.refs_1_, ...), custom_call_target="tpu_custom_call" | custom-call | flops 1000000000 | bytes 2000000 | tf_op jit(solution)/shard_map/attn_bwd/pallas_call | solution.py:476
  51.7 1.4 %collective-permute-start.17 = (bf16[2,128,768]{2,1,0:T(8,128)(2,1)S(1)}, bf16[2,128,768]{2,1,0:T(8,128)(2,1)S(1)}, u32[]{:S(2)}, u32[]{:S(2)}) collective-permute-start(bf16[2,128,768]{2,1,0:T(8,128)(2,1)S(1)} %get-tuple-element.207), channel_id=1, source_target_pairs={{0,16},{8,24},{16,0},{24,8},{1,17},{9,25},{17,1},{25,9},{2,18},{10... | collective-permute-start | bytes 1179656 | tf_op jit(solution)/shard_map/ppermute | solution.py:23
  53.1 1.5 %out.1 = bf16[128,768]{1,0:T(8,128)(2,1)} custom-call(f32[128,768]{1,0:T(8,128)S(1)} %get-tuple-element.204.x1_ref, bf16[128,3072]{1,0:T(8,128)(2,1)S(1)} %get-tuple-element.205.act, bf16[3072,768]{1,0:T(8,128)(2,1)S(1)} %copy-done, f32[768]{0:T(1024)S(1)} %copy-done.10), custom_call_target="tpu_custom_call" | custom-call | flops 1000000000 | bytes 2000000 | tf_op jit(solution)/shard_map/out/pallas_call | solution.py:476
  54.6 3.6 %collective-permute-done.19 = bf16[2,96,768]{2,1,0:T(8,128)(2,1)S(1)} collective-permute-done((bf16[2,96,768]{2,1,0:T(8,128)(2,1)S(1)}, bf16[2,96,768]{2,1,0:T(8,128)(2,1)S(1)}, u32[]{:S(2)}, u32[]{:S(2)}) %collective-permute-start.19) | collective-permute-done | bytes 294944 | tf_op jit(solution)/shard_map/ppermute | solution.py:23
  59.0 2.6 %collective-permute-done.18 = bf16[2,96,1024]{2,1,0:T(8,128)(2,1)S(1)} collective-permute-done((bf16[2,96,1024]{2,1,0:T(8,128)(2,1)S(1)}, bf16[2,96,1024]{2,1,0:T(8,128)(2,1)S(1)}, u32[]{:S(2)}, u32[]{:S(2)}) %collective-permute-start.18) | collective-permute-done | bytes 393248 | tf_op jit(solution)/shard_map/ppermute | solution.py:23
  64.1 3.3 %collective-permute-start.28 = (bf16[1,96,1024]{2,1,0:T(8,128)(2,1)S(1)}, bf16[1,96,1024]{2,1,0:T(8,128)(2,1)S(1)}, u32[]{:S(2)}, u32[]{:S(2)}) collective-permute-start(bf16[1,96,1024]{2,1,0:T(8,128)(2,1)S(1)} %get-tuple-element.260), channel_id=1, source_target_pairs={{0,4},{1,5},{2,6},{3,7},{4,0},{5,1},{6,2},{7,3},{8,12},{9,13},{10,... | collective-permute-start | bytes 589832 | tf_op jit(solution)/shard_map/ppermute | solution.py:23
  71.6 2.4 %collective-permute-done.22 = bf16[2,96,640]{2,1,0:T(8,128)(2,1)S(1)} collective-permute-done((bf16[2,96,640]{2,1,0:T(8,128)(2,1)S(1)}, bf16[2,96,640]{2,1,0:T(8,128)(2,1)S(1)}, u32[]{:S(2)}, u32[]{:S(2)}) %collective-permute-start.22) | collective-permute-done | bytes 245792 | tf_op jit(solution)/shard_map/ppermute | solution.py:23
  79.4 2.0 %collective-permute-done.24 = bf16[1,96,640]{2,1,0:T(8,128)(2,1)S(1)} collective-permute-done((bf16[1,96,640]{2,1,0:T(8,128)(2,1)S(1)}, bf16[1,96,640]{2,1,0:T(8,128)(2,1)S(1)}, u32[]{:S(2)}, u32[]{:S(2)}) %collective-permute-start.24) | collective-permute-done | bytes 122912 | tf_op jit(solution)/shard_map/ppermute | solution.py:23
  86.6 1.5 %up_final.1 = (f32[96,3072]{1,0:T(8,128)}, f32[96,768]{1,0:T(8,128)}, f32[96]{0:T(128)}, f32[96]{0:T(128)}, f32[96]{0:T(128)}, /*index=5*/f32[96]{0:T(128)}, f32[384]{0:T(512)}) custom-call(bf16[96,1024]{1,0:T(8,128)(2,1)S(1)} %fusion.12.refs_0_, bf16[96,1024]{1,0:T(8,128)(2,1)S(1)} %collective-permute-done.32.refs_1_, ...), custom_call_target="tpu_custom_call" | custom-call | flops 1000000000 | bytes 2000000 | tf_op jit(solution)/shard_map/up_final/pallas_call | solution.py:476
  88.0 2.6 %collective-permute-done.30.refs_2_ = bf16[96,640]{1,0:T(8,128)(2,1)S(1)} collective-permute-done((bf16[96,640]{1,0:T(8,128)(2,1)S(1)}, bf16[96,640]{1,0:T(8,128)(2,1)S(1)}, u32[]{:S(2)}, u32[]{:S(2)}) %collective-permute-start.30) | collective-permute-done | bytes 122912 | tf_op jit(solution)/shard_map/ppermute | solution.py:23
  (106 shorter events, 33.2 us)
Async XLA Ops:
  0.7 14.1 %collective-permute-start = (bf16[128,768]{1,0:T(8,128)(2,1)}, bf16[128,768]{1,0:T(8,128)(2,1)S(1)}, u32[]{:S(2)}, u32[]{:S(2)}) collective-permute-start(bf16[128,768]{1,0:T(8,128)(2,1)} %bitcast.21), channel_id=1, source_target_pairs={{0,8},{8,0},{16,24},{24,16},{1,9},{9,1},{17,25},{25,17},{2,10},{10... | collective-permute-start | bytes 589832 | tf_op jit(solution)/shard_map/ppermute | solution.py:23
  3.7 12.6 %collective-permute-start.1 = (bf16[128,768]{1,0:T(8,128)(2,1)}, bf16[128,768]{1,0:T(8,128)(2,1)S(1)}, u32[]{:S(2)}, u32[]{:S(2)}) collective-permute-start(bf16[128,768]{1,0:T(8,128)(2,1)} %bitcast.22), channel_id=1, source_target_pairs={{0,16},{8,24},{16,0},{24,8},{1,17},{9,25},{17,1},{25,9},{2,18},{10... | collective-permute-start | bytes 589832 | tf_op jit(solution)/shard_map/ppermute | solution.py:23
  5.2 11.1 %collective-permute-start.2 = (bf16[128,768]{1,0:T(8,128)(2,1)}, bf16[128,768]{1,0:T(8,128)(2,1)S(1)}, u32[]{:S(2)}, u32[]{:S(2)}) collective-permute-start(bf16[128,768]{1,0:T(8,128)(2,1)} %bitcast.23), channel_id=1, source_target_pairs={{0,24},{8,16},{16,8},{24,0},{1,25},{9,17},{17,9},{25,1},{2,26},{10... | collective-permute-start | bytes 589832 | tf_op jit(solution)/shard_map/ppermute | solution.py:23
  7.4 12.0 %collective-permute-start.8 = (bf16[128,768]{1,0:T(8,128)(2,1)S(1)}, bf16[128,768]{1,0:T(8,128)(2,1)S(1)}, u32[]{:S(2)}, u32[]{:S(2)}) collective-permute-start(bf16[128,768]{1,0:T(8,128)(2,1)S(1)} %bitcast.28), channel_id=1, source_target_pairs={{0,8},{8,0},{16,24},{24,16},{1,9},{9,1},{17,25},{25,17},{2,10},{10... | collective-permute-start | bytes 589832 | tf_op jit(solution)/shard_map/ppermute | solution.py:23
  9.5 14.4 %collective-permute-start.7 = (bf16[128,768]{1,0:T(8,128)(2,1)S(1)}, bf16[128,768]{1,0:T(8,128)(2,1)S(1)}, u32[]{:S(2)}, u32[]{:S(2)}) collective-permute-start(bf16[128,768]{1,0:T(8,128)(2,1)S(1)} %bitcast.29), channel_id=1, source_target_pairs={{0,16},{8,24},{16,0},{24,8},{1,17},{9,25},{17,1},{25,9},{2,18},{10... | collective-permute-start | bytes 589832 | tf_op jit(solution)/shard_map/ppermute | solution.py:23
  14.8 9.2 %collective-permute-start.6 = (bf16[128,768]{1,0:T(8,128)(2,1)S(1)}, bf16[128,768]{1,0:T(8,128)(2,1)S(1)}, u32[]{:S(2)}, u32[]{:S(2)}) collective-permute-start(bf16[128,768]{1,0:T(8,128)(2,1)S(1)} %bitcast.30), channel_id=1, source_target_pairs={{0,24},{8,16},{16,8},{24,0},{1,25},{9,17},{17,9},{25,1},{2,26},{10... | collective-permute-start | bytes 589832 | tf_op jit(solution)/shard_map/ppermute | solution.py:23
  20.1 7.5 %collective-permute-start.4 = (bf16[64,384]{1,0:T(8,128)(2,1)S(1)}, bf16[64,384]{1,0:T(8,128)(2,1)S(1)}, u32[]{:S(2)}, u32[]{:S(2)}) collective-permute-start(bf16[64,384]{1,0:T(8,128)(2,1)S(1)} %get-tuple-element.137), channel_id=1, source_target_pairs={{0,16},{8,24},{16,0},{24,8},{1,17},{9,25},{17,1},{25,9},{2,18},{10... | collective-permute-start | bytes 147464 | tf_op jit(solution)/shard_map/ppermute | solution.py:23
  24.0 10.3 %collective-permute-start.12 = (bf16[192,384]{1,0:T(8,128)(2,1)S(1)}, bf16[192,384]{1,0:T(8,128)(2,1)S(1)}, u32[]{:S(2)}, u32[]{:S(2)}) collective-permute-start(bf16[192,384]{1,0:T(8,128)(2,1)S(1)} %get-tuple-element.158), channel_id=1, source_target_pairs={{0,8},{8,0},{16,24},{24,16},{1,9},{9,1},{17,25},{25,17},{2,10},{10... | collective-permute-start | bytes 442376 | tf_op jit(solution)/shard_map/ppermute | solution.py:23
  25.2 9.9 %collective-permute-start.13 = (bf16[192,384]{1,0:T(8,128)(2,1)S(1)}, bf16[192,384]{1,0:T(8,128)(2,1)S(1)}, u32[]{:S(2)}, u32[]{:S(2)}) collective-permute-start(bf16[192,384]{1,0:T(8,128)(2,1)S(1)} %get-tuple-element.159), channel_id=1, source_target_pairs={{0,16},{8,24},{16,0},{24,8},{1,17},{9,25},{17,1},{25,9},{2,18},{10... | collective-permute-start | bytes 442376 | tf_op jit(solution)/shard_map/ppermute | solution.py:23
  26.3 8.9 %collective-permute-start.14 = (bf16[192,384]{1,0:T(8,128)(2,1)S(1)}, bf16[192,384]{1,0:T(8,128)(2,1)S(1)}, u32[]{:S(2)}, u32[]{:S(2)}) collective-permute-start(bf16[192,384]{1,0:T(8,128)(2,1)S(1)} %get-tuple-element.160), channel_id=1, source_target_pairs={{0,24},{8,16},{16,8},{24,0},{1,25},{9,17},{17,9},{25,1},{2,26},{10... | collective-permute-start | bytes 442376 | tf_op jit(solution)/shard_map/ppermute | solution.py:23
  41.9 16.3 %collective-permute-start.19 = (bf16[2,96,768]{2,1,0:T(8,128)(2,1)S(1)}, bf16[2,96,768]{2,1,0:T(8,128)(2,1)S(1)}, u32[]{:S(2)}, u32[]{:S(2)}) collective-permute-start(bf16[2,96,768]{2,1,0:T(8,128)(2,1)S(1)} %get-tuple-element.256), channel_id=1, source_target_pairs={{0,4},{1,5},{2,6},{3,7},{4,0},{5,1},{6,2},{7,3},{8,12},{9,13},{10,... | collective-permute-start | bytes 884744 | tf_op jit(solution)/shard_map/ppermute | solution.py:23
  44.8 16.7 %collective-permute-start.18 = (bf16[2,96,1024]{2,1,0:T(8,128)(2,1)S(1)}, bf16[2,96,1024]{2,1,0:T(8,128)(2,1)S(1)}, u32[]{:S(2)}, u32[]{:S(2)}) collective-permute-start(bf16[2,96,1024]{2,1,0:T(8,128)(2,1)S(1)} %get-tuple-element.254), channel_id=1, source_target_pairs={{0,2},{1,3},{2,0},{3,1},{4,6},{5,7},{6,4},{7,5},{8,10},{9,11},{10,... | collective-permute-start | bytes 1179656 | tf_op jit(solution)/shard_map/ppermute | solution.py:23
  51.7 10.5 %collective-permute-start.17 = (bf16[2,128,768]{2,1,0:T(8,128)(2,1)S(1)}, bf16[2,128,768]{2,1,0:T(8,128)(2,1)S(1)}, u32[]{:S(2)}, u32[]{:S(2)}) collective-permute-start(bf16[2,128,768]{2,1,0:T(8,128)(2,1)S(1)} %get-tuple-element.207), channel_id=1, source_target_pairs={{0,16},{8,24},{16,0},{24,8},{1,17},{9,25},{17,1},{25,9},{2,18},{10... | collective-permute-start | bytes 1179656 | tf_op jit(solution)/shard_map/ppermute | solution.py:23
  53.1 10.4 %collective-permute-start.21 = (bf16[4,96,640]{2,1,0:T(8,128)(2,1)S(1)}, bf16[4,96,640]{2,1,0:T(8,128)(2,1)S(1)}, u32[]{:S(2)}, u32[]{:S(2)}) collective-permute-start(bf16[4,96,640]{2,1,0:T(8,128)(2,1)S(1)} %get-tuple-element.214), channel_id=1, source_target_pairs={{0,1},{1,0},{2,3},{3,2},{4,5},{5,4},{6,7},{7,6},{8,9},{9,8},{10,11... | collective-permute-start | bytes 1474568 | tf_op jit(solution)/shard_map/ppermute | solution.py:23
  58.3 9.7 %collective-permute-start.23 = (bf16[1,96,768]{2,1,0:T(8,128)(2,1)S(1)}, bf16[1,96,768]{2,1,0:T(8,128)(2,1)S(1)}, u32[]{:S(2)}, u32[]{:S(2)}) collective-permute-start(bf16[1,96,768]{2,1,0:T(8,128)(2,1)S(1)} %get-tuple-element.262), channel_id=1, source_target_pairs={{0,2},{1,3},{2,0},{3,1},{4,6},{5,7},{6,4},{7,5},{8,10},{9,11},{10,... | collective-permute-start | bytes 442376 | tf_op jit(solution)/shard_map/ppermute | solution.py:23
  63.6 10.4 %collective-permute-start.22 = (bf16[2,96,640]{2,1,0:T(8,128)(2,1)S(1)}, bf16[2,96,640]{2,1,0:T(8,128)(2,1)S(1)}, u32[]{:S(2)}, u32[]{:S(2)}) collective-permute-start(bf16[2,96,640]{2,1,0:T(8,128)(2,1)S(1)} %get-tuple-element.258), channel_id=1, source_target_pairs={{0,2},{1,3},{2,0},{3,1},{4,6},{5,7},{6,4},{7,5},{8,10},{9,11},{10,... | collective-permute-start | bytes 737288 | tf_op jit(solution)/shard_map/ppermute | solution.py:23
  64.1 10.5 %collective-permute-start.28 = (bf16[1,96,1024]{2,1,0:T(8,128)(2,1)S(1)}, bf16[1,96,1024]{2,1,0:T(8,128)(2,1)S(1)}, u32[]{:S(2)}, u32[]{:S(2)}) collective-permute-start(bf16[1,96,1024]{2,1,0:T(8,128)(2,1)S(1)} %get-tuple-element.260), channel_id=1, source_target_pairs={{0,4},{1,5},{2,6},{3,7},{4,0},{5,1},{6,2},{7,3},{8,12},{9,13},{10,... | collective-permute-start | bytes 589832 | tf_op jit(solution)/shard_map/ppermute | solution.py:23
  68.1 7.8 %collective-permute-start.25 = (bf16[96,768]{1,0:T(8,128)(2,1)S(1)}, bf16[96,768]{1,0:T(8,128)(2,1)S(1)}, u32[]{:S(2)}, u32[]{:S(2)}) collective-permute-start(bf16[96,768]{1,0:T(8,128)(2,1)S(1)} %fusion.13.refs_0_), channel_id=1, source_target_pairs={{0,8},{8,0},{16,24},{24,16},{1,9},{9,1},{17,25},{25,17},{2,10},{10... | collective-permute-start | bytes 442376 | tf_op jit(solution)/shard_map/ppermute | solution.py:23
  69.3 7.8 %collective-permute-start.26 = (bf16[96,768]{1,0:T(8,128)(2,1)S(1)}, bf16[96,768]{1,0:T(8,128)(2,1)S(1)}, u32[]{:S(2)}, u32[]{:S(2)}) collective-permute-start(bf16[96,768]{1,0:T(8,128)(2,1)S(1)} %fusion.13.refs_0_), channel_id=1, source_target_pairs={{0,16},{8,24},{16,0},{24,8},{1,17},{9,25},{17,1},{25,9},{2,18},{10... | collective-permute-start | bytes 442376 | tf_op jit(solution)/shard_map/ppermute | solution.py:23
  70.4 7.9 %collective-permute-start.27 = (bf16[96,768]{1,0:T(8,128)(2,1)S(1)}, bf16[96,768]{1,0:T(8,128)(2,1)S(1)}, u32[]{:S(2)}, u32[]{:S(2)}) collective-permute-start(bf16[96,768]{1,0:T(8,128)(2,1)S(1)} %fusion.13.refs_0_), channel_id=1, source_target_pairs={{0,24},{8,16},{16,8},{24,0},{1,25},{9,17},{17,9},{25,1},{2,26},{10... | collective-permute-start | bytes 442376 | tf_op jit(solution)/shard_map/ppermute | solution.py:23
  74.7 9.2 %collective-permute-start.32 = (bf16[96,1024]{1,0:T(8,128)(2,1)S(1)}, bf16[96,1024]{1,0:T(8,128)(2,1)S(1)}, u32[]{:S(2)}, u32[]{:S(2)}) collective-permute-start(bf16[96,1024]{1,0:T(8,128)(2,1)S(1)} %fusion.12.refs_0_), channel_id=1, source_target_pairs={{0,8},{8,0},{16,24},{24,16},{1,9},{9,1},{17,25},{25,17},{2,10},{10... | collective-permute-start | bytes 589832 | tf_op jit(solution)/shard_map/ppermute | solution.py:23
  75.9 10.4 %collective-permute-start.33 = (bf16[96,1024]{1,0:T(8,128)(2,1)S(1)}, bf16[96,1024]{1,0:T(8,128)(2,1)S(1)}, u32[]{:S(2)}, u32[]{:S(2)}) collective-permute-start(bf16[96,1024]{1,0:T(8,128)(2,1)S(1)} %fusion.12.refs_0_), channel_id=1, source_target_pairs={{0,16},{8,24},{16,0},{24,8},{1,17},{9,25},{17,1},{25,9},{2,18},{10... | collective-permute-start | bytes 589832 | tf_op jit(solution)/shard_map/ppermute | solution.py:23
  77.1 9.5 %collective-permute-start.34 = (bf16[96,1024]{1,0:T(8,128)(2,1)S(1)}, bf16[96,1024]{1,0:T(8,128)(2,1)S(1)}, u32[]{:S(2)}, u32[]{:S(2)}) collective-permute-start(bf16[96,1024]{1,0:T(8,128)(2,1)S(1)} %fusion.12.refs_0_), channel_id=1, source_target_pairs={{0,24},{8,16},{16,8},{24,0},{1,25},{9,17},{17,9},{25,1},{2,26},{10... | collective-permute-start | bytes 589832 | tf_op jit(solution)/shard_map/ppermute | solution.py:23
  82.4 8.2 %collective-permute-start.30 = (bf16[96,640]{1,0:T(8,128)(2,1)S(1)}, bf16[96,640]{1,0:T(8,128)(2,1)S(1)}, u32[]{:S(2)}, u32[]{:S(2)}) collective-permute-start(bf16[96,640]{1,0:T(8,128)(2,1)S(1)} %fusion.14.refs_0_), channel_id=1, source_target_pairs={{0,16},{8,24},{16,0},{24,8},{1,17},{9,25},{17,1},{25,9},{2,18},{10... | collective-permute-start | bytes 368648 | tf_op jit(solution)/shard_map/ppermute | solution.py:23
  (26 other events, 133.4 us)

commit v7 on v6

--- a/solution.py
+++ b/solution.py
@@ -69,7 +69,7 @@
 HOPS = {"d": "far", "u": "near", "a": "near"}
 GATHER = {"d": None, "u": None, "a": None}
 DH = (2, 1)
-ORDER = "pq cs t2 t1 af fs c1 pm c2 c3 lo fa up dn d0 u0 bw ou d1 u1 h1 a0 h2 d2 a1 u2 d3 d4 a2 h3 u3 u4 a3 a4".split()
+ORDER = "pq cs t1 t2 af c1 fs pm c2 c3 lo fa up dn d0 u0 bw ou d1 u1 h1 a0 h2 d2 a1 u2 d3 d4 a2 h3 u3 u4 a3 a4".split()
 
 
 def flat(ref):

time: 92 us -> 92 us (level)
  no operation moved by 1% of the time
where the time goes in v7:
time: 92 us; the launch traced here: 91.8 us
  starting transfers between devices  43.7 us (48%)
  Pallas kernels  26.8 us (29%)
  waiting for transfers between devices  14.9 us (16%)
  local copies, waits for them, and re-layouts  3.02 us (3%)
  other arithmetic  2.46 us (3%)
  between operations  0.96 us (1%)
    ppermute x35, starting transfers between devices, exchange(): return lax.ppermute(value, axis, [(j, j ^ step) for j in range(size)])  43.7 us
    pallas_call x13, Pallas kernels, kernel(): pl.pallas_call(body, out_shape=outs, scratch_shapes=list(scratch), name=n...  26.8 us
    ppermute x35, waiting for transfers between devices, exchange(): return lax.ppermute(value, axis, [(j, j ^ step) for j in range(size)])  14.9 us
    unnamed x30, local copies, waits for them, and re-layouts  3.02 us
  transfers between devices with their start and end apart: 35, of which 9 were waited for; matrix products, arithmetic and copies ran while one was open for 3% of the time, Pallas kernels for 28%

profile of v7, /device:TPU:0, one launch (start us, length us, event | category | flops | bytes accessed | tf_op | source)
XLA Modules:
  0.0 91.8 jit_solution(4797448645716543001)
XLA Ops:
  0.7 3.0 %collective-permute-start = (bf16[128,768]{1,0:T(8,128)(2,1)}, bf16[128,768]{1,0:T(8,128)(2,1)S(1)}, u32[]{:S(2)}, u32[]{:S(2)}) collective-permute-start(bf16[128,768]{1,0:T(8,128)(2,1)} %bitcast.21), channel_id=1, source_target_pairs={{0,8},{8,0},{16,24},{24,16},{1,9},{9,1},{17,25},{25,17},{2,10},{10... | collective-permute-start | bytes 589832 | tf_op jit(solution)/shard_map/ppermute | solution.py:23
  3.7 1.5 %collective-permute-start.1 = (bf16[128,768]{1,0:T(8,128)(2,1)}, bf16[128,768]{1,0:T(8,128)(2,1)S(1)}, u32[]{:S(2)}, u32[]{:S(2)}) collective-permute-start(bf16[128,768]{1,0:T(8,128)(2,1)} %bitcast.22), channel_id=1, source_target_pairs={{0,16},{8,24},{16,0},{24,8},{1,17},{9,25},{17,1},{25,9},{2,18},{10... | collective-permute-start | bytes 589832 | tf_op jit(solution)/shard_map/ppermute | solution.py:23
  5.2 2.0 %copy-done.11 = bf16[768,2304]{1,0:T(8,128)(2,1)S(1)} copy-done((bf16[768,2304]{1,0:T(8,128)(2,1)S(1)}, bf16[768,2304]{1,0:T(8,128)(2,1)}, u32[]{:S(2)}) %copy-start.11) | copy-done | bytes 3538968
  7.4 2.1 %collective-permute-start.8 = (bf16[128,768]{1,0:T(8,128)(2,1)S(1)}, bf16[128,768]{1,0:T(8,128)(2,1)S(1)}, u32[]{:S(2)}, u32[]{:S(2)}) collective-permute-start(bf16[128,768]{1,0:T(8,128)(2,1)S(1)} %bitcast.28), channel_id=1, source_target_pairs={{0,8},{8,0},{16,24},{24,16},{1,9},{9,1},{17,25},{25,17},{2,10},{10... | collective-permute-start | bytes 589832 | tf_op jit(solution)/shard_map/ppermute | solution.py:23
  9.5 1.5 %collective-permute-start.7 = (bf16[128,768]{1,0:T(8,128)(2,1)S(1)}, bf16[128,768]{1,0:T(8,128)(2,1)S(1)}, u32[]{:S(2)}, u32[]{:S(2)}) collective-permute-start(bf16[128,768]{1,0:T(8,128)(2,1)S(1)} %bitcast.29), channel_id=1, source_target_pairs={{0,16},{8,24},{16,0},{24,8},{1,17},{9,25},{17,1},{25,9},{2,18},{10... | collective-permute-start | bytes 589832 | tf_op jit(solution)/shard_map/ppermute | solution.py:23
  14.7 1.5 %collective-permute-start.6 = (bf16[128,768]{1,0:T(8,128)(2,1)S(1)}, bf16[128,768]{1,0:T(8,128)(2,1)S(1)}, u32[]{:S(2)}, u32[]{:S(2)}) collective-permute-start(bf16[128,768]{1,0:T(8,128)(2,1)S(1)} %bitcast.30), channel_id=1, source_target_pairs={{0,24},{8,16},{16,8},{24,0},{1,25},{9,17},{17,9},{25,1},{2,26},{10... | collective-permute-start | bytes 589832 | tf_op jit(solution)/shard_map/ppermute | solution.py:23
  16.2 3.0 %attn_fwd.1 = (bf16[512,576]{1,0:T(8,128)(2,1)S(1)}, f32[512,128]{1,0:T(8,128)S(1)}, f32[8,512]{1,0:T(8,128)S(1)}, f32[512,128]{1,0:T(8,128)S(1)}, bf16[512,192]...) custom-call(bf16[128,768]{1,0:T(8,128)(2,1)S(1)} %bitcast.24, ...), custom_call_target="tpu_custom_call" | custom-call | flops 6000000000 | bytes 12000000 | tf_op jit(solution)/shard_map/attn_fwd/pallas_call | solution.py:476
  20.1 1.5 %collective-permute-start.4 = (bf16[64,384]{1,0:T(8,128)(2,1)S(1)}, bf16[64,384]{1,0:T(8,128)(2,1)S(1)}, u32[]{:S(2)}, u32[]{:S(2)}) collective-permute-start(bf16[64,384]{1,0:T(8,128)(2,1)S(1)} %get-tuple-element.137), channel_id=1, source_target_pairs={{0,16},{8,24},{16,0},{24,8},{1,17},{9,25},{17,1},{25,9},{2,18},{10... | collective-permute-start | bytes 147464 | tf_op jit(solution)/shard_map/ppermute | solution.py:23
  27.5 4.0 %local.1 = (bf16[128,3072]{1,0:T(8,128)(2,1)S(1)}, f32[128,768]{1,0:T(8,128)S(1)}, f32[128,768]{1,0:T(8,128)S(1)}, f32[8,768]{1,0:T(8,128)S(1)}, bf16[128,384]{1...) custom-call(bf16[128,768]{1,0:T(8,128)(2,1)S(1)} %bitcast.25, ...), custom_call_target="tpu_custom_call" | custom-call | flops 5000000000 | bytes 10000000 | tf_op jit(solution)/shard_map/local/pallas_call | solution.py:476
  31.4 1.6 %collective-permute-start.10 = (bf16[128,384]{1,0:T(8,128)(2,1)S(1)}, bf16[128,384]{1,0:T(8,128)(2,1)S(1)}, u32[]{:S(2)}, u32[]{:S(2)}) collective-permute-start(bf16[128,384]{1,0:T(8,128)(2,1)S(1)} %get-tuple-element.152), channel_id=1, source_target_pairs={{0,16},{8,24},{16,0},{24,8},{1,17},{9,25},{17,1},{25,9},{2,18},{10... | collective-permute-start | bytes 294920 | tf_op jit(solution)/shard_map/ppermute | solution.py:23
  35.0 3.6 %up.1 = (bf16[512,768]{1,0:T(8,128)(2,1)S(1)}, bf16[512,768]{1,0:T(8,128)(2,1)S(1)}, f32[512,768]{1,0:T(8,128)S(1)}, bf16[4,96,768]{2,1,0:T(8,128)(2,1)S(1)}, bf16[4,96,768]{2,1,0:T(8,128)(2,1)S(1)}) custom-call(bf16[128,768]{1,0:T(8,128)(2,1)S(1)} %bitcast.26, bf16[128,768]{1,0:T(8,128)(2,1)S(1)} %collective-permute-done.refs_1_, ...), custom_call_target="tpu_custom_call" | custom-call | flops 1000000000 | bytes 2000000 | tf_op jit(solution)/shard_map/up/pallas_call | solution.py:476
  38.9 1.9 %down.1 = (bf16[4,96,1024]{2,1,0:T(8,128)(2,1)S(1)}, bf16[4,96,1024]{2,1,0:T(8,128)(2,1)S(1)}) custom-call(bf16[128,768]{1,0:T(8,128)(2,1)S(1)} %bitcast.33, bf16[128,768]{1,0:T(8,128)(2,1)S(1)} %collective-permute-done.8.refs_12_.refs_1_, bf16[128,768]{1,0:T(8,128)(2,1)S(1)} %collective-permute-done.7.refs_13_.refs_2_, ...), custom_call_target="tpu_custom_call" | custom-call | flops 1000000000 | bytes 2000000 | tf_op jit(solution)/shard_map/down/pallas_call | solution.py:476
  41.9 2.6 %collective-permute-start.19 = (bf16[2,96,768]{2,1,0:T(8,128)(2,1)S(1)}, bf16[2,96,768]{2,1,0:T(8,128)(2,1)S(1)}, u32[]{:S(2)}, u32[]{:S(2)}) collective-permute-start(bf16[2,96,768]{2,1,0:T(8,128)(2,1)S(1)} %get-tuple-element.256), channel_id=1, source_target_pairs={{0,4},{1,5},{2,6},{3,7},{4,0},{5,1},{6,2},{7,3},{8,12},{9,13},{10,... | collective-permute-start | bytes 884744 | tf_op jit(solution)/shard_map/ppermute | solution.py:23
  44.8 1.7 %collective-permute-start.18 = (bf16[2,96,1024]{2,1,0:T(8,128)(2,1)S(1)}, bf16[2,96,1024]{2,1,0:T(8,128)(2,1)S(1)}, u32[]{:S(2)}, u32[]{:S(2)}) collective-permute-start(bf16[2,96,1024]{2,1,0:T(8,128)(2,1)S(1)} %get-tuple-element.254), channel_id=1, source_target_pairs={{0,2},{1,3},{2,0},{3,1},{4,6},{5,7},{6,4},{7,5},{8,10},{9,11},{10,... | collective-permute-start | bytes 1179656 | tf_op jit(solution)/shard_map/ppermute | solution.py:23
  46.5 5.2 %attn_bwd.1 = (f32[128,768]{1,0:T(8,128)S(1)}, f32[128,768]{1,0:T(8,128)S(1)}, bf16[2,128,768]{2,1,0:T(8,128)(2,1)S(1)}, bf16[4,96,640]{2,1,0:T(8,128)(2,1)S(1)}, bf16[4,96,640]{2,1,0:T(8,128)(2,1)S(1)}) custom-call(bf16[128,768]{1,0:T(8,128)(2,1)S(1)} %bitcast.27, bf16[128,768]{1,0:T(8,128)(2,1)S(1)} %collective-permute-done.refs_1_, ...), custom_call_target="tpu_custom_call" | custom-call | flops 1000000000 | bytes 2000000 | tf_op jit(solution)/shard_map/attn_bwd/pallas_call | solution.py:476
  51.7 1.4 %collective-permute-start.17 = (bf16[2,128,768]{2,1,0:T(8,128)(2,1)S(1)}, bf16[2,128,768]{2,1,0:T(8,128)(2,1)S(1)}, u32[]{:S(2)}, u32[]{:S(2)}) collective-permute-start(bf16[2,128,768]{2,1,0:T(8,128)(2,1)S(1)} %get-tuple-element.207), channel_id=1, source_target_pairs={{0,16},{8,24},{16,0},{24,8},{1,17},{9,25},{17,1},{25,9},{2,18},{10... | collective-permute-start | bytes 1179656 | tf_op jit(solution)/shard_map/ppermute | solution.py:23
  53.1 1.5 %out.1 = bf16[128,768]{1,0:T(8,128)(2,1)} custom-call(f32[128,768]{1,0:T(8,128)S(1)} %get-tuple-element.204.x1_ref, bf16[128,3072]{1,0:T(8,128)(2,1)S(1)} %get-tuple-element.205.act, bf16[3072,768]{1,0:T(8,128)(2,1)S(1)} %copy-done, f32[768]{0:T(1024)S(1)} %copy-done.10), custom_call_target="tpu_custom_call" | custom-call | flops 1000000000 | bytes 2000000 | tf_op jit(solution)/shard_map/out/pallas_call | solution.py:476
  54.6 3.6 %collective-permute-done.19 = bf16[2,96,768]{2,1,0:T(8,128)(2,1)S(1)} collective-permute-done((bf16[2,96,768]{2,1,0:T(8,128)(2,1)S(1)}, bf16[2,96,768]{2,1,0:T(8,128)(2,1)S(1)}, u32[]{:S(2)}, u32[]{:S(2)}) %collective-permute-start.19) | collective-permute-done | bytes 294944 | tf_op jit(solution)/shard_map/ppermute | solution.py:23
  58.9 2.6 %collective-permute-done.18 = bf16[2,96,1024]{2,1,0:T(8,128)(2,1)S(1)} collective-permute-done((bf16[2,96,1024]{2,1,0:T(8,128)(2,1)S(1)}, bf16[2,96,1024]{2,1,0:T(8,128)(2,1)S(1)}, u32[]{:S(2)}, u32[]{:S(2)}) %collective-permute-start.18) | collective-permute-done | bytes 393248 | tf_op jit(solution)/shard_map/ppermute | solution.py:23
  64.1 3.4 %collective-permute-start.28 = (bf16[1,96,1024]{2,1,0:T(8,128)(2,1)S(1)}, bf16[1,96,1024]{2,1,0:T(8,128)(2,1)S(1)}, u32[]{:S(2)}, u32[]{:S(2)}) collective-permute-start(bf16[1,96,1024]{2,1,0:T(8,128)(2,1)S(1)} %get-tuple-element.260), channel_id=1, source_target_pairs={{0,4},{1,5},{2,6},{3,7},{4,0},{5,1},{6,2},{7,3},{8,12},{9,13},{10,... | collective-permute-start | bytes 589832 | tf_op jit(solution)/shard_map/ppermute | solution.py:23
  71.6 2.4 %collective-permute-done.22 = bf16[2,96,640]{2,1,0:T(8,128)(2,1)S(1)} collective-permute-done((bf16[2,96,640]{2,1,0:T(8,128)(2,1)S(1)}, bf16[2,96,640]{2,1,0:T(8,128)(2,1)S(1)}, u32[]{:S(2)}, u32[]{:S(2)}) %collective-permute-start.22) | collective-permute-done | bytes 245792 | tf_op jit(solution)/shard_map/ppermute | solution.py:23
  79.4 2.0 %collective-permute-done.24 = bf16[1,96,640]{2,1,0:T(8,128)(2,1)S(1)} collective-permute-done((bf16[1,96,640]{2,1,0:T(8,128)(2,1)S(1)}, bf16[1,96,640]{2,1,0:T(8,128)(2,1)S(1)}, u32[]{:S(2)}, u32[]{:S(2)}) %collective-permute-start.24) | collective-permute-done | bytes 122912 | tf_op jit(solution)/shard_map/ppermute | solution.py:23
  86.6 1.5 %up_final.1 = (f32[96,3072]{1,0:T(8,128)}, f32[96,768]{1,0:T(8,128)}, f32[96]{0:T(128)}, f32[96]{0:T(128)}, f32[96]{0:T(128)}, /*index=5*/f32[96]{0:T(128)}, f32[384]{0:T(512)}) custom-call(bf16[96,1024]{1,0:T(8,128)(2,1)S(1)} %fusion.12.refs_0_, bf16[96,1024]{1,0:T(8,128)(2,1)S(1)} %collective-permute-done.32.refs_1_, ...), custom_call_target="tpu_custom_call" | custom-call | flops 1000000000 | bytes 2000000 | tf_op jit(solution)/shard_map/up_final/pallas_call | solution.py:476
  88.0 2.6 %collective-permute-done.30.refs_2_ = bf16[96,640]{1,0:T(8,128)(2,1)S(1)} collective-permute-done((bf16[96,640]{1,0:T(8,128)(2,1)S(1)}, bf16[96,640]{1,0:T(8,128)(2,1)S(1)}, u32[]{:S(2)}, u32[]{:S(2)}) %collective-permute-start.30) | collective-permute-done | bytes 122912 | tf_op jit(solution)/shard_map/ppermute | solution.py:23
  (106 shorter events, 33.1 us)
Async XLA Ops:
  0.7 14.0 %collective-permute-start = (bf16[128,768]{1,0:T(8,128)(2,1)}, bf16[128,768]{1,0:T(8,128)(2,1)S(1)}, u32[]{:S(2)}, u32[]{:S(2)}) collective-permute-start(bf16[128,768]{1,0:T(8,128)(2,1)} %bitcast.21), channel_id=1, source_target_pairs={{0,8},{8,0},{16,24},{24,16},{1,9},{9,1},{17,25},{25,17},{2,10},{10... | collective-permute-start | bytes 589832 | tf_op jit(solution)/shard_map/ppermute | solution.py:23
  3.7 12.5 %collective-permute-start.1 = (bf16[128,768]{1,0:T(8,128)(2,1)}, bf16[128,768]{1,0:T(8,128)(2,1)S(1)}, u32[]{:S(2)}, u32[]{:S(2)}) collective-permute-start(bf16[128,768]{1,0:T(8,128)(2,1)} %bitcast.22), channel_id=1, source_target_pairs={{0,16},{8,24},{16,0},{24,8},{1,17},{9,25},{17,1},{25,9},{2,18},{10... | collective-permute-start | bytes 589832 | tf_op jit(solution)/shard_map/ppermute | solution.py:23
  5.2 11.0 %collective-permute-start.2 = (bf16[128,768]{1,0:T(8,128)(2,1)}, bf16[128,768]{1,0:T(8,128)(2,1)S(1)}, u32[]{:S(2)}, u32[]{:S(2)}) collective-permute-start(bf16[128,768]{1,0:T(8,128)(2,1)} %bitcast.23), channel_id=1, source_target_pairs={{0,24},{8,16},{16,8},{24,0},{1,25},{9,17},{17,9},{25,1},{2,26},{10... | collective-permute-start | bytes 589832 | tf_op jit(solution)/shard_map/ppermute | solution.py:23
  7.4 11.8 %collective-permute-start.8 = (bf16[128,768]{1,0:T(8,128)(2,1)S(1)}, bf16[128,768]{1,0:T(8,128)(2,1)S(1)}, u32[]{:S(2)}, u32[]{:S(2)}) collective-permute-start(bf16[128,768]{1,0:T(8,128)(2,1)S(1)} %bitcast.28), channel_id=1, source_target_pairs={{0,8},{8,0},{16,24},{24,16},{1,9},{9,1},{17,25},{25,17},{2,10},{10... | collective-permute-start | bytes 589832 | tf_op jit(solution)/shard_map/ppermute | solution.py:23
  9.5 14.3 %collective-permute-start.7 = (bf16[128,768]{1,0:T(8,128)(2,1)S(1)}, bf16[128,768]{1,0:T(8,128)(2,1)S(1)}, u32[]{:S(2)}, u32[]{:S(2)}) collective-permute-start(bf16[128,768]{1,0:T(8,128)(2,1)S(1)} %bitcast.29), channel_id=1, source_target_pairs={{0,16},{8,24},{16,0},{24,8},{1,17},{9,25},{17,1},{25,9},{2,18},{10... | collective-permute-start | bytes 589832 | tf_op jit(solution)/shard_map/ppermute | solution.py:23
  14.7 9.2 %collective-permute-start.6 = (bf16[128,768]{1,0:T(8,128)(2,1)S(1)}, bf16[128,768]{1,0:T(8,128)(2,1)S(1)}, u32[]{:S(2)}, u32[]{:S(2)}) collective-permute-start(bf16[128,768]{1,0:T(8,128)(2,1)S(1)} %bitcast.30), channel_id=1, source_target_pairs={{0,24},{8,16},{16,8},{24,0},{1,25},{9,17},{17,9},{25,1},{2,26},{10... | collective-permute-start | bytes 589832 | tf_op jit(solution)/shard_map/ppermute | solution.py:23
  23.9 10.4 %collective-permute-start.12 = (bf16[192,384]{1,0:T(8,128)(2,1)S(1)}, bf16[192,384]{1,0:T(8,128)(2,1)S(1)}, u32[]{:S(2)}, u32[]{:S(2)}) collective-permute-start(bf16[192,384]{1,0:T(8,128)(2,1)S(1)} %get-tuple-element.158), channel_id=1, source_target_pairs={{0,8},{8,0},{16,24},{24,16},{1,9},{9,1},{17,25},{25,17},{2,10},{10... | collective-permute-start | bytes 442376 | tf_op jit(solution)/shard_map/ppermute | solution.py:23
  25.2 9.8 %collective-permute-start.13 = (bf16[192,384]{1,0:T(8,128)(2,1)S(1)}, bf16[192,384]{1,0:T(8,128)(2,1)S(1)}, u32[]{:S(2)}, u32[]{:S(2)}) collective-permute-start(bf16[192,384]{1,0:T(8,128)(2,1)S(1)} %get-tuple-element.159), channel_id=1, source_target_pairs={{0,16},{8,24},{16,0},{24,8},{1,17},{9,25},{17,1},{25,9},{2,18},{10... | collective-permute-start | bytes 442376 | tf_op jit(solution)/shard_map/ppermute | solution.py:23
  26.3 8.7 %collective-permute-start.14 = (bf16[192,384]{1,0:T(8,128)(2,1)S(1)}, bf16[192,384]{1,0:T(8,128)(2,1)S(1)}, u32[]{:S(2)}, u32[]{:S(2)}) collective-permute-start(bf16[192,384]{1,0:T(8,128)(2,1)S(1)} %get-tuple-element.160), channel_id=1, source_target_pairs={{0,24},{8,16},{16,8},{24,0},{1,25},{9,17},{17,9},{25,1},{2,26},{10... | collective-permute-start | bytes 442376 | tf_op jit(solution)/shard_map/ppermute | solution.py:23
  41.9 16.3 %collective-permute-start.19 = (bf16[2,96,768]{2,1,0:T(8,128)(2,1)S(1)}, bf16[2,96,768]{2,1,0:T(8,128)(2,1)S(1)}, u32[]{:S(2)}, u32[]{:S(2)}) collective-permute-start(bf16[2,96,768]{2,1,0:T(8,128)(2,1)S(1)} %get-tuple-element.256), channel_id=1, source_target_pairs={{0,4},{1,5},{2,6},{3,7},{4,0},{5,1},{6,2},{7,3},{8,12},{9,13},{10,... | collective-permute-start | bytes 884744 | tf_op jit(solution)/shard_map/ppermute | solution.py:23
  44.8 16.8 %collective-permute-start.18 = (bf16[2,96,1024]{2,1,0:T(8,128)(2,1)S(1)}, bf16[2,96,1024]{2,1,0:T(8,128)(2,1)S(1)}, u32[]{:S(2)}, u32[]{:S(2)}) collective-permute-start(bf16[2,96,1024]{2,1,0:T(8,128)(2,1)S(1)} %get-tuple-element.254), channel_id=1, source_target_pairs={{0,2},{1,3},{2,0},{3,1},{4,6},{5,7},{6,4},{7,5},{8,10},{9,11},{10,... | collective-permute-start | bytes 1179656 | tf_op jit(solution)/shard_map/ppermute | solution.py:23
  51.7 10.5 %collective-permute-start.17 = (bf16[2,128,768]{2,1,0:T(8,128)(2,1)S(1)}, bf16[2,128,768]{2,1,0:T(8,128)(2,1)S(1)}, u32[]{:S(2)}, u32[]{:S(2)}) collective-permute-start(bf16[2,128,768]{2,1,0:T(8,128)(2,1)S(1)} %get-tuple-element.207), channel_id=1, source_target_pairs={{0,16},{8,24},{16,0},{24,8},{1,17},{9,25},{17,1},{25,9},{2,18},{10... | collective-permute-start | bytes 1179656 | tf_op jit(solution)/shard_map/ppermute | solution.py:23
  53.1 10.4 %collective-permute-start.21 = (bf16[4,96,640]{2,1,0:T(8,128)(2,1)S(1)}, bf16[4,96,640]{2,1,0:T(8,128)(2,1)S(1)}, u32[]{:S(2)}, u32[]{:S(2)}) collective-permute-start(bf16[4,96,640]{2,1,0:T(8,128)(2,1)S(1)} %get-tuple-element.214), channel_id=1, source_target_pairs={{0,1},{1,0},{2,3},{3,2},{4,5},{5,4},{6,7},{7,6},{8,9},{9,8},{10,11... | collective-permute-start | bytes 1474568 | tf_op jit(solution)/shard_map/ppermute | solution.py:23
  58.3 9.7 %collective-permute-start.23 = (bf16[1,96,768]{2,1,0:T(8,128)(2,1)S(1)}, bf16[1,96,768]{2,1,0:T(8,128)(2,1)S(1)}, u32[]{:S(2)}, u32[]{:S(2)}) collective-permute-start(bf16[1,96,768]{2,1,0:T(8,128)(2,1)S(1)} %get-tuple-element.262), channel_id=1, source_target_pairs={{0,2},{1,3},{2,0},{3,1},{4,6},{5,7},{6,4},{7,5},{8,10},{9,11},{10,... | collective-permute-start | bytes 442376 | tf_op jit(solution)/shard_map/ppermute | solution.py:23
  63.6 10.4 %collective-permute-start.22 = (bf16[2,96,640]{2,1,0:T(8,128)(2,1)S(1)}, bf16[2,96,640]{2,1,0:T(8,128)(2,1)S(1)}, u32[]{:S(2)}, u32[]{:S(2)}) collective-permute-start(bf16[2,96,640]{2,1,0:T(8,128)(2,1)S(1)} %get-tuple-element.258), channel_id=1, source_target_pairs={{0,2},{1,3},{2,0},{3,1},{4,6},{5,7},{6,4},{7,5},{8,10},{9,11},{10,... | collective-permute-start | bytes 737288 | tf_op jit(solution)/shard_map/ppermute | solution.py:23
  64.1 10.6 %collective-permute-start.28 = (bf16[1,96,1024]{2,1,0:T(8,128)(2,1)S(1)}, bf16[1,96,1024]{2,1,0:T(8,128)(2,1)S(1)}, u32[]{:S(2)}, u32[]{:S(2)}) collective-permute-start(bf16[1,96,1024]{2,1,0:T(8,128)(2,1)S(1)} %get-tuple-element.260), channel_id=1, source_target_pairs={{0,4},{1,5},{2,6},{3,7},{4,0},{5,1},{6,2},{7,3},{8,12},{9,13},{10,... | collective-permute-start | bytes 589832 | tf_op jit(solution)/shard_map/ppermute | solution.py:23
  68.1 7.8 %collective-permute-start.25 = (bf16[96,768]{1,0:T(8,128)(2,1)S(1)}, bf16[96,768]{1,0:T(8,128)(2,1)S(1)}, u32[]{:S(2)}, u32[]{:S(2)}) collective-permute-start(bf16[96,768]{1,0:T(8,128)(2,1)S(1)} %fusion.13.refs_0_), channel_id=1, source_target_pairs={{0,8},{8,0},{16,24},{24,16},{1,9},{9,1},{17,25},{25,17},{2,10},{10... | collective-permute-start | bytes 442376 | tf_op jit(solution)/shard_map/ppermute | solution.py:23
  69.3 7.8 %collective-permute-start.26 = (bf16[96,768]{1,0:T(8,128)(2,1)S(1)}, bf16[96,768]{1,0:T(8,128)(2,1)S(1)}, u32[]{:S(2)}, u32[]{:S(2)}) collective-permute-start(bf16[96,768]{1,0:T(8,128)(2,1)S(1)} %fusion.13.refs_0_), channel_id=1, source_target_pairs={{0,16},{8,24},{16,0},{24,8},{1,17},{9,25},{17,1},{25,9},{2,18},{10... | collective-permute-start | bytes 442376 | tf_op jit(solution)/shard_map/ppermute | solution.py:23
  70.4 7.9 %collective-permute-start.27 = (bf16[96,768]{1,0:T(8,128)(2,1)S(1)}, bf16[96,768]{1,0:T(8,128)(2,1)S(1)}, u32[]{:S(2)}, u32[]{:S(2)}) collective-permute-start(bf16[96,768]{1,0:T(8,128)(2,1)S(1)} %fusion.13.refs_0_), channel_id=1, source_target_pairs={{0,24},{8,16},{16,8},{24,0},{1,25},{9,17},{17,9},{25,1},{2,26},{10... | collective-permute-start | bytes 442376 | tf_op jit(solution)/shard_map/ppermute | solution.py:23
  74.1 7.3 %collective-permute-start.24 = (bf16[1,96,640]{2,1,0:T(8,128)(2,1)S(1)}, bf16[1,96,640]{2,1,0:T(8,128)(2,1)S(1)}, u32[]{:S(2)}, u32[]{:S(2)}) collective-permute-start(bf16[1,96,640]{2,1,0:T(8,128)(2,1)S(1)} %get-tuple-element.264), channel_id=1, source_target_pairs={{0,4},{1,5},{2,6},{3,7},{4,0},{5,1},{6,2},{7,3},{8,12},{9,13},{10,... | collective-permute-start | bytes 368648 | tf_op jit(solution)/shard_map/ppermute | solution.py:23
  74.7 9.2 %collective-permute-start.32 = (bf16[96,1024]{1,0:T(8,128)(2,1)S(1)}, bf16[96,1024]{1,0:T(8,128)(2,1)S(1)}, u32[]{:S(2)}, u32[]{:S(2)}) collective-permute-start(bf16[96,1024]{1,0:T(8,128)(2,1)S(1)} %fusion.12.refs_0_), channel_id=1, source_target_pairs={{0,8},{8,0},{16,24},{24,16},{1,9},{9,1},{17,25},{25,17},{2,10},{10... | collective-permute-start | bytes 589832 | tf_op jit(solution)/shard_map/ppermute | solution.py:23
  75.8 10.4 %collective-permute-start.33 = (bf16[96,1024]{1,0:T(8,128)(2,1)S(1)}, bf16[96,1024]{1,0:T(8,128)(2,1)S(1)}, u32[]{:S(2)}, u32[]{:S(2)}) collective-permute-start(bf16[96,1024]{1,0:T(8,128)(2,1)S(1)} %fusion.12.refs_0_), channel_id=1, source_target_pairs={{0,16},{8,24},{16,0},{24,8},{1,17},{9,25},{17,1},{25,9},{2,18},{10... | collective-permute-start | bytes 589832 | tf_op jit(solution)/shard_map/ppermute | solution.py:23
  77.1 9.5 %collective-permute-start.34 = (bf16[96,1024]{1,0:T(8,128)(2,1)S(1)}, bf16[96,1024]{1,0:T(8,128)(2,1)S(1)}, u32[]{:S(2)}, u32[]{:S(2)}) collective-permute-start(bf16[96,1024]{1,0:T(8,128)(2,1)S(1)} %fusion.12.refs_0_), channel_id=1, source_target_pairs={{0,24},{8,16},{16,8},{24,0},{1,25},{9,17},{17,9},{25,1},{2,26},{10... | collective-permute-start | bytes 589832 | tf_op jit(solution)/shard_map/ppermute | solution.py:23
  82.4 8.2 %collective-permute-start.30 = (bf16[96,640]{1,0:T(8,128)(2,1)S(1)}, bf16[96,640]{1,0:T(8,128)(2,1)S(1)}, u32[]{:S(2)}, u32[]{:S(2)}) collective-permute-start(bf16[96,640]{1,0:T(8,128)(2,1)S(1)} %fusion.14.refs_0_), channel_id=1, source_target_pairs={{0,16},{8,24},{16,0},{24,8},{1,17},{9,25},{17,1},{25,9},{2,18},{10... | collective-permute-start | bytes 368648 | tf_op jit(solution)/shard_map/ppermute | solution.py:23
  (26 other events, 132.4 us)

commit v8 on v7

--- a/solution.py
+++ b/solution.py
@@ -69,7 +69,11 @@
 HOPS = {"d": "far", "u": "near", "a": "near"}
 GATHER = {"d": None, "u": None, "a": None}
 DH = (2, 1)
-ORDER = "pq cs t1 t2 af c1 fs pm c2 c3 lo fa up dn d0 u0 bw ou d1 u1 h1 a0 h2 d2 a1 u2 d3 d4 a2 h3 u3 u4 a3 a4".split()
+ORDER = (
+    "pq", "cs", "t1", "t2", "af", "c1", "fs", "pm", "c2", "c3", "lo", "fa",
+    "up", "dn", "d0", "u0", "bw", "ou", "d1", "u1", "h1", "a0", "h2", "d2",
+    "a1", "u2", "d3", "d4", "a2", "h3", "u3", "u4", "a3", "a4",
+)
 
 
 def flat(ref):

time: 92 us -> 92 us (level)
  no operation moved by 1% of the time
where the time goes in v8:
time: 92 us; the launch traced here: 91.8 us
  starting transfers between devices  43.7 us (48%)
  Pallas kernels  26.8 us (29%)
  waiting for transfers between devices  14.9 us (16%)
  local copies, waits for them, and re-layouts  3.02 us (3%)
  other arithmetic  2.46 us (3%)
  between operations  0.96 us (1%)
    ppermute x35, starting transfers between devices, exchange(): return lax.ppermute(value, axis, [(j, j ^ step) for j in range(size)])  43.7 us
    pallas_call x13, Pallas kernels, kernel(): pl.pallas_call(body, out_shape=outs, scratch_shapes=list(scratch), name=n...  26.8 us
    ppermute x35, waiting for transfers between devices, exchange(): return lax.ppermute(value, axis, [(j, j ^ step) for j in range(size)])  14.9 us
    unnamed x30, local copies, waits for them, and re-layouts  3.02 us
  transfers between devices with their start and end apart: 35, of which 9 were waited for; matrix products, arithmetic and copies ran while one was open for 3% of the time, Pallas kernels for 28%

profile of v8, /device:TPU:0, one launch (start us, length us, event | category | flops | bytes accessed | tf_op | source)
XLA Modules:
  0.0 91.8 jit_solution(4797448645716543001)
XLA Ops:
  0.7 3.0 %collective-permute-start = (bf16[128,768]{1,0:T(8,128)(2,1)}, bf16[128,768]{1,0:T(8,128)(2,1)S(1)}, u32[]{:S(2)}, u32[]{:S(2)}) collective-permute-start(bf16[128,768]{1,0:T(8,128)(2,1)} %bitcast.21), channel_id=1, source_target_pairs={{0,8},{8,0},{16,24},{24,16},{1,9},{9,1},{17,25},{25,17},{2,10},{10... | collective-permute-start | bytes 589832 | tf_op jit(solution)/shard_map/ppermute | solution.py:23
  3.7 1.5 %collective-permute-start.1 = (bf16[128,768]{1,0:T(8,128)(2,1)}, bf16[128,768]{1,0:T(8,128)(2,1)S(1)}, u32[]{:S(2)}, u32[]{:S(2)}) collective-permute-start(bf16[128,768]{1,0:T(8,128)(2,1)} %bitcast.22), channel_id=1, source_target_pairs={{0,16},{8,24},{16,0},{24,8},{1,17},{9,25},{17,1},{25,9},{2,18},{10... | collective-permute-start | bytes 589832 | tf_op jit(solution)/shard_map/ppermute | solution.py:23
  5.2 2.0 %copy-done.11 = bf16[768,2304]{1,0:T(8,128)(2,1)S(1)} copy-done((bf16[768,2304]{1,0:T(8,128)(2,1)S(1)}, bf16[768,2304]{1,0:T(8,128)(2,1)}, u32[]{:S(2)}) %copy-start.11) | copy-done | bytes 3538968
  7.4 2.1 %collective-permute-start.8 = (bf16[128,768]{1,0:T(8,128)(2,1)S(1)}, bf16[128,768]{1,0:T(8,128)(2,1)S(1)}, u32[]{:S(2)}, u32[]{:S(2)}) collective-permute-start(bf16[128,768]{1,0:T(8,128)(2,1)S(1)} %bitcast.28), channel_id=1, source_target_pairs={{0,8},{8,0},{16,24},{24,16},{1,9},{9,1},{17,25},{25,17},{2,10},{10... | collective-permute-start | bytes 589832 | tf_op jit(solution)/shard_map/ppermute | solution.py:23
  9.5 1.5 %collective-permute-start.7 = (bf16[128,768]{1,0:T(8,128)(2,1)S(1)}, bf16[128,768]{1,0:T(8,128)(2,1)S(1)}, u32[]{:S(2)}, u32[]{:S(2)}) collective-permute-start(bf16[128,768]{1,0:T(8,128)(2,1)S(1)} %bitcast.29), channel_id=1, source_target_pairs={{0,16},{8,24},{16,0},{24,8},{1,17},{9,25},{17,1},{25,9},{2,18},{10... | collective-permute-start | bytes 589832 | tf_op jit(solution)/shard_map/ppermute | solution.py:23
  14.7 1.5 %collective-permute-start.6 = (bf16[128,768]{1,0:T(8,128)(2,1)S(1)}, bf16[128,768]{1,0:T(8,128)(2,1)S(1)}, u32[]{:S(2)}, u32[]{:S(2)}) collective-permute-start(bf16[128,768]{1,0:T(8,128)(2,1)S(1)} %bitcast.30), channel_id=1, source_target_pairs={{0,24},{8,16},{16,8},{24,0},{1,25},{9,17},{17,9},{25,1},{2,26},{10... | collective-permute-start | bytes 589832 | tf_op jit(solution)/shard_map/ppermute | solution.py:23
  16.2 3.0 %attn_fwd.1 = (bf16[512,576]{1,0:T(8,128)(2,1)S(1)}, f32[512,128]{1,0:T(8,128)S(1)}, f32[8,512]{1,0:T(8,128)S(1)}, f32[512,128]{1,0:T(8,128)S(1)}, bf16[512,192]...) custom-call(bf16[128,768]{1,0:T(8,128)(2,1)S(1)} %bitcast.24, ...), custom_call_target="tpu_custom_call" | custom-call | flops 6000000000 | bytes 12000000 | tf_op jit(solution)/shard_map/attn_fwd/pallas_call | solution.py:480
  20.1 1.5 %collective-permute-start.4 = (bf16[64,384]{1,0:T(8,128)(2,1)S(1)}, bf16[64,384]{1,0:T(8,128)(2,1)S(1)}, u32[]{:S(2)}, u32[]{:S(2)}) collective-permute-start(bf16[64,384]{1,0:T(8,128)(2,1)S(1)} %get-tuple-element.137), channel_id=1, source_target_pairs={{0,16},{8,24},{16,0},{24,8},{1,17},{9,25},{17,1},{25,9},{2,18},{10... | collective-permute-start | bytes 147464 | tf_op jit(solution)/shard_map/ppermute | solution.py:23
  27.5 4.0 %local.1 = (bf16[128,3072]{1,0:T(8,128)(2,1)S(1)}, f32[128,768]{1,0:T(8,128)S(1)}, f32[128,768]{1,0:T(8,128)S(1)}, f32[8,768]{1,0:T(8,128)S(1)}, bf16[128,384]{1...) custom-call(bf16[128,768]{1,0:T(8,128)(2,1)S(1)} %bitcast.25, ...), custom_call_target="tpu_custom_call" | custom-call | flops 5000000000 | bytes 10000000 | tf_op jit(solution)/shard_map/local/pallas_call | solution.py:480
  31.4 1.6 %collective-permute-start.10 = (bf16[128,384]{1,0:T(8,128)(2,1)S(1)}, bf16[128,384]{1,0:T(8,128)(2,1)S(1)}, u32[]{:S(2)}, u32[]{:S(2)}) collective-permute-start(bf16[128,384]{1,0:T(8,128)(2,1)S(1)} %get-tuple-element.152), channel_id=1, source_target_pairs={{0,16},{8,24},{16,0},{24,8},{1,17},{9,25},{17,1},{25,9},{2,18},{10... | collective-permute-start | bytes 294920 | tf_op jit(solution)/shard_map/ppermute | solution.py:23
  35.0 3.6 %up.1 = (bf16[512,768]{1,0:T(8,128)(2,1)S(1)}, bf16[512,768]{1,0:T(8,128)(2,1)S(1)}, f32[512,768]{1,0:T(8,128)S(1)}, bf16[4,96,768]{2,1,0:T(8,128)(2,1)S(1)}, bf16[4,96,768]{2,1,0:T(8,128)(2,1)S(1)}) custom-call(bf16[128,768]{1,0:T(8,128)(2,1)S(1)} %bitcast.26, bf16[128,768]{1,0:T(8,128)(2,1)S(1)} %collective-permute-done.refs_1_, ...), custom_call_target="tpu_custom_call" | custom-call | flops 1000000000 | bytes 2000000 | tf_op jit(solution)/shard_map/up/pallas_call | solution.py:480
  38.9 1.9 %down.1 = (bf16[4,96,1024]{2,1,0:T(8,128)(2,1)S(1)}, bf16[4,96,1024]{2,1,0:T(8,128)(2,1)S(1)}) custom-call(bf16[128,768]{1,0:T(8,128)(2,1)S(1)} %bitcast.33, bf16[128,768]{1,0:T(8,128)(2,1)S(1)} %collective-permute-done.8.refs_12_.refs_1_, bf16[128,768]{1,0:T(8,128)(2,1)S(1)} %collective-permute-done.7.refs_13_.refs_2_, ...), custom_call_target="tpu_custom_call" | custom-call | flops 1000000000 | bytes 2000000 | tf_op jit(solution)/shard_map/down/pallas_call | solution.py:480
  41.9 2.6 %collective-permute-start.19 = (bf16[2,96,768]{2,1,0:T(8,128)(2,1)S(1)}, bf16[2,96,768]{2,1,0:T(8,128)(2,1)S(1)}, u32[]{:S(2)}, u32[]{:S(2)}) collective-permute-start(bf16[2,96,768]{2,1,0:T(8,128)(2,1)S(1)} %get-tuple-element.256), channel_id=1, source_target_pairs={{0,4},{1,5},{2,6},{3,7},{4,0},{5,1},{6,2},{7,3},{8,12},{9,13},{10,... | collective-permute-start | bytes 884744 | tf_op jit(solution)/shard_map/ppermute | solution.py:23
  44.8 1.7 %collective-permute-start.18 = (bf16[2,96,1024]{2,1,0:T(8,128)(2,1)S(1)}, bf16[2,96,1024]{2,1,0:T(8,128)(2,1)S(1)}, u32[]{:S(2)}, u32[]{:S(2)}) collective-permute-start(bf16[2,96,1024]{2,1,0:T(8,128)(2,1)S(1)} %get-tuple-element.254), channel_id=1, source_target_pairs={{0,2},{1,3},{2,0},{3,1},{4,6},{5,7},{6,4},{7,5},{8,10},{9,11},{10,... | collective-permute-start | bytes 1179656 | tf_op jit(solution)/shard_map/ppermute | solution.py:23
  46.5 5.2 %attn_bwd.1 = (f32[128,768]{1,0:T(8,128)S(1)}, f32[128,768]{1,0:T(8,128)S(1)}, bf16[2,128,768]{2,1,0:T(8,128)(2,1)S(1)}, bf16[4,96,640]{2,1,0:T(8,128)(2,1)S(1)}, bf16[4,96,640]{2,1,0:T(8,128)(2,1)S(1)}) custom-call(bf16[128,768]{1,0:T(8,128)(2,1)S(1)} %bitcast.27, bf16[128,768]{1,0:T(8,128)(2,1)S(1)} %collective-permute-done.refs_1_, ...), custom_call_target="tpu_custom_call" | custom-call | flops 1000000000 | bytes 2000000 | tf_op jit(solution)/shard_map/attn_bwd/pallas_call | solution.py:480
  51.7 1.4 %collective-permute-start.17 = (bf16[2,128,768]{2,1,0:T(8,128)(2,1)S(1)}, bf16[2,128,768]{2,1,0:T(8,128)(2,1)S(1)}, u32[]{:S(2)}, u32[]{:S(2)}) collective-permute-start(bf16[2,128,768]{2,1,0:T(8,128)(2,1)S(1)} %get-tuple-element.207), channel_id=1, source_target_pairs={{0,16},{8,24},{16,0},{24,8},{1,17},{9,25},{17,1},{25,9},{2,18},{10... | collective-permute-start | bytes 1179656 | tf_op jit(solution)/shard_map/ppermute | solution.py:23
  53.1 1.5 %out.1 = bf16[128,768]{1,0:T(8,128)(2,1)} custom-call(f32[128,768]{1,0:T(8,128)S(1)} %get-tuple-element.204.x1_ref, bf16[128,3072]{1,0:T(8,128)(2,1)S(1)} %get-tuple-element.205.act, bf16[3072,768]{1,0:T(8,128)(2,1)S(1)} %copy-done, f32[768]{0:T(1024)S(1)} %copy-done.10), custom_call_target="tpu_custom_call" | custom-call | flops 1000000000 | bytes 2000000 | tf_op jit(solution)/shard_map/out/pallas_call | solution.py:480
  54.6 3.6 %collective-permute-done.19 = bf16[2,96,768]{2,1,0:T(8,128)(2,1)S(1)} collective-permute-done((bf16[2,96,768]{2,1,0:T(8,128)(2,1)S(1)}, bf16[2,96,768]{2,1,0:T(8,128)(2,1)S(1)}, u32[]{:S(2)}, u32[]{:S(2)}) %collective-permute-start.19) | collective-permute-done | bytes 294944 | tf_op jit(solution)/shard_map/ppermute | solution.py:23
  58.9 2.6 %collective-permute-done.18 = bf16[2,96,1024]{2,1,0:T(8,128)(2,1)S(1)} collective-permute-done((bf16[2,96,1024]{2,1,0:T(8,128)(2,1)S(1)}, bf16[2,96,1024]{2,1,0:T(8,128)(2,1)S(1)}, u32[]{:S(2)}, u32[]{:S(2)}) %collective-permute-start.18) | collective-permute-done | bytes 393248 | tf_op jit(solution)/shard_map/ppermute | solution.py:23
  64.1 3.4 %collective-permute-start.28 = (bf16[1,96,1024]{2,1,0:T(8,128)(2,1)S(1)}, bf16[1,96,1024]{2,1,0:T(8,128)(2,1)S(1)}, u32[]{:S(2)}, u32[]{:S(2)}) collective-permute-start(bf16[1,96,1024]{2,1,0:T(8,128)(2,1)S(1)} %get-tuple-element.260), channel_id=1, source_target_pairs={{0,4},{1,5},{2,6},{3,7},{4,0},{5,1},{6,2},{7,3},{8,12},{9,13},{10,... | collective-permute-start | bytes 589832 | tf_op jit(solution)/shard_map/ppermute | solution.py:23
  71.6 2.4 %collective-permute-done.22 = bf16[2,96,640]{2,1,0:T(8,128)(2,1)S(1)} collective-permute-done((bf16[2,96,640]{2,1,0:T(8,128)(2,1)S(1)}, bf16[2,96,640]{2,1,0:T(8,128)(2,1)S(1)}, u32[]{:S(2)}, u32[]{:S(2)}) %collective-permute-start.22) | collective-permute-done | bytes 245792 | tf_op jit(solution)/shard_map/ppermute | solution.py:23
  79.4 2.0 %collective-permute-done.24 = bf16[1,96,640]{2,1,0:T(8,128)(2,1)S(1)} collective-permute-done((bf16[1,96,640]{2,1,0:T(8,128)(2,1)S(1)}, bf16[1,96,640]{2,1,0:T(8,128)(2,1)S(1)}, u32[]{:S(2)}, u32[]{:S(2)}) %collective-permute-start.24) | collective-permute-done | bytes 122912 | tf_op jit(solution)/shard_map/ppermute | solution.py:23
  86.6 1.5 %up_final.1 = (f32[96,3072]{1,0:T(8,128)}, f32[96,768]{1,0:T(8,128)}, f32[96]{0:T(128)}, f32[96]{0:T(128)}, f32[96]{0:T(128)}, /*index=5*/f32[96]{0:T(128)}, f32[384]{0:T(512)}) custom-call(bf16[96,1024]{1,0:T(8,128)(2,1)S(1)} %fusion.12.refs_0_, bf16[96,1024]{1,0:T(8,128)(2,1)S(1)} %collective-permute-done.32.refs_1_, ...), custom_call_target="tpu_custom_call" | custom-call | flops 1000000000 | bytes 2000000 | tf_op jit(solution)/shard_map/up_final/pallas_call | solution.py:480
  88.0 2.6 %collective-permute-done.30.refs_2_ = bf16[96,640]{1,0:T(8,128)(2,1)S(1)} collective-permute-done((bf16[96,640]{1,0:T(8,128)(2,1)S(1)}, bf16[96,640]{1,0:T(8,128)(2,1)S(1)}, u32[]{:S(2)}, u32[]{:S(2)}) %collective-permute-start.30) | collective-permute-done | bytes 122912 | tf_op jit(solution)/shard_map/ppermute | solution.py:23
  (106 shorter events, 33.1 us)
Async XLA Ops:
  0.7 14.0 %collective-permute-start = (bf16[128,768]{1,0:T(8,128)(2,1)}, bf16[128,768]{1,0:T(8,128)(2,1)S(1)}, u32[]{:S(2)}, u32[]{:S(2)}) collective-permute-start(bf16[128,768]{1,0:T(8,128)(2,1)} %bitcast.21), channel_id=1, source_target_pairs={{0,8},{8,0},{16,24},{24,16},{1,9},{9,1},{17,25},{25,17},{2,10},{10... | collective-permute-start | bytes 589832 | tf_op jit(solution)/shard_map/ppermute | solution.py:23
  3.7 12.5 %collective-permute-start.1 = (bf16[128,768]{1,0:T(8,128)(2,1)}, bf16[128,768]{1,0:T(8,128)(2,1)S(1)}, u32[]{:S(2)}, u32[]{:S(2)}) collective-permute-start(bf16[128,768]{1,0:T(8,128)(2,1)} %bitcast.22), channel_id=1, source_target_pairs={{0,16},{8,24},{16,0},{24,8},{1,17},{9,25},{17,1},{25,9},{2,18},{10... | collective-permute-start | bytes 589832 | tf_op jit(solution)/shard_map/ppermute | solution.py:23
  5.2 11.0 %collective-permute-start.2 = (bf16[128,768]{1,0:T(8,128)(2,1)}, bf16[128,768]{1,0:T(8,128)(2,1)S(1)}, u32[]{:S(2)}, u32[]{:S(2)}) collective-permute-start(bf16[128,768]{1,0:T(8,128)(2,1)} %bitcast.23), channel_id=1, source_target_pairs={{0,24},{8,16},{16,8},{24,0},{1,25},{9,17},{17,9},{25,1},{2,26},{10... | collective-permute-start | bytes 589832 | tf_op jit(solution)/shard_map/ppermute | solution.py:23
  7.4 11.8 %collective-permute-start.8 = (bf16[128,768]{1,0:T(8,128)(2,1)S(1)}, bf16[128,768]{1,0:T(8,128)(2,1)S(1)}, u32[]{:S(2)}, u32[]{:S(2)}) collective-permute-start(bf16[128,768]{1,0:T(8,128)(2,1)S(1)} %bitcast.28), channel_id=1, source_target_pairs={{0,8},{8,0},{16,24},{24,16},{1,9},{9,1},{17,25},{25,17},{2,10},{10... | collective-permute-start | bytes 589832 | tf_op jit(solution)/shard_map/ppermute | solution.py:23
  9.5 14.3 %collective-permute-start.7 = (bf16[128,768]{1,0:T(8,128)(2,1)S(1)}, bf16[128,768]{1,0:T(8,128)(2,1)S(1)}, u32[]{:S(2)}, u32[]{:S(2)}) collective-permute-start(bf16[128,768]{1,0:T(8,128)(2,1)S(1)} %bitcast.29), channel_id=1, source_target_pairs={{0,16},{8,24},{16,0},{24,8},{1,17},{9,25},{17,1},{25,9},{2,18},{10... | collective-permute-start | bytes 589832 | tf_op jit(solution)/shard_map/ppermute | solution.py:23
  14.7 9.2 %collective-permute-start.6 = (bf16[128,768]{1,0:T(8,128)(2,1)S(1)}, bf16[128,768]{1,0:T(8,128)(2,1)S(1)}, u32[]{:S(2)}, u32[]{:S(2)}) collective-permute-start(bf16[128,768]{1,0:T(8,128)(2,1)S(1)} %bitcast.30), channel_id=1, source_target_pairs={{0,24},{8,16},{16,8},{24,0},{1,25},{9,17},{17,9},{25,1},{2,26},{10... | collective-permute-start | bytes 589832 | tf_op jit(solution)/shard_map/ppermute | solution.py:23
  23.9 10.4 %collective-permute-start.12 = (bf16[192,384]{1,0:T(8,128)(2,1)S(1)}, bf16[192,384]{1,0:T(8,128)(2,1)S(1)}, u32[]{:S(2)}, u32[]{:S(2)}) collective-permute-start(bf16[192,384]{1,0:T(8,128)(2,1)S(1)} %get-tuple-element.158), channel_id=1, source_target_pairs={{0,8},{8,0},{16,24},{24,16},{1,9},{9,1},{17,25},{25,17},{2,10},{10... | collective-permute-start | bytes 442376 | tf_op jit(solution)/shard_map/ppermute | solution.py:23
  25.2 9.8 %collective-permute-start.13 = (bf16[192,384]{1,0:T(8,128)(2,1)S(1)}, bf16[192,384]{1,0:T(8,128)(2,1)S(1)}, u32[]{:S(2)}, u32[]{:S(2)}) collective-permute-start(bf16[192,384]{1,0:T(8,128)(2,1)S(1)} %get-tuple-element.159), channel_id=1, source_target_pairs={{0,16},{8,24},{16,0},{24,8},{1,17},{9,25},{17,1},{25,9},{2,18},{10... | collective-permute-start | bytes 442376 | tf_op jit(solution)/shard_map/ppermute | solution.py:23
  26.3 8.7 %collective-permute-start.14 = (bf16[192,384]{1,0:T(8,128)(2,1)S(1)}, bf16[192,384]{1,0:T(8,128)(2,1)S(1)}, u32[]{:S(2)}, u32[]{:S(2)}) collective-permute-start(bf16[192,384]{1,0:T(8,128)(2,1)S(1)} %get-tuple-element.160), channel_id=1, source_target_pairs={{0,24},{8,16},{16,8},{24,0},{1,25},{9,17},{17,9},{25,1},{2,26},{10... | collective-permute-start | bytes 442376 | tf_op jit(solution)/shard_map/ppermute | solution.py:23
  41.9 16.3 %collective-permute-start.19 = (bf16[2,96,768]{2,1,0:T(8,128)(2,1)S(1)}, bf16[2,96,768]{2,1,0:T(8,128)(2,1)S(1)}, u32[]{:S(2)}, u32[]{:S(2)}) collective-permute-start(bf16[2,96,768]{2,1,0:T(8,128)(2,1)S(1)} %get-tuple-element.256), channel_id=1, source_target_pairs={{0,4},{1,5},{2,6},{3,7},{4,0},{5,1},{6,2},{7,3},{8,12},{9,13},{10,... | collective-permute-start | bytes 884744 | tf_op jit(solution)/shard_map/ppermute | solution.py:23
  44.8 16.8 %collective-permute-start.18 = (bf16[2,96,1024]{2,1,0:T(8,128)(2,1)S(1)}, bf16[2,96,1024]{2,1,0:T(8,128)(2,1)S(1)}, u32[]{:S(2)}, u32[]{:S(2)}) collective-permute-start(bf16[2,96,1024]{2,1,0:T(8,128)(2,1)S(1)} %get-tuple-element.254), channel_id=1, source_target_pairs={{0,2},{1,3},{2,0},{3,1},{4,6},{5,7},{6,4},{7,5},{8,10},{9,11},{10,... | collective-permute-start | bytes 1179656 | tf_op jit(solution)/shard_map/ppermute | solution.py:23
  51.7 10.5 %collective-permute-start.17 = (bf16[2,128,768]{2,1,0:T(8,128)(2,1)S(1)}, bf16[2,128,768]{2,1,0:T(8,128)(2,1)S(1)}, u32[]{:S(2)}, u32[]{:S(2)}) collective-permute-start(bf16[2,128,768]{2,1,0:T(8,128)(2,1)S(1)} %get-tuple-element.207), channel_id=1, source_target_pairs={{0,16},{8,24},{16,0},{24,8},{1,17},{9,25},{17,1},{25,9},{2,18},{10... | collective-permute-start | bytes 1179656 | tf_op jit(solution)/shard_map/ppermute | solution.py:23
  53.1 10.4 %collective-permute-start.21 = (bf16[4,96,640]{2,1,0:T(8,128)(2,1)S(1)}, bf16[4,96,640]{2,1,0:T(8,128)(2,1)S(1)}, u32[]{:S(2)}, u32[]{:S(2)}) collective-permute-start(bf16[4,96,640]{2,1,0:T(8,128)(2,1)S(1)} %get-tuple-element.214), channel_id=1, source_target_pairs={{0,1},{1,0},{2,3},{3,2},{4,5},{5,4},{6,7},{7,6},{8,9},{9,8},{10,11... | collective-permute-start | bytes 1474568 | tf_op jit(solution)/shard_map/ppermute | solution.py:23
  58.3 9.7 %collective-permute-start.23 = (bf16[1,96,768]{2,1,0:T(8,128)(2,1)S(1)}, bf16[1,96,768]{2,1,0:T(8,128)(2,1)S(1)}, u32[]{:S(2)}, u32[]{:S(2)}) collective-permute-start(bf16[1,96,768]{2,1,0:T(8,128)(2,1)S(1)} %get-tuple-element.262), channel_id=1, source_target_pairs={{0,2},{1,3},{2,0},{3,1},{4,6},{5,7},{6,4},{7,5},{8,10},{9,11},{10,... | collective-permute-start | bytes 442376 | tf_op jit(solution)/shard_map/ppermute | solution.py:23
  63.6 10.4 %collective-permute-start.22 = (bf16[2,96,640]{2,1,0:T(8,128)(2,1)S(1)}, bf16[2,96,640]{2,1,0:T(8,128)(2,1)S(1)}, u32[]{:S(2)}, u32[]{:S(2)}) collective-permute-start(bf16[2,96,640]{2,1,0:T(8,128)(2,1)S(1)} %get-tuple-element.258), channel_id=1, source_target_pairs={{0,2},{1,3},{2,0},{3,1},{4,6},{5,7},{6,4},{7,5},{8,10},{9,11},{10,... | collective-permute-start | bytes 737288 | tf_op jit(solution)/shard_map/ppermute | solution.py:23
  64.1 10.6 %collective-permute-start.28 = (bf16[1,96,1024]{2,1,0:T(8,128)(2,1)S(1)}, bf16[1,96,1024]{2,1,0:T(8,128)(2,1)S(1)}, u32[]{:S(2)}, u32[]{:S(2)}) collective-permute-start(bf16[1,96,1024]{2,1,0:T(8,128)(2,1)S(1)} %get-tuple-element.260), channel_id=1, source_target_pairs={{0,4},{1,5},{2,6},{3,7},{4,0},{5,1},{6,2},{7,3},{8,12},{9,13},{10,... | collective-permute-start | bytes 589832 | tf_op jit(solution)/shard_map/ppermute | solution.py:23
  68.1 7.8 %collective-permute-start.25 = (bf16[96,768]{1,0:T(8,128)(2,1)S(1)}, bf16[96,768]{1,0:T(8,128)(2,1)S(1)}, u32[]{:S(2)}, u32[]{:S(2)}) collective-permute-start(bf16[96,768]{1,0:T(8,128)(2,1)S(1)} %fusion.13.refs_0_), channel_id=1, source_target_pairs={{0,8},{8,0},{16,24},{24,16},{1,9},{9,1},{17,25},{25,17},{2,10},{10... | collective-permute-start | bytes 442376 | tf_op jit(solution)/shard_map/ppermute | solution.py:23
  69.3 7.8 %collective-permute-start.26 = (bf16[96,768]{1,0:T(8,128)(2,1)S(1)}, bf16[96,768]{1,0:T(8,128)(2,1)S(1)}, u32[]{:S(2)}, u32[]{:S(2)}) collective-permute-start(bf16[96,768]{1,0:T(8,128)(2,1)S(1)} %fusion.13.refs_0_), channel_id=1, source_target_pairs={{0,16},{8,24},{16,0},{24,8},{1,17},{9,25},{17,1},{25,9},{2,18},{10... | collective-permute-start | bytes 442376 | tf_op jit(solution)/shard_map/ppermute | solution.py:23
  70.4 7.9 %collective-permute-start.27 = (bf16[96,768]{1,0:T(8,128)(2,1)S(1)}, bf16[96,768]{1,0:T(8,128)(2,1)S(1)}, u32[]{:S(2)}, u32[]{:S(2)}) collective-permute-start(bf16[96,768]{1,0:T(8,128)(2,1)S(1)} %fusion.13.refs_0_), channel_id=1, source_target_pairs={{0,24},{8,16},{16,8},{24,0},{1,25},{9,17},{17,9},{25,1},{2,26},{10... | collective-permute-start | bytes 442376 | tf_op jit(solution)/shard_map/ppermute | solution.py:23
  74.1 7.3 %collective-permute-start.24 = (bf16[1,96,640]{2,1,0:T(8,128)(2,1)S(1)}, bf16[1,96,640]{2,1,0:T(8,128)(2,1)S(1)}, u32[]{:S(2)}, u32[]{:S(2)}) collective-permute-start(bf16[1,96,640]{2,1,0:T(8,128)(2,1)S(1)} %get-tuple-element.264), channel_id=1, source_target_pairs={{0,4},{1,5},{2,6},{3,7},{4,0},{5,1},{6,2},{7,3},{8,12},{9,13},{10,... | collective-permute-start | bytes 368648 | tf_op jit(solution)/shard_map/ppermute | solution.py:23
  74.7 9.2 %collective-permute-start.32 = (bf16[96,1024]{1,0:T(8,128)(2,1)S(1)}, bf16[96,1024]{1,0:T(8,128)(2,1)S(1)}, u32[]{:S(2)}, u32[]{:S(2)}) collective-permute-start(bf16[96,1024]{1,0:T(8,128)(2,1)S(1)} %fusion.12.refs_0_), channel_id=1, source_target_pairs={{0,8},{8,0},{16,24},{24,16},{1,9},{9,1},{17,25},{25,17},{2,10},{10... | collective-permute-start | bytes 589832 | tf_op jit(solution)/shard_map/ppermute | solution.py:23
  75.8 10.4 %collective-permute-start.33 = (bf16[96,1024]{1,0:T(8,128)(2,1)S(1)}, bf16[96,1024]{1,0:T(8,128)(2,1)S(1)}, u32[]{:S(2)}, u32[]{:S(2)}) collective-permute-start(bf16[96,1024]{1,0:T(8,128)(2,1)S(1)} %fusion.12.refs_0_), channel_id=1, source_target_pairs={{0,16},{8,24},{16,0},{24,8},{1,17},{9,25},{17,1},{25,9},{2,18},{10... | collective-permute-start | bytes 589832 | tf_op jit(solution)/shard_map/ppermute | solution.py:23
  77.1 9.5 %collective-permute-start.34 = (bf16[96,1024]{1,0:T(8,128)(2,1)S(1)}, bf16[96,1024]{1,0:T(8,128)(2,1)S(1)}, u32[]{:S(2)}, u32[]{:S(2)}) collective-permute-start(bf16[96,1024]{1,0:T(8,128)(2,1)S(1)} %fusion.12.refs_0_), channel_id=1, source_target_pairs={{0,24},{8,16},{16,8},{24,0},{1,25},{9,17},{17,9},{25,1},{2,26},{10... | collective-permute-start | bytes 589832 | tf_op jit(solution)/shard_map/ppermute | solution.py:23
  82.4 8.2 %collective-permute-start.30 = (bf16[96,640]{1,0:T(8,128)(2,1)S(1)}, bf16[96,640]{1,0:T(8,128)(2,1)S(1)}, u32[]{:S(2)}, u32[]{:S(2)}) collective-permute-start(bf16[96,640]{1,0:T(8,128)(2,1)S(1)} %fusion.14.refs_0_), channel_id=1, source_target_pairs={{0,16},{8,24},{16,0},{24,8},{1,17},{9,25},{17,1},{25,9},{2,18},{10... | collective-permute-start | bytes 368648 | tf_op jit(solution)/shard_map/ppermute | solution.py:23
  (26 other events, 132.4 us)
